TPU v7x, 32 devices: a whole 2x2x4 slice. The times are simulated.
32 devices in a mesh: lat: 16 (over z, y, x), mp: 2 (over core).
Axes of the slice: x: 2, y: 2, z: 4, core: 2. Of those that a mesh axis runs over, the one named last changes fastest.
Arguments:
- field: bfloat16 [32, 180, 768], P('lat', None, 'mp'), may hold values from -6 to 6
- row_group: int32 [32], replicated, may hold values from 0 to 7, as said below
- row_valid: int32 [32], replicated, may hold values from 0 to 1, as said below
- norm1_gain: float32 [768], P('mp'), may hold values from 0.5 to 1.5
- norm1_bias: float32 [768], P('mp'), may hold values from -4 to 4
- spec_w1: bfloat16 [2, 8, 96, 96], P(None, 'mp'), may hold values from -0.4375 to 0.4375
- spec_b1: float32 [2, 8, 96], P(None, 'mp'), may hold values from -4 to 4
- spec_w2: bfloat16 [2, 8, 96, 96], P(None, 'mp'), may hold values from -0.4375 to 0.4375
- spec_b2: float32 [2, 8, 96], P(None, 'mp'), may hold values from -0.3125 to 0.3125
- norm2_gain: float32 [768], P('mp'), may hold values from 0.5 to 1.5
- norm2_bias: float32 [768], P('mp'), may hold values from -4 to 4
- fc1_weight: bfloat16 [768, 3072], P(None, 'mp'), may hold values from -0.21875 to 0.21875
- fc1_bias: float32 [3072], P('mp'), may hold values from -6 to 6
- fc2_weight: bfloat16 [3072, 768], P('mp'), may hold values from -0.109375 to 0.109375
- fc2_bias: float32 [768], P('mp'), may hold values from -4 to 4
- cotangent: bfloat16 [32, 180, 768], P('lat', None, 'mp'), may hold values from -8 to 8
Outputs:
- out_field: bfloat16 [32, 180, 768], P('lat', None, 'mp')
- grad_field: float32 [32, 180, 768], P('lat', None, 'mp')
- grad_norm1_gain: float32 [768], P('mp')
- grad_norm1_bias: float32 [768], P('mp')
- grad_spec_w1: float32 [2, 8, 96, 96], P(None, 'mp')
- grad_spec_b1: float32 [2, 8, 96], P(None, 'mp')
- grad_spec_w2: float32 [2, 8, 96, 96], P(None, 'mp')
- grad_spec_b2: float32 [2, 8, 96], P(None, 'mp')
- grad_norm2_gain: float32 [768], P('mp')
- grad_norm2_bias: float32 [768], P('mp')
- grad_fc1_weight: float32 [768, 3072], P('lat', 'mp')
- grad_fc1_bias: float32 [3072], P('mp')
- grad_fc2_weight: float32 [3072, 768], P('mp', 'lat')
- grad_fc2_bias: float32 [768], P('mp')
Inputs may be any that keep to these rules, and one draw needn't show every extreme that they name: `row_group`: among rows with row_valid 1, group 0 has exactly 17 rows, always including the first row, the row in the middle and the last row; each group from 1 to 7 has exactly 2. Rows of a group lie anywhere. `row_valid`: exactly 1 row is 0.
All inputs are finite; a program needn't handle non-finite values.
Results may differ from a plain program's by a relative error of at most 0.0095.
The roundings to bfloat16 on the way count: a program that leaves them out, or rounds other values in their place, can miss the bound.
Values may be sent and summed in bfloat16 or wider, within the bound.
No kernel may reach another device: no remote copies, remote signals or barrier semaphores. Data moves between devices by JAX's collectives and lax.ppermute only.
A program may use at most 256 MiB of HBM per device.

v0:
```python
import math

import jax
import jax.numpy as jnp
from jax import lax
from jax.sharding import PartitionSpec as P

LON_FINE = 180
LON_COARSE = 45
GROUPS = 8


EPSILON = 1e-05
SHRINK = 0.01
HIGHEST = lax.Precision.HIGHEST


def row_tables(row_group, row_valid):
    member = (row_group[:, None] == jnp.arange(GROUPS, dtype=jnp.int32)[None, :]).astype(
        jnp.int32
    ) * row_valid[:, None]
    counts = jnp.sum(member, axis=0)
    before = jnp.cumsum(member, axis=0) - member
    offset = jnp.sum(before * member, axis=1)
    length = jnp.maximum(jnp.sum(member * counts[None, :], axis=1), 1)
    return (offset, length)


def latitude_pair(left_info, right_info, turn_sign):
    off_left, len_left, grp_left, val_left = left_info
    off_right, len_right, grp_right, val_right = right_info
    phases = off_left[:, None] * off_right[None, :] % len_left[:, None]
    lengths = len_left[:, None].astype(jnp.float32)
    angles = 2.0 * math.pi * phases.astype(jnp.float32) / lengths
    kept_pair = (
        (grp_left[:, None] == grp_right[None, :])
        & (val_left[:, None] > 0)
        & (val_right[None, :] > 0)
    ).astype(jnp.float32)
    scaling = kept_pair * lax.rsqrt(lengths)
    return (scaling * jnp.cos(angles), turn_sign * scaling * jnp.sin(angles))


def longitude_tables(widths, columns):
    indices = jnp.arange(columns, dtype=jnp.int32)
    phases = (indices[:, None] * indices[None, :])[None, :, :] % widths[:, None, None]
    lengths = widths[:, None, None].astype(jnp.float32)
    angles = 2.0 * math.pi * phases.astype(jnp.float32) / lengths
    inside = (
        (indices[None, :, None] < widths[:, None, None])
        & (indices[None, None, :] < widths[:, None, None])
    ).astype(jnp.float32)
    scaling = inside * lax.rsqrt(lengths)
    return (scaling * jnp.cos(angles), scaling * jnp.sin(angles))


def complex_rows(real_mat, imag_mat, values, channels):
    leading = jnp.einsum("ab,bwc->awc", real_mat, values, precision=HIGHEST)
    trailing = jnp.einsum("ab,bwc->awc", imag_mat, values, precision=HIGHEST)
    return jnp.concatenate(
        [
            leading[..., :channels] - trailing[..., channels:],
            leading[..., channels:] + trailing[..., :channels],
        ],
        axis=-1,
    )


def lon_forward(lon_cos, lon_sin, values):
    return jnp.concatenate(
        [
            jnp.einsum("rkw,rwc->rkc", lon_cos, values, precision=HIGHEST),
            -jnp.einsum("rkw,rwc->rkc", lon_sin, values, precision=HIGHEST),
        ],
        axis=-1,
    )


def lon_back(lon_cos, lon_sin, values, channels):
    return jnp.einsum(
        "rkw,rwc->rkc", lon_cos, values[..., :channels], precision=HIGHEST
    ) - jnp.einsum("rkw,rwc->rkc", lon_sin, values[..., channels:], precision=HIGHEST)


def smooth_gate(values):
    return jax.nn.gelu(values, approximate=True)


def shrinkage(values):
    return values - SHRINK * jnp.tanh(values / SHRINK)


def cycle_term(row_info, local_info, turn_sign, values, channels):
    window = tuple((listing for listing in row_info))
    real_mat, imag_mat = latitude_pair(window, local_info, turn_sign)
    return complex_rows(real_mat, imag_mat, values, channels)


def latitude_forward(values, turn_sign, row_info, local_info):
    rows_dev, columns, doubled = values.shape
    channels = doubled // 2
    return lax.psum_scatter(
        cycle_term(row_info, local_info, turn_sign, values, channels),
        "lat",
        scatter_dimension=0,
        tiled=True,
    )


def latitude_backward(values, turn_sign, row_info, local_info):
    rows_dev, columns, doubled = values.shape
    channels = doubled // 2
    return lax.psum_scatter(
        cycle_term(row_info, local_info, turn_sign, values, channels),
        "lat",
        scatter_dimension=0,
        tiled=True,
    )


def norm_forward(values, gain_vec, bias_vec, full_width):
    sum_plain, sum_square = lax.psum(
        (jnp.sum(values, axis=-1), jnp.sum(values * values, axis=-1)), "mp"
    )
    average = sum_plain / full_width
    inverse_std = lax.rsqrt(sum_square / full_width - average * average + EPSILON)
    centred = (values - average[..., None]) * inverse_std[..., None]
    return (centred * gain_vec + bias_vec, centred, inverse_std)


def norm_backward(grad_in, centred, inverse_std, gain_vec, full_width):
    scaled = grad_in * gain_vec
    sum_scaled, sum_cross = lax.psum(
        (jnp.sum(scaled, axis=-1), jnp.sum(scaled * centred, axis=-1)), "mp"
    )
    result = inverse_std[..., None] * (
        scaled - sum_scaled[..., None] / full_width - centred * sum_cross[..., None] / full_width
    )
    return (result, jnp.sum(grad_in * centred, axis=(0, 1)), jnp.sum(grad_in, axis=(0, 1)))


def complex_layer(real_in, imag_in, weight, bias):

    def product_of(values, matrix):
        return jnp.einsum("rwnb,nbc->rwnc", values, matrix, preferred_element_type=jnp.float32)

    real_out = product_of(real_in, weight[0]) - product_of(imag_in, weight[1]) + bias[0]
    imag_out = product_of(real_in, weight[1]) + product_of(imag_in, weight[0]) + bias[1]
    return (real_out, imag_out)


def complex_back(grad_real, grad_imag, in_real, in_imag, weight):

    def times_turned(values, matrix):
        return jnp.einsum("rwnc,nbc->rwnb", values, matrix, preferred_element_type=jnp.float32)

    def outer_sum(left_vals, right_vals):
        return jnp.einsum(
            "rwnb,rwnc->nbc", left_vals, right_vals, preferred_element_type=jnp.float32
        )

    in_grad_real = times_turned(grad_real, weight[0]) + times_turned(grad_imag, weight[1])
    in_grad_imag = times_turned(grad_imag, weight[0]) - times_turned(grad_real, weight[1])
    weight_grad = jnp.stack(
        [
            outer_sum(in_real, grad_real) + outer_sum(in_imag, grad_imag),
            outer_sum(in_real, grad_imag) - outer_sum(in_imag, grad_real),
        ]
    )
    bias_grad = jnp.stack(
        [
            jnp.sum(grad_real.astype(jnp.float32), axis=(0, 1)),
            jnp.sum(grad_imag.astype(jnp.float32), axis=(0, 1)),
        ]
    )
    return (in_grad_real, in_grad_imag, weight_grad, bias_grad)


def body(
    field,
    row_group,
    row_valid,
    norm1_gain,
    norm1_bias,
    spec_w1,
    spec_b1,
    spec_w2,
    spec_b2,
    norm2_gain,
    norm2_bias,
    fc1_weight,
    fc1_bias,
    fc2_weight,
    fc2_bias,
    cotangent,
):
    rows_dev, columns, channels = field.shape
    full_width = channels * lax.axis_size("mp")
    blocks = spec_w1.shape[1]
    block_size = spec_w1.shape[2]
    offset, length = row_tables(row_group, row_valid)
    row_info = (offset, length, row_group, row_valid)
    row_start = lax.axis_index("lat") * rows_dev
    local_info = tuple(
        (lax.dynamic_slice_in_dim(listing, row_start, rows_dev) for listing in row_info)
    )
    widths = jnp.where(local_info[2] == 0, LON_FINE, LON_COARSE).astype(jnp.int32)
    lon_cos, lon_sin = longitude_tables(widths, columns)
    positions = jnp.arange(columns, dtype=jnp.int32)
    token_mask = ((local_info[3][:, None] > 0) & (positions[None, :] < widths[:, None])).astype(
        jnp.float32
    )[..., None]
    grid_shape = (rows_dev, columns, blocks, block_size)
    incoming = field.astype(jnp.float32)
    normed, centred_one, inverse_one = norm_forward(incoming, norm1_gain, norm1_bias, full_width)
    spec_in = lon_forward(lon_cos, lon_sin, normed * token_mask)
    spectrum = latitude_forward(spec_in, -1.0, row_info, local_info)
    spec_low = spectrum.astype(jnp.bfloat16)
    low_real = spec_low[..., :channels].reshape(grid_shape)
    low_imag = spec_low[..., channels:].reshape(grid_shape)
    first_real, first_imag = complex_layer(low_real, low_imag, spec_w1, spec_b1)
    hidden_real = smooth_gate(first_real).astype(jnp.bfloat16)
    hidden_imag = smooth_gate(first_imag).astype(jnp.bfloat16)
    second_real, second_imag = complex_layer(hidden_real, hidden_imag, spec_w2, spec_b2)
    shrunk = jnp.concatenate(
        [
            shrinkage(second_real).reshape(rows_dev, columns, channels),
            shrinkage(second_imag).reshape(rows_dev, columns, channels),
        ],
        axis=-1,
    )
    spatial = latitude_forward(shrunk, 1.0, row_info, local_info)
    filtered = lon_back(lon_cos, lon_sin, spatial, channels) * token_mask
    mixed_one = incoming + filtered + normed
    normed_two, centred_two, inverse_two = norm_forward(
        mixed_one, norm2_gain, norm2_bias, full_width
    )
    normed_low = normed_two.astype(jnp.bfloat16)
    gathered = lax.all_gather(normed_low, "mp", axis=2, tiled=True).reshape(
        rows_dev * columns, full_width
    )
    pre_act = jnp.dot(gathered, fc1_weight, preferred_element_type=jnp.float32) + fc1_bias
    act_low = smooth_gate(pre_act).astype(jnp.bfloat16)
    partial_out = jnp.dot(act_low, fc2_weight, preferred_element_type=jnp.float32).reshape(
        rows_dev, columns, full_width
    )
    mlp_out = (
        lax.psum_scatter(
            partial_out.astype(jnp.bfloat16), "mp", scatter_dimension=2, tiled=True
        ).astype(jnp.float32)
        + fc2_bias
    )
    out_field = (mixed_one + mlp_out).astype(jnp.bfloat16)
    grad_out = cotangent.astype(jnp.float32)
    grad_fc2_bias = jnp.sum(grad_out, axis=(0, 1))
    grad_gathered = lax.all_gather(cotangent, "mp", axis=2, tiled=True).reshape(
        rows_dev * columns, full_width
    )
    grad_act = jnp.einsum(
        "td,hd->th", grad_gathered, fc2_weight, preferred_element_type=jnp.float32
    )
    grad_fc2_weight = jnp.einsum(
        "th,td->hd", act_low, grad_gathered, preferred_element_type=jnp.float32
    )
    grad_pre = jax.vjp(smooth_gate, pre_act)[1](grad_act)[0].astype(jnp.bfloat16)
    grad_fc1_bias = jnp.sum(grad_pre.astype(jnp.float32), axis=0)
    grad_fc1_weight = jnp.einsum(
        "td,th->dh", gathered, grad_pre, preferred_element_type=jnp.float32
    )
    grad_partial = jnp.einsum(
        "th,dh->td", grad_pre, fc1_weight, preferred_element_type=jnp.float32
    ).reshape(rows_dev, columns, full_width)
    grad_normed_two = lax.psum_scatter(
        grad_partial.astype(jnp.bfloat16), "mp", scatter_dimension=2, tiled=True
    ).astype(jnp.float32)
    back_two, grad_norm2_gain, grad_norm2_bias = norm_backward(
        grad_normed_two, centred_two, inverse_two, norm2_gain, full_width
    )
    grad_mixed = grad_out + back_two
    grad_spatial = lon_forward(lon_cos, lon_sin, grad_mixed * token_mask)
    grad_shrunk = latitude_backward(grad_spatial, -1.0, row_info, local_info)
    grad_second_real = jax.vjp(shrinkage, second_real)[1](
        grad_shrunk[..., :channels].reshape(grid_shape)
    )[0].astype(jnp.bfloat16)
    grad_second_imag = jax.vjp(shrinkage, second_imag)[1](
        grad_shrunk[..., channels:].reshape(grid_shape)
    )[0].astype(jnp.bfloat16)
    grad_hidden_real, grad_hidden_imag, grad_spec_w2, grad_spec_b2 = complex_back(
        grad_second_real, grad_second_imag, hidden_real, hidden_imag, spec_w2
    )
    grad_first_real = jax.vjp(smooth_gate, first_real)[1](grad_hidden_real)[0].astype(jnp.bfloat16)
    grad_first_imag = jax.vjp(smooth_gate, first_imag)[1](grad_hidden_imag)[0].astype(jnp.bfloat16)
    grad_low_real, grad_low_imag, grad_spec_w1, grad_spec_b1 = complex_back(
        grad_first_real, grad_first_imag, low_real, low_imag, spec_w1
    )
    grad_spectrum = jnp.concatenate(
        [
            grad_low_real.reshape(rows_dev, columns, channels),
            grad_low_imag.reshape(rows_dev, columns, channels),
        ],
        axis=-1,
    )
    grad_spec_in = latitude_backward(grad_spectrum, 1.0, row_info, local_info)
    grad_normed = grad_mixed + lon_back(lon_cos, lon_sin, grad_spec_in, channels) * token_mask
    back_one, grad_norm1_gain, grad_norm1_bias = norm_backward(
        grad_normed, centred_one, inverse_one, norm1_gain, full_width
    )
    grad_field = grad_mixed + back_one
    matrices = (
        lax.psum_scatter(grad_fc1_weight, "lat", scatter_dimension=0, tiled=True),
        lax.psum_scatter(grad_fc2_weight, "lat", scatter_dimension=1, tiled=True),
    )
    totals = lax.psum(
        (
            grad_norm1_gain,
            grad_norm1_bias,
            grad_spec_w1,
            grad_spec_b1,
            grad_spec_w2,
            grad_spec_b2,
            grad_norm2_gain,
            grad_norm2_bias,
            grad_fc1_bias,
            grad_fc2_bias,
        ),
        "lat",
    )
    return (
        out_field,
        grad_field,
        totals[0],
        totals[1],
        totals[2],
        totals[3],
        totals[4],
        totals[5],
        totals[6],
        totals[7],
        matrices[0],
        totals[8],
        matrices[1],
        totals[9],
    )


def solution(mesh):
    placed = (
        P("lat", None, "mp"),
        P(),
        P(),
        P("mp"),
        P("mp"),
        P(None, "mp", None, None),
        P(None, "mp", None),
        P(None, "mp", None, None),
        P(None, "mp", None),
        P("mp"),
        P("mp"),
        P(None, "mp"),
        P("mp"),
        P("mp", None),
        P("mp"),
        P("lat", None, "mp"),
    )
    return jax.shard_map(
        body,
        mesh=mesh,
        in_specs=placed,
        out_specs=(
            P("lat", None, "mp"),
            P("lat", None, "mp"),
            P("mp"),
            P("mp"),
            P(None, "mp", None, None),
            P(None, "mp", None),
            P(None, "mp", None, None),
            P(None, "mp", None),
            P("mp"),
            P("mp"),
            P("lat", "mp"),
            P("mp"),
            P("mp", "lat"),
            P("mp"),
        ),
        check_vma=False,
    )
```

profile of v0, /device:TPU:0, one launch (start us, length us, event | category | flops | bytes accessed | tf_op | source)
XLA Modules:
  0.0 2959.7 jit_solution(13592764408654442728)
XLA Ops:
  12.7 2.6 all-reduce.9
  15.3 6.8 convolution_negate_fusion.1
  22.1 6.1 fusion.82
  28.7 26.2 fusion.38
  54.9 30.1 %fusion.36 = f32[32,180,768]{2,0,1:T(8,128)} fusion(f32[2,180,768]{2,1,0:T(8,128)S(1)} %pad_maximum_fusion.4, f32[32,2]{0,1:T(2,128)S(1)} %get-tuple-element.137, f32[32,2]{0,1:T(2,128)S(1)} %get-tuple-element.111), kind=kOutput, calls=%fused_computation.92 | convolution fusion | flops 106168448 | bytes 18801152 | tf_op jit(solution)/shard_map/ab,bwc->awc/dot_general | solution.py:59
  85.0 14.5 slice_subtract_fusion.3
  99.5 12.1 pad_maximum_fusion
  111.6 755.6 %all-reduce.20 = bf16[32,180,768]{2,0,1:T(8,128)(2,1)} all-reduce(f32[32,180,768]{2,0,1:T(8,128)} %pad_maximum_fusion), channel_id=2, replica_groups=mesh['lat'=16,'mp'=2] {'lat'}, use_global_device_ids=true, to_apply=%region_8.10.clone | all-reduce | flops 4423680 | bytes 26542080
  868.4 2.2 dynamic-slice_convert_fusion
  874.8 2.7 multiply_convert_fusion.2
  883.5 2.8 reshape.237
  886.3 2.5 multiply_subtract_fusion.1
  889.9 2.8 reshape.236
  895.2 17.2 fusion.161
  912.4 26.6 fusion.168
  939.0 14.5 slice_subtract_fusion.2
  953.5 12.2 pad_maximum_fusion.1
  965.8 2.4 all_gather.7
  969.1 2.0 reshape.216
  971.0 4.3 fusion.207
  975.4 465.4 %all-reduce.15.cloned.1.call-done = f32[32,180,768]{2,0,1:T(8,128)} async-done(((f32[32,180,768]{2,0,1:T(8,128)}), f32[32,180,768]{2,0,1:T(8,128)}) %all-reduce.15.cloned.1.call-update) | async-done | bytes 17694736
  1440.8 3.1 constant_dynamic-slice_fusion.5
  1444.0 5.7 fusion.79
  1449.8 7.0 fusion.204
  1456.8 2.4 all-reduce.8
  1460.5 2.3 all_gather.6
  1462.8 2.0 reshape.215
  1464.8 6.0 convert_reduce_fusion
  1471.8 1.9 convolution_convert_fusion
  1476.8 3.8 convolution_convert_fusion.1
  1486.9 2.4 all-reduce.7
  1489.3 6.2 reduce-scatter.17.cloned.1.call-done
  1497.8 1.6 convert_add_fusion
  1499.5 5.8 convolution_negate_fusion
  1505.3 6.0 fusion.85
  1511.3 17.2 fusion.32
  1528.5 26.2 fusion.34
  1554.7 14.5 slice_subtract_fusion.1
  1569.2 12.5 pad_maximum_fusion.2
  1581.7 479.6 %all-reduce.17.cloned.1.call-done = f32[32,180,768]{2,0,1:T(8,128)} async-done(((f32[32,180,768]{2,0,1:T(8,128)}), f32[32,180,768]{2,0,1:T(8,128)}) %all-reduce.17.cloned.1.call-update) | async-done | bytes 17694736
  2061.3 3.8 constant_dynamic-slice_fusion.4
  2065.1 1.6 reshape.258
  2066.7 1.8 convert_reduce_fusion.4
  2070.6 2.7 reshape.259
  2073.3 1.5 convert_reduce_fusion.3
  2082.0 2.8 reshape.239
  2087.3 2.8 reshape.238
  2092.7 17.2 fusion.159
  2109.9 26.3 fusion.165
  2137.9 14.7 slice_subtract_fusion
  2152.6 12.1 pad_maximum_fusion.3
  2166.7 5.6 fusion.203
  2173.7 3.6 fusion.208
  2179.2 484.8 %all-reduce.19.cloned.1.call-done = (f32[32,180,768]{2,0,1:T(8,128)}, f32[2,4,96,96]{3,2,1,0:T(8,128)}, f32[2,4,96,96]{3,2,1,0:T(8,128)}) async-done(((f32[32,180,768]{2,0,1:T(8,128)}, f32[2,4,96,96]{3,2,1,0:T(8,128)}, f32[2,4,96,96]{3,2,1,0:T(8,128)}), (f32[32,180,768]{2,0,1:T(8,128)}, f32[2,4,96,96]{3,2,1,0:T(8,128)}, f32[2,4,96,96]{3,2,1,0:T(8,128)})) %all-reduce.19.cloned.1.call-update) | async-done | bytes 18284560
  2664.0 3.1 constant_dynamic-slice_fusion.3
  2667.2 5.7 fusion.76
  2672.9 7.3 fusion.73
  2680.3 2.6 all-reduce.6
  2682.9 1.5 fusion.72
  2685.5 74.9 %all-reduce.4 = (f32[384]{0:T(512)}, f32[384]{0:T(512)}, f32[2,4,96]{2,1,0:T(4,128)}, f32[2,4,96]{2,1,0:T(4,128)}, f32[384]{0:T(512)}, /*index=5*/f32[384]{0:T(512)}, f32[1536]{0:T(1024)}, f32[384]{0:T(512)}) all-reduce(f32[384]{0:T(512)S(1)} %get-tuple-element.73, ...), channel_id=1, replica_groups=mesh['lat'=16,'mp'=2] {'lat'}, use_global_device_ids=true, to_apply=%region_27.29 | all-reduce | flops 4992 | bytes 39936 | tf_op jit(solution)/shard_map/psum | solution.py:313
  2760.3 46.4 %reduce-scatter.15.cloned.1.call-done = f32[1536,48]{0,1:T(8,128)} async-done(((f32[1536,768]{0,1:T(8,128)}), f32[1536,48]{0,1:T(8,128)}) %reduce-scatter.15.cloned.1.call-update) | async-done | bytes 294928 | tf_op jit(solution)/shard_map/reduce_scatter | solution.py:311
  2806.7 142.2 %reduce-scatter.13.cloned.1.call-done = f32[48,1536]{1,0:T(8,128)} async-done(((f32[768,1536]{1,0:T(8,128)}), f32[48,1536]{1,0:T(8,128)}) %reduce-scatter.13.cloned.1.call-update) | async-done | bytes 294928 | tf_op jit(solution)/shard_map/reduce_scatter | solution.py:310
  2948.9 1.8 copy.262
  2950.7 1.8 copy.263
  (228 shorter events, 57.7 us)
Async XLA Ops:
  7.2 1457.6 %copy-start = (bf16[768,1536]{1,0:T(8,128)(2,1)S(1)}, bf16[768,1536]{1,0:T(8,128)(2,1)}, u32[]{:S(2)}) copy-start(bf16[768,1536]{1,0:T(8,128)(2,1)} %param.29) | copy-start | bytes 7077892
  7.2 14.9 copy-start.20
  7.2 14.9 copy-start.49
  7.2 14.9 copy-start.64
  7.2 1433.6 %all-reduce.15.cloned.1.call-start = ((), (), s32[]{:S(2)}) async-start(), calls=%async_computation.8 | async-start | bytes 35389440
  9.6 18.7 copy-start.55
  11.3 16.9 copy-start.29
  11.3 16.9 copy-start.58
  11.4 16.9 copy-start.61
  12.7 15.6 copy-start.45
  12.7 15.6 copy-start.52
  15.2 13.1 copy-start.38
  15.3 1434.4 %copy-start.36 = (f32[2,180]{1,0:T(2,128)}, f32[2,180]{1,0:T(2,128)S(1)}, u32[]{:S(2)}) copy-start(f32[2,180]{1,0:T(2,128)S(1)} %get-tuple-element.140) | copy-start | bytes 4324
  22.1 6.3 copy-start.34
  111.6 755.6 %copy-start.66 = (u32[32]{0:T(128)S(1)}, u32[32]{0:T(128)}, u32[]{:S(2)}) copy-start(u32[32]{0:T(128)} %constant.91) | copy-start | bytes 388
  867.2 4.2 copy-start.14
  870.6 3.2 copy-start.42
  872.5 4.9 copy-start.13
  874.8 4.2 copy-start.43
  874.8 4.2 copy-start.7
  874.8 4.2 copy-start.27
  965.7 518.3 %reduce-scatter.19.cloned.1.call-start = ((), (), s32[]{:S(2)}) async-start(), calls=%async_computation.7 | async-start | bytes 884736
  975.3 468.6 %copy-start.30 = (s32[180,180]{1,0:T(8,128)S(1)}, s32[180,180]{1,0:T(8,128)}, u32[]{:S(2)}) copy-start(s32[180,180]{1,0:T(8,128)} %copy-done.29) | copy-start | bytes 388804
  975.3 468.6 %copy-start.53 = (pred[2,180]{1,0:T(4,128)(4,1)S(1)}, pred[2,180]{1,0:T(4,128)(4,1)}, u32[]{:S(2)}) copy-start(pred[2,180]{1,0:T(4,128)(4,1)} %copy-done.52) | copy-start | bytes 1084
  975.3 468.6 %copy-start.56 = (f32[2]{0:T(128)S(1)}, f32[2]{0:T(128)}, u32[]{:S(2)}) copy-start(f32[2]{0:T(128)} %copy-done.55) | copy-start | bytes 28
  975.3 468.6 %copy-start.59 = (s32[2]{0:T(128)S(1)}, s32[2]{0:T(128)}, u32[]{:S(2)}) copy-start(s32[2]{0:T(128)} %copy-done.58) | copy-start | bytes 28
  975.4 468.6 %copy-start.62 = (f32[2]{0:T(128)S(1)}, f32[2]{0:T(128)}, u32[]{:S(2)}) copy-start(f32[2]{0:T(128)} %copy-done.61) | copy-start | bytes 28
  975.4 474.3 %copy-start.39 = (f32[2,180]{1,0:T(2,128)S(1)}, f32[2,180]{1,0:T(2,128)}, u32[]{:S(2)}) copy-start(f32[2,180]{1,0:T(2,128)} %copy-done.38) | copy-start | bytes 4324
  975.4 474.3 %copy-start.46 = (f32[2,180]{1,0:T(2,128)S(1)}, f32[2,180]{1,0:T(2,128)}, u32[]{:S(2)}) copy-start(f32[2,180]{1,0:T(2,128)} %copy-done.45) | copy-start | bytes 4324
  975.4 474.3 %copy-start.50 = (f32[384]{0:T(512)S(1)}, f32[384]{0:T(512)}, u32[]{:S(2)}) copy-start(f32[384]{0:T(512)} %param.21) | copy-start | bytes 4612
  975.4 474.3 %copy-start.65 = (f32[384]{0:T(512)S(1)}, f32[384]{0:T(512)}, u32[]{:S(2)}) copy-start(f32[384]{0:T(512)} %param.22) | copy-start | bytes 4612
  1440.8 8.9 copy-start.21
  1449.8 9.5 copy-start.32
  1449.8 9.5 copy-start.44
  1476.7 18.8 reduce-scatter.17.cloned.1.call-start
  1480.7 5.3 copy-start.6
  1482.6 15.2 copy-start.19
  1482.6 15.3 copy-start.48
  1482.6 578.7 %all-reduce.17.cloned.1.call-start = ((), (), s32[]{:S(2)}) async-start(), calls=%async_computation.9 | async-start | bytes 35389440
  1485.9 13.5 copy-start.63
  1499.5 5.8 copy-start.11
  1581.7 486.8 %copy-start.3 = (bf16[2,180,4,96]{3,1,0,2:T(8,128)(2,1)S(1)}, bf16[2,180,4,96]{3,1,0,2:T(8,128)(2,1)}, u32[]{:S(2)}) copy-start(bf16[2,180,4,96]{3,1,0,2:T(8,128)(2,1)} %copy-done.2) | copy-start | bytes 829444
  1581.7 1082.3 %all-reduce.19.cloned.1.call-start = ((), (), s32[]{:S(2)}) async-start(), calls=%async_computation.10 | async-start | bytes 36962304
  2066.7 6.6 copy-start.9
  2073.3 2.8 copy-start.68
  2079.1 2.9 copy-start.4
  2109.9 26.3 copy-start.23
  2109.9 26.7 copy-start.24
  2165.6 641.1 %reduce-scatter.15.cloned.1.call-start = ((), (), s32[]{:S(2)}) async-start(), calls=%async_computation.5 | async-start | bytes 5013504 | tf_op jit(solution)/shard_map/reduce_scatter | solution.py:311
  2172.3 776.6 %reduce-scatter.13.cloned.1.call-start = ((), (), s32[]{:S(2)}) async-start(), calls=%async_computation.4 | async-start | bytes 5013504 | tf_op jit(solution)/shard_map/reduce_scatter | solution.py:310
  2177.3 489.8 %copy-start.31 = (s32[180,180]{1,0:T(8,128)S(1)}, s32[180,180]{1,0:T(8,128)}, u32[]{:S(2)}) copy-start(s32[180,180]{1,0:T(8,128)} %copy-done.29) | copy-start | bytes 388804
  2177.3 489.8 %copy-start.54 = (pred[2,180]{1,0:T(4,128)(4,1)S(1)}, pred[2,180]{1,0:T(4,128)(4,1)}, u32[]{:S(2)}) copy-start(pred[2,180]{1,0:T(4,128)(4,1)} %copy-done.52) | copy-start | bytes 1084
  2177.3 489.8 %copy-start.57 = (f32[2]{0:T(128)S(1)}, f32[2]{0:T(128)}, u32[]{:S(2)}) copy-start(f32[2]{0:T(128)} %copy-done.55) | copy-start | bytes 28
  2177.4 489.8 %copy-start.60 = (s32[2]{0:T(128)S(1)}, s32[2]{0:T(128)}, u32[]{:S(2)}) copy-start(s32[2]{0:T(128)} %copy-done.58) | copy-start | bytes 28
  2663.9 8.9 copy-start.12
  2663.9 8.9 copy-start.22
  2663.9 8.9 copy-start.37
  2664.0 8.9 copy-start.40
  2664.0 9.0 copy-start.47
  2664.0 9.0 copy-start.51
  2680.2 5.2 copy-start.33
  2680.3 5.2 copy-start.35
  2680.3 5.2 copy-start.41
  2682.9 269.6 %copy-start.1 = (bf16[768,1536]{1,0:T(8,128)(2,1)S(1)}, bf16[768,1536]{1,0:T(8,128)(2,1)}, u32[]{:S(2)}) copy-start(bf16[768,1536]{1,0:T(8,128)(2,1)} %param.29) | copy-start | bytes 7077892
  (12 other events, 15.7 us)
Sparse Core Ops, SparseCore 0:
  965.8 474.9 all-reduce.14
  1476.9 7.1 reduce-scatter.18
  1486.3 9.1 reduce-scatter.16
  1581.8 479.4 all-reduce.16
  2165.8 498.1 all-reduce.18
  2670.4 136.2 reduce-scatter.14
  2812.4 136.3 reduce-scatter.12
where the time goes:
time: 2970 us; the launch traced here: 2960 us
  waiting for transfers between devices  1630 us (55%)
  blocking collectives  845 us (28%)
  matrix products  285 us (10%)
  other arithmetic  122 us (4%)
  local copies, waits for them, and re-layouts  65.1 us (2%)
    unnamed x12, waiting for transfers between devices  1440 us
    unnamed x1, blocking collectives  756 us
    reduce_scatter x1, waiting for transfers between devices, body(): lax.psum_scatter(grad_fc1_weight, 'lat', scatter_dimension=0, tiled=True)  142 us
    dot_general x4, matrix products, complex_rows(): leading = jnp.einsum('ab,bwc->awc', real_mat, values, precision=HIGHEST)  105 us
    dot_general x4, matrix products, complex_rows(): trailing = jnp.einsum('ab,bwc->awc', imag_mat, values, precision=HIGHEST)  81.7 us
    psum x1, blocking collectives, body(): lax.psum((grad_norm1_gain, grad_norm1_bias, grad_spec_w1, grad_spec_b1, g...  74.9 us
  transfers between devices with their start and end apart: 7, of which 7 were waited for; matrix products, arithmetic and copies ran while one was open for 2% of the time, Pallas kernels for 0%

commit v1 on v0

v1 whole, which is shorter than its diff:
```python
import math

import jax
import jax.numpy as jnp
import numpy as np
from jax import lax
from jax.sharding import PartitionSpec as P

LON_FINE = 180
LON_COARSE = 45
GROUPS = 8
EPSILON = 1e-05
SHRINK = 0.01
HALVES = LON_FINE // 2 + 1
BF = jnp.bfloat16
F32 = jnp.float32


def split_two(values):
    high = lax.reduce_precision(values, 8, 7)
    return high.astype(BF), (values - high).astype(BF)


def mm(left, right):
    return lax.dot_general(left, right, (((1,), (0,)), ((), ())), preferred_element_type=F32)


def mm_t(left, right):
    return lax.dot_general(left, right, (((0,), (0,)), ((), ())), preferred_element_type=F32)


def mm_nt(left, right):
    return lax.dot_general(left, right, (((1,), (1,)), ((), ())), preferred_element_type=F32)


def longitude_constant(width, parts, share, rows_dev, columns):
    freq = np.arange(parts * share).reshape(parts, share)
    cols = np.arange(columns)
    phases = (freq[..., None] * cols) % width
    angles = 2.0 * np.pi * phases / width
    inside = (freq[..., None] * 2 <= width) & (cols < width)
    scale = inside / np.sqrt(width)
    pair = np.stack([scale * np.cos(angles), -scale * np.sin(angles)], axis=1)
    full = np.zeros((parts, rows_dev, 2, share, rows_dev, columns), np.float32)
    for r in range(rows_dev):
        full[:, r, :, :, r, :] = pair
    return full.reshape(parts * rows_dev * 2 * share, rows_dev * columns)


def np_split(values):
    high = values.astype(jnp.bfloat16)
    low = (values - high.astype(np.float32)).astype(jnp.bfloat16)
    return high, low


def row_tables(row_group, row_valid):
    member = (row_group[:, None] == jnp.arange(GROUPS, dtype=jnp.int32)[None, :]).astype(
        jnp.int32
    ) * row_valid[:, None]
    counts = jnp.sum(member, axis=0)
    before = jnp.cumsum(member, axis=0) - member
    offset = jnp.sum(before * member, axis=1)
    length = jnp.maximum(jnp.sum(member * counts[None, :], axis=1), 1)
    return (offset, length)


def latitude_tables(row_group, row_valid):
    offset, length = row_tables(row_group, row_valid)
    phases = offset[:, None] * offset[None, :] % length[:, None]
    lengths = length[:, None].astype(F32)
    angles = 2.0 * math.pi * phases.astype(F32) / lengths
    kept = (
        (row_group[:, None] == row_group[None, :])
        & (row_valid[:, None] > 0)
        & (row_valid[None, :] > 0)
    ).astype(F32) * lax.rsqrt(lengths)
    return kept * jnp.cos(angles), kept * jnp.sin(angles)


def latitude_matrix(row_group, row_valid, rows, rows_dev, share, first_freq):
    cos_mat, sin_mat = latitude_tables(row_group, row_valid)
    both = jnp.concatenate([cos_mat, sin_mat], axis=1)
    width = jnp.where(row_group == 0, LON_FINE, LON_COARSE).astype(jnp.int32)
    freq = first_freq + jnp.arange(share, dtype=jnp.int32)
    lone = (freq[None, :] == 0) | (2 * freq[None, :] == width[:, None])
    keep = jnp.stack([jnp.ones((rows, share), F32), 1.0 - lone.astype(F32)]).reshape(-1)
    keep = jnp.concatenate([keep, keep])[:, None]
    left = np.kron(np.eye(rows), np.ones((share, 1))).astype(np.float32)
    right = np.zeros((2, 2, 2, rows, rows, 2, share), np.float32)
    signs = {
        (0, 0): ((1, 0), (0, 1)),
        (1, 0): ((0, 1), (-1, 0)),
        (0, 1): ((1, 0), (0, -1)),
        (1, 1): ((0, -1), (-1, 0)),
    }
    eye = np.eye(rows)[:, :, None]
    for (part, sign), (cos_sign, sin_sign) in signs.items():
        for inner in range(2):
            right[part, sign, 0, :, :, inner, :] = cos_sign[inner] * eye
            right[part, sign, 1, :, :, inner, :] = sin_sign[inner] * eye
    right = right.reshape(4, 2 * rows, rows * 2 * share)
    same = np.kron(np.ones((rows, 2 * rows)), np.eye(share)).astype(np.float32)

    def expand(values):
        spread = mm(jnp.asarray(left, BF), values).astype(BF)
        return jnp.concatenate(
            [mm(spread, jnp.asarray(right[i], BF)) * same for i in range(4)], axis=0
        )

    high, low = split_two(both)
    return (expand(high) * keep).astype(BF), (expand(low) * keep).astype(BF)


def times_split(pair, values):
    high, low = split_two(values)
    return mm(pair[0], high) + mm(pair[1], high) + mm(pair[0], low)


def times_split_t(pair, values):
    high, low = split_two(values)
    return mm_t(pair[0], high) + mm_t(pair[1], high) + mm_t(pair[0], low)


GELU_A = math.sqrt(2.0 / math.pi)
GELU_B = 0.044715


def gelu_pair(v):
    square = v * v
    tanh = jnp.tanh(GELU_A * v * (1.0 + GELU_B * square))
    half = 0.5 * (1.0 + tanh)
    slope = half + 0.5 * v * (1.0 - tanh * tanh) * (GELU_A * (1.0 + 3.0 * GELU_B * square))
    return v * half, slope


def block_diagonal(weight):
    blocks, size = weight.shape[0], weight.shape[1]
    spread = jnp.tile(weight.reshape(blocks * size, size), (1, blocks))
    mask = np.kron(np.eye(blocks), np.ones((size, size))).astype(np.bool_)
    return jnp.where(mask, spread, jnp.zeros_like(spread))


def diagonal_blocks(full, blocks, size):
    return jnp.concatenate(
        [full[n * size : (n + 1) * size, n * size : (n + 1) * size] for n in range(blocks)], axis=0
    )


def normalise(values, total, square, width):
    average = total / width
    inverse = lax.rsqrt(square / width - average * average + EPSILON)
    return (values - average) * inverse, inverse


def body(
    field,
    row_group,
    row_valid,
    norm1_gain,
    norm1_bias,
    spec_w1,
    spec_b1,
    spec_w2,
    spec_b2,
    norm2_gain,
    norm2_bias,
    fc1_weight,
    fc1_bias,
    fc2_weight,
    fc2_bias,
    cotangent,
):
    rows_dev, columns, ch = field.shape
    parts, mp = lax.axis_size("lat"), lax.axis_size("mp")
    me = lax.axis_index("lat")
    rows = rows_dev * parts
    full_width = ch * mp
    tokens = rows_dev * columns
    blocks, size = spec_w1.shape[1], spec_w1.shape[2]
    hidden = fc1_weight.shape[1]
    share = -(-HALVES // parts)
    group = 2 * rows_dev * share
    patches = rows * 2 * share

    lon_fine = longitude_constant(LON_FINE, parts, share, rows_dev, columns)
    lon_coarse = longitude_constant(LON_COARSE, parts, share, rows_dev, columns)
    local_group = lax.dynamic_slice_in_dim(row_group, me * rows_dev, rows_dev)
    local_valid = lax.dynamic_slice_in_dim(row_valid, me * rows_dev, rows_dev)
    pick = jnp.broadcast_to(
        (local_group == 0)[None, :, None], (parts, rows_dev, 2 * share)
    ).reshape(-1, 1)
    lon = tuple(
        jnp.where(pick, jnp.asarray(f), jnp.asarray(c))
        for f, c in zip(np_split(lon_fine), np_split(lon_coarse))
    )
    lat = latitude_matrix(row_group, row_valid, rows, rows_dev, share, me * share)
    keep_row = jnp.broadcast_to((local_valid > 0)[:, None], (rows_dev, columns)).reshape(tokens, 1)

    x_low = field.reshape(tokens, ch)
    dy_low = cotangent.reshape(tokens, ch)
    x = x_low.astype(F32)
    dy = dy_low.astype(F32)

    sums = lax.psum(
        jnp.concatenate(
            [jnp.sum(x, axis=1, keepdims=True), jnp.sum(x * x, axis=1, keepdims=True)], axis=1
        ),
        "mp",
    )
    xh1, inv1 = normalise(x, sums[:, :1], sums[:, 1:], full_width)
    u = xh1 * norm1_gain + norm1_bias

    def to_freq(values):
        packed = times_split(lon, values).astype(BF).reshape(parts, group, ch)
        got = lax.all_to_all(packed, "lat", 0, 0, tiled=True)
        return got.reshape(patches, ch)

    def to_freq32(values):
        packed = times_split(lon, values).reshape(parts, group, ch)
        got = lax.all_to_all(packed, "lat", 0, 0, tiled=True)
        return got.reshape(patches, ch)

    w1r, w1i = block_diagonal(spec_w1[0]), block_diagonal(spec_w1[1])
    w2r, w2i = block_diagonal(spec_w2[0]), block_diagonal(spec_w2[1])
    b1 = spec_b1.reshape(2, 1, ch)
    b2 = spec_b2.reshape(2, 1, ch)

    z = to_freq32(u)
    s = times_split(lat, z).astype(BF)
    sr, si = s[:patches], s[patches:]
    a1r = mm(sr, w1r) - mm(si, w1i) + b1[0]
    a1i = mm(sr, w1i) + mm(si, w1r) + b1[1]
    h1r, slope_r = gelu_pair(a1r)
    h1i, slope_i = gelu_pair(a1i)
    h1r, h1i = h1r.astype(BF), h1i.astype(BF)
    a2r = mm(h1r, w2r) - mm(h1i, w2i) + b2[0]
    a2i = mm(h1r, w2i) + mm(h1i, w2r) + b2[1]
    tr, ti = jnp.tanh(a2r / SHRINK), jnp.tanh(a2i / SHRINK)
    shrunk = jnp.concatenate([a2r - SHRINK * tr, a2i - SHRINK * ti], axis=0)
    eo = times_split_t(lat, shrunk).astype(BF).reshape(parts, group, ch)
    eo = lax.all_to_all(eo, "lat", 0, 0, tiled=True).reshape(parts * group, ch)
    filtered = mm_t(lon[0], eo) + mm_t(lon[1], eo)
    x1 = x + filtered + u

    x1_all = lax.all_gather(x1, "mp", axis=1, tiled=True)
    gain2 = lax.all_gather(jnp.stack([norm2_gain, norm2_bias]), "mp", axis=1, tiled=True)
    dy_all = lax.all_gather(dy_low, "mp", axis=1, tiled=True)
    xh2, inv2 = normalise(
        x1_all,
        jnp.sum(x1_all, axis=1, keepdims=True),
        jnp.sum(x1_all * x1_all, axis=1, keepdims=True),
        full_width,
    )
    n = (xh2 * gain2[0] + gain2[1]).astype(BF)
    p = mm(n, fc1_weight) + fc1_bias
    q, slope = gelu_pair(p)
    q = q.astype(BF)
    dp = (mm_nt(dy_all, fc2_weight) * slope).astype(BF)
    out_part = mm(q, fc2_weight)
    dn_part = mm_nt(dp, fc1_weight)
    g_fc1 = mm_t(n, dp)
    g_fc2 = mm_t(dy_all, q)
    g_fc1_bias = jnp.sum(dp.astype(F32), axis=0)
    scaled = dn_part * gain2[0]
    stat2 = lax.psum(
        jnp.concatenate(
            [
                jnp.sum(scaled, axis=1, keepdims=True),
                jnp.sum(scaled * xh2, axis=1, keepdims=True),
            ],
            axis=1,
        ),
        "mp",
    )
    both = jnp.stack([out_part, dn_part]).astype(BF).reshape(2, tokens, mp, ch)
    both = lax.all_to_all(both.transpose(2, 0, 1, 3), "mp", 0, 0, tiled=True)
    both = jnp.sum(both.astype(F32), axis=0)
    out_field = (x1 + both[0] + fc2_bias).astype(BF)
    dn = both[1]

    weights = jnp.stack(
        [g_fc1.reshape(parts, full_width // parts, hidden), g_fc2.reshape(parts, full_width // parts, hidden)],
        axis=1,
    ).astype(BF)
    weights = lax.all_to_all(weights, "lat", 0, 0, tiled=True)
    weights = jnp.sum(weights.astype(F32), axis=0)

    mine = lax.axis_index("mp") * ch
    xh2_own = lax.dynamic_slice_in_dim(xh2, mine, ch, axis=1)
    dx1 = dy + inv2 * (
        dn * norm2_gain - stat2[:, :1] / full_width - xh2_own * (stat2[:, 1:] / full_width)
    )
    g_norm2_gain = jnp.sum(dn * xh2_own, axis=0)
    g_norm2_bias = jnp.sum(dn, axis=0)

    dz = to_freq(jnp.where(keep_row, dx1, 0.0))
    dsh = mm(lat[0], dz) + mm(lat[1], dz)
    dar = (dsh[:patches] * (tr * tr)).astype(BF)
    dai = (dsh[patches:] * (ti * ti)).astype(BF)
    g_w2r = mm_t(h1r, dar) + mm_t(h1i, dai)
    g_w2i = mm_t(h1r, dai) - mm_t(h1i, dar)
    dhr = mm_nt(dar, w2r) + mm_nt(dai, w2i)
    dhi = mm_nt(dai, w2r) - mm_nt(dar, w2i)
    dcr = (dhr * slope_r).astype(BF)
    dci = (dhi * slope_i).astype(BF)
    g_w1r = mm_t(sr, dcr) + mm_t(si, dci)
    g_w1i = mm_t(sr, dci) - mm_t(si, dcr)
    dspectrum = jnp.concatenate(
        [mm_nt(dcr, w1r) + mm_nt(dci, w1i), mm_nt(dci, w1r) - mm_nt(dcr, w1i)], axis=0
    )
    deo = times_split_t(lat, dspectrum).astype(BF).reshape(parts, group, ch)
    g_spec = jnp.concatenate(
        [diagonal_blocks(g, blocks, size) for g in (g_w1r, g_w1i, g_w2r, g_w2i)], axis=0
    )
    spec_rows = g_spec.size // (parts * ch)
    g_spec = g_spec.astype(BF).reshape(parts, spec_rows, ch)
    deo = jnp.concatenate([deo, g_spec], axis=1)
    deo = lax.all_to_all(deo, "lat", 0, 0, tiled=True)
    g_spec = jnp.sum(deo[:, group:].astype(F32), axis=0)
    deo = deo[:, :group].reshape(parts * group, ch)
    du = dx1 + mm_t(lon[0], deo) + mm_t(lon[1], deo)

    scaled = du * norm1_gain
    stat1 = lax.psum(
        jnp.concatenate(
            [
                jnp.sum(scaled, axis=1, keepdims=True),
                jnp.sum(scaled * xh1, axis=1, keepdims=True),
            ],
            axis=1,
        ),
        "mp",
    )
    grad_field = dx1 + inv1 * (
        scaled - stat1[:, :1] / full_width - xh1 * (stat1[:, 1:] / full_width)
    )

    def column_sums(values):
        return jnp.sum(values.astype(F32), axis=0)

    small = [
        column_sums(du * xh1),
        column_sums(du),
        column_sums(dcr),
        column_sums(dci),
        column_sums(dar),
        column_sums(dai),
        g_norm2_gain,
        g_norm2_bias,
        column_sums(dy),
        g_fc1_bias,
    ]
    small = jnp.concatenate(small).reshape(-1, ch)
    tail = jnp.concatenate([g_spec, small], axis=0)
    tail = lax.all_to_all(
        jnp.broadcast_to(tail[None], (parts, *tail.shape)), "lat", 0, 0, tiled=True
    )
    small = jnp.sum(tail[:, spec_rows:], axis=0)
    g_spec = tail[:, :spec_rows].reshape(2, 2, blocks, size, size)
    return (
        out_field.reshape(field.shape),
        grad_field.reshape(field.shape),
        small[0],
        small[1],
        g_spec[0],
        small[2:4].reshape(2, blocks, size),
        g_spec[1],
        small[4:6].reshape(2, blocks, size),
        small[6],
        small[7],
        weights[0],
        small[9:].reshape(hidden),
        weights[1].T,
        small[8],
    )


def solution(mesh):
    placed = (
        P("lat", None, "mp"),
        P(),
        P(),
        P("mp"),
        P("mp"),
        P(None, "mp", None, None),
        P(None, "mp", None),
        P(None, "mp", None, None),
        P(None, "mp", None),
        P("mp"),
        P("mp"),
        P(None, "mp"),
        P("mp"),
        P("mp", None),
        P("mp"),
        P("lat", None, "mp"),
    )
    return jax.shard_map(
        body,
        mesh=mesh,
        in_specs=placed,
        out_specs=(
            P("lat", None, "mp"),
            P("lat", None, "mp"),
            P("mp"),
            P("mp"),
            P(None, "mp", None, None),
            P(None, "mp", None),
            P(None, "mp", None, None),
            P(None, "mp", None),
            P("mp"),
            P("mp"),
            P("lat", "mp"),
            P("mp"),
            P("mp", "lat"),
            P("mp"),
        ),
        check_vma=False,
    )
```

time: 2970 us -> 323 us (0.11)
  the two profiles are of different devices: /device:TPU:0 before, /device:TPU:14 now
where the time goes in v1:
time: 323 us; the launch traced here: 321 us
  waiting for transfers between devices  121 us (37%)
  matrix products  49.7 us (15%)
  blocking collectives  43.8 us (14%)
  local copies, waits for them, and re-layouts  39.1 us (12%)
  starting transfers between devices  29.2 us (9%)
  other arithmetic  23 us (7%)
  between operations  15.6 us (5%)
    all_to_all x1, waiting for transfers between devices, body(): weights = lax.all_to_all(weights, 'lat', 0, 0, tiled=True)  93.7 us
    dot_general x31, matrix products, mm(): lax.dot_general(left, right, (((1,), (0,)), ((), ())), preferred_element_...  24.1 us
    all_to_all x1, blocking collectives, to_freq(): got = lax.all_to_all(packed, 'lat', 0, 0, tiled=True)  14.8 us
    all_to_all x1, waiting for transfers between devices, body(): lax.all_to_all(jnp.broadcast_to(tail[None], (parts, *tail.shape)), 'lat',...  14.8 us
    all_to_all x1, blocking collectives, body(): eo = lax.all_to_all(eo, 'lat', 0, 0, tiled=True).reshape(parts * group, ch)  14.7 us
    dot_general x20, matrix products, mm_t(): lax.dot_general(left, right, (((0,), (0,)), ((), ())), preferred_element_...  14.6 us
    all_to_all x1, waiting for transfers between devices, body(): deo = lax.all_to_all(deo, 'lat', 0, 0, tiled=True)  12.6 us
    unnamed x190, local copies, waits for them, and re-layouts  11 us
  transfers between devices with their start and end apart: 6, of which 3 were waited for; matrix products, arithmetic and copies ran while one was open for 12% of the time, Pallas kernels for 0%

profile of v1, /device:TPU:14, one launch (start us, length us, event | category | flops | bytes accessed | tf_op | source)
XLA Modules:
  0.0 321.4 jit_solution(15430993906033152529)
XLA Ops:
  7.3 1.9 copy.75
  9.2 2.2 convert_reduce_fusion.9
  11.4 1.1 reshape.284
  13.3 1.0 copy.77
  14.4 1.0 copy.76
  15.5 2.5 psum.21
  19.5 1.3 convolution_add_fusion.10
  20.8 7.3 %all-to-all-start = ((f32[16,24,384]{2,1,0:T(8,128)}), f32[16,24,384]{2,1,0:T(8,128)}, u32[]{:S(2)}, u32[]{:S(2)}) async-start(f32[16,24,384]{2,1,0:T(8,128)} %bitcast.163), calls=%async_computation | async-start | bytes 1179648 | tf_op jit(solution)/shard_map/all_to_all | solution.py:220
  29.4 0.9 convolution_multiply_fusion.1
  30.4 0.9 convolution_multiply_fusion.2
  31.3 0.9 convolution_multiply_fusion.5
  32.2 0.9 convolution_multiply_fusion.6
  33.2 0.9 convolution_multiply_fusion.3
  34.1 0.9 convolution_multiply_fusion.7
  36.6 1.0 fusion.100
  39.1 1.0 fusion.101
  42.7 2.5 fusion.22
  45.3 1.1 broadcast_select_fusion.13
  46.4 1.2 fusion.23
  50.8 1.3 multiply_convert_fusion.2
  53.6 1.3 multiply_convert_fusion.1
  54.9 1.3 multiply_subtract_fusion
  56.2 1.3 multiply_subtract_fusion.1
  59.0 14.7 %all_to_all.35 = bf16[16,24,384]{2,1,0:T(8,128)(2,1)S(1)} all-to-all(bf16[16,24,384]{2,1,0:T(8,128)(2,1)S(1)} %bitcast.171), channel_id=1, replica_groups=mesh['lat'=16,'mp'=2] {'lat'}, dimensions={0} | all-to-all | bytes 589824 | tf_op jit(solution)/shard_map/all_to_all | solution.py:241
  74.3 1.4 fusion.9
  75.7 1.7 copy.82
  77.4 1.7 reshape.273
  79.3 1.8 all_gather.10
  81.2 4.9 %all_gather.11 = bf16[360,768]{1,0:T(8,128)(2,1)} all-gather(bf16[360,384]{1,0:T(8,128)(2,1)} %reshape.273), channel_id=1, replica_groups=mesh['lat'=16,'mp'=2] {'mp'}, dimensions={1}, use_global_device_ids=true | all-gather | bytes 829440 | tf_op jit(solution)/shard_map/all_gather | solution.py:247
  86.1 1.5 fusion.92
  88.4 2.7 convolution_add_fusion
  91.1 2.3 convolution_convert_fusion.2
  93.4 2.5 convert_reduce_fusion.1
  95.9 1.2 multiply_reduce_fusion.2
  98.4 1.2 maximum_bitcast_fusion
  99.5 3.6 %all-to-all-start.2 = ((bf16[2,2,360,384]{3,2,1,0:T(8,128)(2,1)}), bf16[2,2,360,384]{3,2,1,0:T(8,128)(2,1)S(1)}, u32[]{:S(2)}, u32[]{:S(2)}) async-start(bf16[2,2,360,384]{3,2,1,0:T(8,128)(2,1)} %maximum_bitcast_fusion), calls=%async_computation.2 | async-start | bytes 2211840 | tf_op jit(solution)/shard_map/all_to_all | solution.py:276
  103.2 2.6 psum.22
  106.0 2.8 fusion.37
  110.8 14.8 %all_to_all.36 = bf16[16,24,384]{2,1,0:T(8,128)(2,1)S(1)} all-to-all(bf16[16,24,384]{2,1,0:T(8,128)(2,1)S(1)} %bitcast.166), channel_id=1, replica_groups=mesh['lat'=16,'mp'=2] {'lat'}, dimensions={0} | all-to-all | bytes 589824 | tf_op jit(solution)/shard_map/all_to_all | solution.py:215
  130.3 1.2 convert_reduce_fusion.5
  132.5 1.2 fusion.112
  133.7 1.2 convert_reduce_fusion.6
  135.2 1.2 fusion.110
  140.9 1.1 concatenate.50
  142.0 0.9 copy.85
  142.9 2.1 convert_element_type.204
  145.0 1.6 convolution_subtract_fusion.2
  149.8 6.2 %all-to-all-start.4 = ((bf16[16,48,384]{2,1,0:T(8,128)(2,1)}), bf16[16,48,384]{2,1,0:T(8,128)(2,1)S(1)}, u32[]{:S(2)}, u32[]{:S(2)}) async-start(bf16[16,48,384]{2,1,0:T(8,128)(2,1)} %pad_maximum_fusion.3), calls=%async_computation.4 | async-start | bytes 1179648 | tf_op jit(solution)/shard_map/all_to_all | solution.py:318
  156.0 1.3 convert_reduce_fusion.8
  157.4 12.6 %all-to-all-done.4 = bf16[16,48,384]{2,1,0:T(8,128)(2,1)S(1)} async-done(((bf16[16,48,384]{2,1,0:T(8,128)(2,1)}), bf16[16,48,384]{2,1,0:T(8,128)(2,1)S(1)}, u32[]{:S(2)}, u32[]{:S(2)}) %all-to-all-start.4) | async-done | bytes 589856 | tf_op jit(solution)/shard_map/all_to_all | solution.py:318
  170.6 1.4 multiply_reduce_fusion.3
  172.2 1.0 broadcast_in_dim.112
  173.2 6.1 %all-to-all-start.5 = ((f32[16,37,384]{2,1,0:T(8,128)}), f32[16,37,384]{2,1,0:T(8,128)S(1)}, u32[]{:S(2)}, u32[]{:S(2)}) async-start(f32[16,37,384]{2,1,0:T(8,128)} %broadcast_in_dim.112), calls=%async_computation.5 | async-start | bytes 1966080 | tf_op jit(solution)/shard_map/all_to_all | solution.py:355
  179.4 3.2 convolution_convert_fusion.1
  182.6 1.6 convolution_convert_fusion
  184.2 2.6 pad_maximum_fusion
  186.7 14.8 %all-to-all-done.5 = f32[16,37,384]{2,1,0:T(8,128)S(1)} async-done(((f32[16,37,384]{2,1,0:T(8,128)}), f32[16,37,384]{2,1,0:T(8,128)S(1)}, u32[]{:S(2)}, u32[]{:S(2)}) %all-to-all-start.5) | async-done | bytes 909344 | tf_op jit(solution)/shard_map/all_to_all | solution.py:355
  201.5 5.9 %all-to-all-start.6 = ((bf16[16,2,48,1536]{3,2,1,0:T(8,128)(2,1)}), bf16[16,2,48,1536]{3,2,1,0:T(8,128)(2,1)}, u32[]{:S(2)}, u32[]{:S(2)}) async-start(bf16[16,2,48,1536]{3,2,1,0:T(8,128)(2,1)} %pad_maximum_fusion), calls=%async_computation.6 | async-start | bytes 9437184 | tf_op jit(solution)/shard_map/all_to_all | solution.py:285
  207.5 0.9 copy.88
  208.4 2.5 psum.23
  211.3 1.1 copy.89
  212.4 0.9 squeeze.41
  216.8 93.7 %all-to-all-done.6 = bf16[16,2,48,1536]{3,2,1,0:T(8,128)(2,1)} async-done(((bf16[16,2,48,1536]{3,2,1,0:T(8,128)(2,1)}), bf16[16,2,48,1536]{3,2,1,0:T(8,128)(2,1)}, u32[]{:S(2)}, u32[]{:S(2)}) %all-to-all-start.6) | async-done | bytes 4718624 | tf_op jit(solution)/shard_map/all_to_all | solution.py:285
  310.5 3.2 %convert_reduce_fusion = f32[2,48,1536]{2,1,0:T(8,128)S(1)} fusion(bf16[16,2,48,1536]{3,2,1,0:T(8,128)(2,1)} %all-to-all-done.6), kind=kLoop, calls=%fused_computation | loop fusion | flops 4571136 | bytes 5308416 | tf_op jit(solution)/shard_map/reduce_sum | solution.py:286
  (307 shorter events, 39.4 us)
Async XLA Ops:
  7.2 83.9 %copy-start = (bf16[1536,768]{1,0:T(8,128)(2,1)S(1)}, bf16[1536,768]{1,0:T(8,128)(2,1)}, u32[]{:S(2)}) copy-start(bf16[1536,768]{1,0:T(8,128)(2,1)} %param.48) | copy-start | bytes 7077892
  7.2 5.3 %copy-start.63 = (s32[32]{0:T(128)S(1)}, s32[32]{0:T(128)}, u32[]{:S(2)}) copy-start(s32[32]{0:T(128)} %param.36) | copy-start | bytes 388
  7.2 5.3 %copy-start.67 = (s32[32]{0:T(128)S(1)}, s32[32]{0:T(128)}, u32[]{:S(2)}) copy-start(s32[32]{0:T(128)} %param.37) | copy-start | bytes 388
  7.2 10.7 %copy-start.3 = (bf16[384,360]{1,0:T(8,128)(2,1)S(1)}, bf16[384,360]{1,0:T(8,128)(2,1)}, u32[]{:S(2)}) copy-start(bf16[384,360]{1,0:T(8,128)(2,1)} %constant.106.clone) | copy-start | bytes 829444
  7.2 10.7 %copy-start.6 = (bf16[384,360]{1,0:T(8,128)(2,1)S(1)}, bf16[384,360]{1,0:T(8,128)(2,1)}, u32[]{:S(2)}) copy-start(bf16[384,360]{1,0:T(8,128)(2,1)} %constant.107.clone) | copy-start | bytes 829444
  7.2 10.7 %copy-start.59 = (f32[384]{0:T(512)S(1)}, f32[384]{0:T(512)}, u32[]{:S(2)}) copy-start(f32[384]{0:T(512)} %param.38) | copy-start | bytes 4612
  7.3 10.7 %copy-start.62 = (f32[384]{0:T(512)S(1)}, f32[384]{0:T(512)}, u32[]{:S(2)}) copy-start(f32[384]{0:T(512)} %param.39) | copy-start | bytes 4612
  13.3 97.0 %copy-start.60 = (pred[384]{0:T(512)(128)(4,1)}, pred[384]{0:T(512)(128)(4,1)S(1)}, u32[]{:S(2)}) copy-start(pred[384]{0:T(512)(128)(4,1)S(1)} %broadcast_in_dim.56) | copy-start | bytes 1156
  20.8 7.5 %copy-start.68 = (s32[32]{0:T(128)S(1)}, s32[32]{0:T(128)}, u32[]{:S(2)}) copy-start(s32[32]{0:T(128)} %param.37) | copy-start | bytes 388
  20.8 8.1 %copy-start.53 = (bf16[192,32]{1,0:T(8,128)(2,1)S(1)}, bf16[192,32]{1,0:T(8,128)(2,1)}, u32[]{:S(2)}) copy-start(bf16[192,32]{1,0:T(8,128)(2,1)} %constant.110.clone) | copy-start | bytes 36868
  20.8 8.6 %copy-start.2 = (f32[192,384]{1,0:T(8,128)S(1)}, f32[192,384]{1,0:T(8,128)}, u32[]{:S(2)}) copy-start(f32[192,384]{1,0:T(8,128)} %constant.112.clone) | copy-start | bytes 884740
  20.8 8.6 %copy-start.57 = (bf16[64,384]{1,0:T(8,128)(2,1)S(1)}, bf16[64,384]{1,0:T(8,128)(2,1)}, u32[]{:S(2)}) copy-start(bf16[64,384]{1,0:T(8,128)(2,1)} %constant.115.clone) | copy-start | bytes 147460
  20.8 9.6 %copy-start.56 = (bf16[64,384]{1,0:T(8,128)(2,1)S(1)}, bf16[64,384]{1,0:T(8,128)(2,1)}, u32[]{:S(2)}) copy-start(bf16[64,384]{1,0:T(8,128)(2,1)} %constant.114.clone) | copy-start | bytes 147460
  20.8 25.6 %all-to-all-start = ((f32[16,24,384]{2,1,0:T(8,128)}), f32[16,24,384]{2,1,0:T(8,128)}, u32[]{:S(2)}, u32[]{:S(2)}) async-start(f32[16,24,384]{2,1,0:T(8,128)} %bitcast.163), calls=%async_computation | async-start | bytes 1179648 | tf_op jit(solution)/shard_map/all_to_all | solution.py:220
  28.1 58.0 %all-gather.2.cloned.1.call-start = ((), (), s32[]{:S(2)}) async-start(), calls=%async_computation.7 | async-start | bytes 1658880 | tf_op jit(solution)/shard_map/all_gather | solution.py:245
  29.4 3.8 %copy-start.55 = (bf16[64,384]{1,0:T(8,128)(2,1)S(1)}, bf16[64,384]{1,0:T(8,128)(2,1)}, u32[]{:S(2)}) copy-start(bf16[64,384]{1,0:T(8,128)(2,1)} %constant.113.clone) | copy-start | bytes 147460
  32.2 3.0 copy-start.73
  32.2 3.7 %copy-start.74 = (f32[2,4,96]{2,1,0:T(4,128)S(1)}, f32[2,4,96]{2,1,0:T(4,128)}, u32[]{:S(2)}) copy-start(f32[2,4,96]{2,1,0:T(4,128)} %param.41) | copy-start | bytes 9220
  34.1 8.1 %copy-start.54 = (bf16[64,384]{1,0:T(8,128)(2,1)S(1)}, bf16[64,384]{1,0:T(8,128)(2,1)}, u32[]{:S(2)}) copy-start(bf16[64,384]{1,0:T(8,128)(2,1)} %constant.111.clone) | copy-start | bytes 147460
  42.7 2.6 copy-start.49
  42.7 2.6 copy-start.50
  42.7 2.6 copy-start.51
  42.7 2.6 copy-start.52
  42.7 2.6 copy-start.58
  49.2 4.3 %copy-start.11 = (bf16[768,384]{1,0:T(8,128)(2,1)}, bf16[768,384]{1,0:T(8,128)(2,1)S(1)}, u32[]{:S(2)}) copy-start(bf16[768,384]{1,0:T(8,128)(2,1)S(1)} %fusion.1) | copy-start | bytes 1769476
  58.4 15.3 %copy-start.4 = (bf16[384,360]{1,0:T(8,128)(2,1)S(1)}, bf16[384,360]{1,0:T(8,128)(2,1)}, u32[]{:S(2)}) copy-start(bf16[384,360]{1,0:T(8,128)(2,1)} %constant.106.clone) | copy-start | bytes 829444
  58.5 15.3 %copy-start.7 = (bf16[384,360]{1,0:T(8,128)(2,1)S(1)}, bf16[384,360]{1,0:T(8,128)(2,1)}, u32[]{:S(2)}) copy-start(bf16[384,360]{1,0:T(8,128)(2,1)} %constant.107.clone) | copy-start | bytes 829444
  59.0 15.3 %copy-start.18 = (bf16[384,360]{1,0:T(8,128)(2,1)S(1)}, bf16[384,360]{1,0:T(8,128)(2,1)}, u32[]{:S(2)}) copy-start(bf16[384,360]{1,0:T(8,128)(2,1)} %constant.108.clone) | copy-start | bytes 829444
  59.0 15.3 %copy-start.22 = (bf16[384,360]{1,0:T(8,128)(2,1)S(1)}, bf16[384,360]{1,0:T(8,128)(2,1)}, u32[]{:S(2)}) copy-start(bf16[384,360]{1,0:T(8,128)(2,1)} %constant.109.clone) | copy-start | bytes 829444
  75.7 3.5 %copy-start.81 = (pred[2]{0:T(512)(128)(4,1)S(1)}, pred[2]{0:T(512)(128)(4,1)}, u32[]{:S(2)}) copy-start(pred[2]{0:T(512)(128)(4,1)} %get-tuple-element.167) | copy-start | bytes 10
  81.1 6.7 %copy-start.71 = (f32[768]{0:T(1024)}, f32[768]{0:T(1024)S(1)}, u32[]{:S(2)}) copy-start(f32[768]{0:T(1024)S(1)} %get-tuple-element.86) | copy-start | bytes 9220
  81.2 14.7 %copy-start.69 = (f32[768]{0:T(1024)}, f32[768]{0:T(1024)S(1)}, u32[]{:S(2)}) copy-start(f32[768]{0:T(1024)S(1)} %get-tuple-element.85) | copy-start | bytes 9220
  86.1 1.6 copy-start.36
  87.9 8.0 %copy-start.39 = (f32[360,768]{1,0:T(8,128)}, f32[360,768]{1,0:T(8,128)S(1)}, u32[]{:S(2)}) copy-start(f32[360,768]{1,0:T(8,128)S(1)} %subtract_multiply_fusion) | copy-start | bytes 3317764
  91.1 2.3 copy-start.87
  91.1 2.3 copy-start.46
  93.4 2.5 copy-start.82
  99.5 6.3 %all-to-all-start.2 = ((bf16[2,2,360,384]{3,2,1,0:T(8,128)(2,1)}), bf16[2,2,360,384]{3,2,1,0:T(8,128)(2,1)S(1)}, u32[]{:S(2)}, u32[]{:S(2)}) async-start(bf16[2,2,360,384]{3,2,1,0:T(8,128)(2,1)} %maximum_bitcast_fusion), calls=%async_computation.2 | async-start | bytes 2211840 | tf_op jit(solution)/shard_map/all_to_all | solution.py:276
  103.1 2.9 copy-start.80
  106.0 2.8 copy-start.15
  106.0 2.8 copy-start.5
  106.0 2.8 copy-start.8
  110.3 15.3 %copy-start.10 = (bf16[768,384]{1,0:T(8,128)(2,1)S(1)}, bf16[768,384]{1,0:T(8,128)(2,1)}, u32[]{:S(2)}) copy-start(bf16[768,384]{1,0:T(8,128)(2,1)} %get-tuple-element.142) | copy-start | bytes 1769476
  131.4 5.0 %copy-start.29 = (bf16[384,384]{1,0:T(8,128)(2,1)}, bf16[384,384]{1,0:T(8,128)(2,1)S(1)}, u32[]{:S(2)}) copy-start(bf16[384,384]{1,0:T(8,128)(2,1)S(1)} %get-tuple-element.164) | copy-start | bytes 884740
  131.5 2.2 copy-start.84
  134.8 2.7 copy-start.31
  136.8 1.8 copy-start.33
  140.2 4.9 %copy-start.26 = (bf16[384,4,96]{0,2,1:T(8,128)(2,1)S(1)}, bf16[384,4,96]{0,2,1:T(8,128)(2,1)}, u32[]{:S(2)}) copy-start(bf16[384,4,96]{0,2,1:T(8,128)(2,1)} %get-tuple-element.133) | copy-start | bytes 884740
  142.9 3.6 %copy-start.30 = (bf16[384,384]{1,0:T(8,128)(2,1)S(1)}, bf16[384,384]{1,0:T(8,128)(2,1)}, u32[]{:S(2)}) copy-start(bf16[384,384]{1,0:T(8,128)(2,1)} %copy-done.29) | copy-start | bytes 884740
  145.0 1.6 copy-start.40
  148.9 8.4 %copy-start.16 = (f32[2,360,384]{2,1,0:T(8,128)S(1)}, f32[2,360,384]{2,1,0:T(8,128)}, u32[]{:S(2)}) copy-start(f32[2,360,384]{2,1,0:T(8,128)} %copy-done.15) | copy-start | bytes 3317764
  149.8 20.2 %copy-start.61 = (pred[384]{0:T(512)(128)(4,1)S(1)}, pred[384]{0:T(512)(128)(4,1)}, u32[]{:S(2)}) copy-start(pred[384]{0:T(512)(128)(4,1)} %copy-done.60) | copy-start | bytes 1156
  149.8 20.1 %all-to-all-start.4 = ((bf16[16,48,384]{2,1,0:T(8,128)(2,1)}), bf16[16,48,384]{2,1,0:T(8,128)(2,1)S(1)}, u32[]{:S(2)}, u32[]{:S(2)}) async-start(bf16[16,48,384]{2,1,0:T(8,128)(2,1)} %pad_maximum_fusion.3), calls=%async_computation.4 | async-start | bytes 1179648 | tf_op jit(solution)/shard_map/all_to_all | solution.py:318
  157.4 13.1 %copy-start.20 = (bf16[384,360]{1,0:T(8,128)(2,1)S(1)}, bf16[384,360]{1,0:T(8,128)(2,1)}, u32[]{:S(2)}) copy-start(bf16[384,360]{1,0:T(8,128)(2,1)} %constant.108.clone) | copy-start | bytes 829444
  157.4 13.1 %copy-start.24 = (bf16[384,360]{1,0:T(8,128)(2,1)S(1)}, bf16[384,360]{1,0:T(8,128)(2,1)}, u32[]{:S(2)}) copy-start(bf16[384,360]{1,0:T(8,128)(2,1)} %constant.109.clone) | copy-start | bytes 829444
  173.2 6.2 %copy-start.70 = (f32[768]{0:T(1024)S(1)}, f32[768]{0:T(1024)}, u32[]{:S(2)}) copy-start(f32[768]{0:T(1024)} %copy-done.69) | copy-start | bytes 9220
  173.2 6.2 %copy-start.72 = (f32[768]{0:T(1024)S(1)}, f32[768]{0:T(1024)}, u32[]{:S(2)}) copy-start(f32[768]{0:T(1024)} %copy-done.71) | copy-start | bytes 9220
  173.2 28.3 %all-to-all-start.5 = ((f32[16,37,384]{2,1,0:T(8,128)}), f32[16,37,384]{2,1,0:T(8,128)S(1)}, u32[]{:S(2)}, u32[]{:S(2)}) async-start(f32[16,37,384]{2,1,0:T(8,128)} %broadcast_in_dim.112), calls=%async_computation.5 | async-start | bytes 1966080 | tf_op jit(solution)/shard_map/all_to_all | solution.py:355
  179.4 3.2 copy-start.47
  179.4 3.2 copy-start.88
  186.7 20.7 %copy-start.45 = (bf16[360,384]{1,0:T(8,128)(2,1)S(1)}, bf16[360,384]{1,0:T(8,128)(2,1)}, u32[]{:S(2)}) copy-start(bf16[360,384]{1,0:T(8,128)(2,1)} %get-tuple-element.103) | copy-start | bytes 829444
  201.5 109.0 %all-to-all-start.6 = ((bf16[16,2,48,1536]{3,2,1,0:T(8,128)(2,1)}), bf16[16,2,48,1536]{3,2,1,0:T(8,128)(2,1)}, u32[]{:S(2)}, u32[]{:S(2)}) async-start(bf16[16,2,48,1536]{3,2,1,0:T(8,128)(2,1)} %pad_maximum_fusion), calls=%async_computation.6 | async-start | bytes 9437184 | tf_op jit(solution)/shard_map/all_to_all | solution.py:285
  207.4 3.5 %copy-start.43 = (f32[360,384]{1,0:T(8,128)S(1)}, f32[360,384]{1,0:T(8,128)}, u32[]{:S(2)}) copy-start(f32[360,384]{1,0:T(8,128)} %get-tuple-element.160) | copy-start | bytes 1658884
  310.5 4.1 %copy-start.1 = (bf16[1536,768]{1,0:T(8,128)(2,1)S(1)}, bf16[1536,768]{1,0:T(8,128)(2,1)}, u32[]{:S(2)}) copy-start(bf16[1536,768]{1,0:T(8,128)(2,1)} %param.48) | copy-start | bytes 7077892
  (31 other events, 35.7 us)
Sparse Core Ops, SparseCore 0:
  75.8 9.3 all-gather.1

commit v2 on v1

v2 whole, which is shorter than its diff:
```python
import functools
import math

import jax
import jax.numpy as jnp
import numpy as np
from jax import lax
from jax.experimental import pallas as pl
from jax.experimental.pallas import tpu as pltpu
from jax.sharding import PartitionSpec as P

LON_FINE = 180
LON_COARSE = 45
GROUPS = 8
EPSILON = 1e-05
SHRINK = 0.01
HALVES = LON_FINE // 2 + 1
BF = jnp.bfloat16
F32 = jnp.float32


def split_two(values):
    high = lax.reduce_precision(values, 8, 7)
    return high.astype(BF), (values - high).astype(BF)


def mm(left, right):
    return lax.dot_general(left, right, (((1,), (0,)), ((), ())), preferred_element_type=F32)


def mm_t(left, right):
    return lax.dot_general(left, right, (((0,), (0,)), ((), ())), preferred_element_type=F32)


def mm_nt(left, right):
    return lax.dot_general(left, right, (((1,), (1,)), ((), ())), preferred_element_type=F32)


def np_split(values):
    high = values.astype(jnp.bfloat16)
    low = (values - high.astype(np.float32)).astype(jnp.bfloat16)
    return high, low


def row_tables(row_group, row_valid):
    member = (row_group[:, None] == jnp.arange(GROUPS, dtype=jnp.int32)[None, :]).astype(
        jnp.int32
    ) * row_valid[:, None]
    counts = jnp.sum(member, axis=0)
    before = jnp.cumsum(member, axis=0) - member
    offset = jnp.sum(before * member, axis=1)
    length = jnp.maximum(jnp.sum(member * counts[None, :], axis=1), 1)
    return (offset, length)


def latitude_tables(row_group, row_valid):
    offset, length = row_tables(row_group, row_valid)
    phases = offset[:, None] * offset[None, :] % length[:, None]
    lengths = length[:, None].astype(F32)
    angles = 2.0 * math.pi * phases.astype(F32) / lengths
    kept = (
        (row_group[:, None] == row_group[None, :])
        & (row_valid[:, None] > 0)
        & (row_valid[None, :] > 0)
    ).astype(F32) * lax.rsqrt(lengths)
    return kept * jnp.cos(angles), kept * jnp.sin(angles)


PIECES = 3
GELU_A = math.sqrt(2.0 / math.pi)
GELU_B = 0.044715


def longitude_tables(parts, share, rows_dev, columns, padded):
    freq = np.arange(parts * share).reshape(parts, share)
    cols = np.arange(columns)
    pairs = []
    for width in (LON_COARSE, LON_FINE):
        angles = 2.0 * np.pi * ((freq[..., None] * cols) % width) / width
        inside = (freq[..., None] * 2 <= width) & (cols < width)
        scale = inside / np.sqrt(width)
        pairs.append(np.stack([scale * np.cos(angles), -scale * np.sin(angles)], axis=1))
    full = np.zeros((2**rows_dev, parts, rows_dev, 2, share, rows_dev, padded), np.float32)
    for choice in range(2**rows_dev):
        for r in range(rows_dev):
            full[choice, :, r, :, :, r, :columns] = pairs[(choice >> r) & 1]
    return np_split(full.reshape(2**rows_dev, parts * rows_dev * 2 * share, rows_dev * padded))


def latitude_spread(rows, share):
    left = np.kron(np.eye(rows), np.ones((share, 1)))
    right = np.zeros((2, 2, 2, rows, rows, 2, share))
    signs = {
        (0, 0): ((1, 0), (0, 1)),
        (1, 0): ((0, 1), (-1, 0)),
        (0, 1): ((1, 0), (0, -1)),
        (1, 1): ((0, -1), (-1, 0)),
    }
    eye = np.eye(rows)[:, :, None]
    for (part, sign), (cos_sign, sin_sign) in signs.items():
        for inner in range(2):
            right[part, sign, 0, :, :, inner, :] = cos_sign[inner] * eye
            right[part, sign, 1, :, :, inner, :] = sin_sign[inner] * eye
    same = np.kron(np.ones((rows, 2 * rows)), np.eye(share))
    low = jnp.bfloat16
    return left.astype(low), right.reshape(4, 2 * rows, -1).astype(low), same.astype(low)


def split_in(values):
    high = values.astype(BF)
    return high, (values - high.astype(F32)).astype(BF)


def times(pair, values):
    high, low = split_in(values)
    return mm(pair[0], high) + mm(pair[1], high) + mm(pair[0], low)


def times_t(pair, values):
    high, low = split_in(values)
    return mm_t(pair[0], high) + mm_t(pair[1], high) + mm_t(pair[0], low)


def gelu_pair(v):
    square = v * v
    tanh = jnp.tanh(GELU_A * v * (1.0 + GELU_B * square))
    half = 0.5 * (1.0 + tanh)
    slope = half + 0.5 * v * (1.0 - tanh * tanh) * (GELU_A * (1.0 + 3.0 * GELU_B * square))
    return v * half, slope


def put_rows(ref, value, r, padded):
    ref[r * padded : r * padded + value.shape[0], :] = value


def column_sum(values):
    return jnp.sum(values, axis=0, keepdims=True)


def norm_one_kernel(columns, padded, groups, all_ref, gain, bias, high, low, freq, base, xh, inverse, pad, tables, sems):
    mp, rows_dev = all_ref.shape[0], all_ref.shape[1]
    width = mp * all_ref.shape[3]
    first = lax.axis_index("lat") * rows_dev
    choice = jnp.int32(0)
    for r in range(rows_dev):
        choice = choice + jnp.where(groups[first + r] == 0, 1 << r, 0).astype(jnp.int32)
    copies = [
        pltpu.make_async_copy(src.at[choice], tables.at[i], sems.at[i])
        for i, src in enumerate((high, low))
    ]
    for copy in copies:
        copy.start()
    pad[...] = jnp.zeros_like(pad)
    for r in range(rows_dev):
        for m in range(mp):
            pad[m, r * padded : r * padded + columns, :] = all_ref[m, r].astype(F32)
    total = sum(jnp.sum(pad[m], axis=1, keepdims=True) for m in range(mp))
    average = total / width
    spread = sum(
        jnp.sum((pad[m] - average) * (pad[m] - average), axis=1, keepdims=True) for m in range(mp)
    )
    inv = lax.rsqrt(spread / width + EPSILON)
    x = pad[lax.axis_index("mp")]
    hat = (x - average) * inv
    u = hat * gain[...] + bias[...]
    base[...] = x + u
    xh[...] = hat
    inverse[...] = inv
    for copy in copies:
        copy.wait()
    freq[...] = times((tables[0], tables[1]), u)


def latitude_kernel(share, tables, left, right, same, keep, high_out, low_out):
    high, low = split_in(tables[...])
    for values, out in ((high, high_out), (low, low_out)):
        spread = mm(left[...], values).astype(BF)
        n = left.shape[0]
        for i in range(4):
            block = mm(spread, right[i]) * same[...].astype(F32)
            if i % 2:
                block = block * keep[...]
            out[i * n : (i + 1) * n, :] = block.astype(BF)


def block_mask(blocks, size):
    shape = (blocks * size, blocks * size)
    row = lax.broadcasted_iota(jnp.int32, shape, 0)
    col = lax.broadcasted_iota(jnp.int32, shape, 1)
    inside = None
    for n in range(blocks):
        one = (row >= n * size) & (row < (n + 1) * size) & (col >= n * size) & (col < (n + 1) * size)
        inside = one if inside is None else inside | one
    return inside


def diagonal(packed, blocks, size):
    whole = jnp.concatenate([packed.astype(F32)] * blocks, axis=0)
    return jnp.where(block_mask(blocks, size), whole, 0.0).astype(BF)


def gather_blocks(full, blocks, size):
    col = lax.broadcasted_iota(jnp.int32, (size, blocks * size), 1)
    out = None
    for n in range(blocks):
        piece = full[n * size : (n + 1) * size, :]
        piece = jnp.where((col >= n * size) & (col < (n + 1) * size), piece, 0.0)
        out = piece if out is None else out + piece
    return out


def filter_kernel(blocks, size, z, high, low, weights, biases, eo, s_out, h_out, slope_out, gate_out):
    w1r, w1i, w2r, w2i = (diagonal(weights[i], blocks, size) for i in range(4))
    n = z.shape[0]
    s = times((high[...], low[...]), z[...]).astype(BF)
    s_out[...] = s
    sr, si = s[:n], s[n:]
    a1r = mm(sr, w1r) - mm(si, w1i) + biases[0:1, :]
    a1i = mm(sr, w1i) + mm(si, w1r) + biases[1:2, :]
    hr, slope = gelu_pair(a1r)
    hr = hr.astype(BF)
    slope_out[:n, :] = slope
    hi, slope = gelu_pair(a1i)
    hi = hi.astype(BF)
    slope_out[n:, :] = slope
    h_out[:n, :] = hr
    h_out[n:, :] = hi
    a2r = mm(hr, w2r) - mm(hi, w2i) + biases[2:3, :]
    a2i = mm(hr, w2i) + mm(hi, w2r) + biases[3:4, :]
    tr = jnp.tanh(a2r * (1.0 / SHRINK))
    ti = jnp.tanh(a2i * (1.0 / SHRINK))
    gate_out[:n, :] = tr * tr
    gate_out[n:, :] = ti * ti
    rh, rl = split_in(a2r - SHRINK * tr)
    ih, il = split_in(a2i - SHRINK * ti)
    out = mm_t(high[:n, :], rh) + mm_t(low[:n, :], rh) + mm_t(high[:n, :], rl)
    out += mm_t(high[n:, :], ih) + mm_t(low[n:, :], ih) + mm_t(high[n:, :], il)
    eo[...] = out.astype(BF)


def mix_kernel(choice, eo, high, low, base, x1):
    got = eo[...]
    x1[...] = base[...] + mm_t(high[0], got) + mm_t(low[0], got)


def second_norm(parts_of):
    width = len(parts_of) * parts_of[0].shape[1]
    total = sum(jnp.sum(v, axis=1, keepdims=True) for v in parts_of)
    average = total / width
    spread = sum(jnp.sum((v - average) * (v - average), axis=1, keepdims=True) for v in parts_of)
    return average, lax.rsqrt(spread / width + EPSILON)


def mlp_kernel(columns, padded, orders, *refs):
    mp, pieces = refs[0].shape[0], len(orders)
    dy_all, norms, places, w1, b1, w2, own = refs[:7]
    others = refs[7 : 6 + mp]
    send = refs[6 + mp]
    grads = refs[7 + mp : 7 + mp + 2 * pieces]
    gb1, n_s, nt_s, dy_s, dyt_s, x1_s, out_acc, dn_acc, pad = refs[7 + mp + 2 * pieces :]
    step, steps = pl.program_id(0), pl.num_programs(0)
    ch, width = own.shape[1], w1.shape[0]
    rows_dev = dy_all.shape[1]

    @pl.when(step == 0)
    def _():
        mine = lax.axis_index("mp")
        x1_s[mine] = own[...]
        for i, other in enumerate(others):
            x1_s[lax.rem(mine + 1 + i, mp)] = other[...]
        average, inv = second_norm([x1_s[m] for m in range(mp)])
        for m in range(mp):
            lanes = slice(m * ch, (m + 1) * ch)
            hat = (x1_s[m] - average) * inv
            n_s[:, lanes] = (hat * norms[m, 0:1, :] + norms[m, 1:2, :]).astype(BF)
            pad[...] = jnp.zeros_like(pad)
            for r in range(rows_dev):
                pad[r * padded : r * padded + columns, :] = dy_all[m, r].astype(F32)
            dy_s[:, lanes] = pad[...].astype(BF)
        me = lax.axis_index("lat")
        lane = lax.broadcasted_iota(jnp.int32, (width, width), 1)
        share = width // lax.axis_size("lat")
        target = (places[:, 0:1] ^ me) * share + places[:, 1:2]
        move = jnp.where(lane == target, 1.0, 0.0).astype(BF)
        nt_s[...] = mm_nt(move, n_s[...]).astype(BF)
        dyt_s[...] = mm_nt(move, dy_s[...]).astype(BF)
        out_acc[...] = jnp.zeros_like(out_acc)
        dn_acc[...] = jnp.zeros_like(dn_acc)

    p = mm(n_s[...], w1[...]) + b1[...]
    q, slope = gelu_pair(p)
    q = q.astype(BF)
    dp = (mm_nt(dy_s[...], w2[...]) * slope).astype(BF)
    dn_acc[...] += mm_nt(dp, w1[...])
    out_acc[...] += mm(q, w2[...])
    gb1[...] = column_sum(dp.astype(F32))
    both = (mm(nt_s[...], dp), mm(dyt_s[...], q))
    for piece, bits in enumerate(orders):
        kept, away = grads[2 * piece : 2 * piece + 2]
        count = len(bits)
        rows = width >> count

        @pl.when((step * pieces) // steps == piece)
        def _():
            for i, grad in enumerate(both):
                for spot in range(2**count):
                    who = sum(((spot >> (count - 1 - b)) & 1) * bit for b, bit in enumerate(bits))
                    block = grad[who * rows : (who + 1) * rows, :].astype(BF)
                    at = (spot % 2 ** (count - 1)) * rows
                    (away if spot >> (count - 1) else kept)[i, at : at + rows, :] = block

    @pl.when(step == steps - 1)
    def _():
        halves = [x1_s[m] for m in range(mp)]
        average, inv = second_norm(halves)
        plain, cross = 0.0, 0.0
        for m in range(mp):
            lanes = slice(m * ch, (m + 1) * ch)
            part = dn_acc[:, lanes]
            scaled = part * norms[m, 0:1, :]
            plain += jnp.sum(scaled, axis=1, keepdims=True)
            cross += jnp.sum(scaled * ((halves[m] - average) * inv), axis=1, keepdims=True)
            send[m, :, :ch] = out_acc[:, lanes].astype(BF)
            send[m, :, ch : 2 * ch] = part.astype(BF)
        spot = lax.broadcasted_iota(jnp.int32, (plain.shape[0], 128), 1)
        stat = jnp.zeros(spot.shape, BF)
        for first, value in ((0, plain), (3, cross)):
            for i in range(3):
                term = value.astype(BF)
                value = value - term.astype(F32)
                stat = jnp.where(spot == first + i, term.astype(F32), stat.astype(F32)).astype(BF)
        for m in range(mp):
            send[m, :, 2 * ch :] = stat


def back_mix_kernel(columns, padded, choice, got, dy, gain, bias2, high, low, own, *refs):
    mp, ch = got.shape[0], own.shape[1]
    others = refs[: mp - 1]
    out_field, dx1, freq, sums, pad = refs[mp - 1 :]
    rows_dev = dy.shape[0]
    width = mp * ch
    x1 = own[...]
    average, inv = second_norm([x1] + [other[...] for other in others])
    hat = (x1 - average) * inv
    total = sum(got[m].astype(F32) for m in range(mp))
    out = x1 + total[:, :ch] + bias2[...]
    dn = total[:, ch : 2 * ch]
    pad[...] = jnp.zeros_like(pad)
    for r in range(rows_dev):
        out_field[r] = out[r * padded : r * padded + columns, :].astype(BF)
        put_rows(pad, dy[r].astype(F32), r, padded)
    grad = pad[...]
    sums[0:1, :] = column_sum(dn * hat)
    sums[1:2, :] = column_sum(dn)
    sums[2:3, :] = column_sum(grad)
    sums[3:8, :] = jnp.zeros((5, ch), F32)
    stats = total[:, 2 * ch : 2 * ch + 128]
    plain = (stats[:, 0:1] + stats[:, 1:2] + stats[:, 2:3]) / width
    cross = (stats[:, 3:4] + stats[:, 4:5] + stats[:, 5:6]) / width
    grad = grad + inv * (dn * gain[...] - plain - hat * cross)
    dx1[...] = grad
    freq[...] = times((high[0], low[0]), grad).astype(BF)


def filter_back_kernel(blocks, size, group, dz, high, low, weights, s_ref, h_ref, slope_ref, gate_ref, mlp_sums, hidden_sums, send, rows, grads_s, sums_s):
    w1r, w1i, w2r, w2i = (diagonal(weights[i], blocks, size) for i in range(4))
    n = dz.shape[0]
    dsh = mm(high[...], dz[...]) + mm(low[...], dz[...])
    da = dsh * gate_ref[...]
    dar, dai = da[:n].astype(BF), da[n:].astype(BF)
    hr, hi = h_ref[:n, :], h_ref[n:, :]
    dcr = ((mm_nt(dar, w2r) + mm_nt(dai, w2i)) * slope_ref[:n, :]).astype(BF)
    dci = ((mm_nt(dai, w2r) - mm_nt(dar, w2i)) * slope_ref[n:, :]).astype(BF)
    rh, rl = split_in(mm_nt(dcr, w1r) + mm_nt(dci, w1i))
    ih, il = split_in(mm_nt(dci, w1r) - mm_nt(dcr, w1i))
    out = mm_t(high[:n, :], rh) + mm_t(low[:n, :], rh) + mm_t(high[:n, :], rl)
    out += mm_t(high[n:, :], ih) + mm_t(low[n:, :], ih) + mm_t(high[n:, :], il)
    parts = rows.shape[0]
    for d in range(parts):
        rows[d, :group, :] = out[d * group : (d + 1) * group, :]
    sr, si = s_ref[:n, :], s_ref[n:, :]
    grads = (
        mm_t(sr, dcr) + mm_t(si, dci),
        mm_t(sr, dci) - mm_t(si, dcr),
        mm_t(hr, dar) + mm_t(hi, dai),
        mm_t(hr, dai) - mm_t(hi, dar),
    )
    for i, grad in enumerate(grads):
        grads_s[i * size : (i + 1) * size, :] = gather_blocks(grad, blocks, size)
    sums_s[...] = jnp.zeros_like(sums_s)
    for i, grad in enumerate((dcr, dci, dar, dai)):
        sums_s[i : i + 1, :] = column_sum(grad.astype(F32))
    sums_s[4:7, :] = mlp_sums[0:3, :]
    sums_s[7 : 7 + hidden_sums.shape[0], :] = hidden_sums[...]
    share = grads_s.shape[0] // parts
    at = group + share
    for d in range(parts):
        rows[d, group:at, :] = grads_s[d * share : (d + 1) * share, :]
        row = sums_s[d : d + 1, :]
        first = row.astype(BF).astype(F32)
        rows[d, at : at + 1, :] = first
        rows[d, at + 1 : at + 2, :] = row - first
        if at + 2 < rows.shape[1]:
            rows[d, at + 2 :, :] = jnp.zeros((rows.shape[1] - at - 2, rows.shape[2]), F32)
    send[...] = rows[...].astype(BF)


def back_norm_kernel(group, share, choice, got, high, low, dx1, xh, gain, du_out, stat, tail, tail_s):
    parts, _, ch = got.shape
    every = got[...].astype(F32)
    deo = every[:, :group, :].reshape(parts * group, ch).astype(BF)
    at = group + share
    tail_s[...] = jnp.zeros_like(tail_s)
    tail_s[:share, :] = jnp.sum(every[:, group:at, :], axis=0)
    total = jnp.sum(every[:, at : at + 1, :], axis=0) + jnp.sum(every[:, at + 1 : at + 2, :], axis=0)
    du = dx1[...] + mm_t(high[0], deo) + mm_t(low[0], deo)
    du_out[...] = du
    hat = xh[...]
    scaled = du * gain[...]
    spot = lax.broadcasted_iota(jnp.int32, stat.shape, 1)
    stat[...] = jnp.where(
        spot == 0,
        jnp.sum(scaled, axis=1, keepdims=True),
        jnp.sum(scaled * hat, axis=1, keepdims=True),
    )
    for i, row in enumerate((total, column_sum(du * hat), column_sum(du))):
        first = row.astype(BF).astype(F32)
        tail_s[share + 2 * i : share + 2 * i + 1, :] = first
        tail_s[share + 2 * i + 1 : share + 2 * i + 2, :] = row - first
    whole_tail = tail_s[...].astype(BF)
    for d in range(parts):
        tail[d] = whole_tail


def last_kernel(columns, padded, width, du, dx1, xh, inverse, gain, stats, out):
    plain = stats[:, 0:1] / width
    cross = stats[:, 1:2] / width
    value = dx1[...] + inverse[...] * (du[...] * gain[...] - plain - xh[...] * cross)
    for r in range(out.shape[0]):
        out[r] = value[r * padded : r * padded + columns, :]


def whole(shape, extra=0):
    return pl.BlockSpec(shape, lambda *_: (0,) * len(shape))


def run(kernel, outs, args, scratch=(), picked=(), choice=None, flops=0, limit=56):
    moved = sum(math.prod(a.shape) * a.dtype.itemsize for a in args)
    moved += sum(math.prod(o.shape) * o.dtype.itemsize for o in outs)
    params = pltpu.CompilerParams(vmem_limit_bytes=limit * 2**20)
    cost = pl.CostEstimate(flops=flops, bytes_accessed=moved, transcendentals=0)
    out_shape = [jax.ShapeDtypeStruct(o.shape, o.dtype) for o in outs]
    if choice is None:
        return pl.pallas_call(
            kernel,
            out_shape=out_shape,
            in_specs=[pl.BlockSpec(memory_space=pltpu.VMEM)] * len(args),
            out_specs=[pl.BlockSpec(memory_space=pltpu.VMEM)] * len(outs),
            scratch_shapes=list(scratch),
            compiler_params=params,
            cost_estimate=cost,
        )(*args)
    specs = [
        pl.BlockSpec((1, *a.shape[1:]), lambda i, c: (c[0], 0, 0)) if i in picked else whole(a.shape)
        for i, a in enumerate(args)
    ]
    return pl.pallas_call(
        kernel,
        out_shape=out_shape,
        grid_spec=pltpu.PrefetchScalarGridSpec(
            num_scalar_prefetch=1,
            grid=(1,),
            in_specs=specs,
            out_specs=[whole(o.shape) for o in outs],
            scratch_shapes=list(scratch),
        ),
        compiler_params=params,
        cost_estimate=cost,
    )(choice, *args)


def halve(kept, away, bit, parts):
    got = lax.ppermute(away, "lat", [(d, d ^ bit) for d in range(parts)])
    half = kept.shape[1] // 2
    away = (kept[:, half:].astype(F32) + got[:, half:].astype(F32)).astype(BF)
    kept = kept[:, :half].astype(F32) + got[:, :half].astype(F32)
    return kept, away


def after(value, arrays):
    return lax.optimization_barrier((value, arrays))


def body(
    field,
    row_group,
    row_valid,
    norm1_gain,
    norm1_bias,
    spec_w1,
    spec_b1,
    spec_w2,
    spec_b2,
    norm2_gain,
    norm2_bias,
    fc1_weight,
    fc1_bias,
    fc2_weight,
    fc2_bias,
    cotangent,
):
    rows_dev, columns, ch = field.shape
    parts, mp = lax.axis_size("lat"), lax.axis_size("mp")
    me = lax.axis_index("lat")
    rows = rows_dev * parts
    full_width = ch * mp
    padded = -(-columns // 16) * 16
    tokens = rows_dev * padded
    blocks, size = spec_w1.shape[1], spec_w1.shape[2]
    hidden = fc1_weight.shape[1]
    share = -(-HALVES // parts)
    group = 2 * rows_dev * share
    patches = parts * group

    def f32(*shape):
        return jax.ShapeDtypeStruct(shape, F32)

    def bf(*shape):
        return jax.ShapeDtypeStruct(shape, BF)

    lon = [jnp.asarray(t) for t in longitude_tables(parts, share, rows_dev, columns, padded)]
    local_group = lax.dynamic_slice_in_dim(row_group, me * rows_dev, rows_dev)
    choice = sum(
        jnp.where(local_group[r] == 0, 1 << r, 0) for r in range(rows_dev)
    ).astype(jnp.int32).reshape(1)
    gain1, bias1 = norm1_gain.reshape(1, ch), norm1_bias.reshape(1, ch)

    field_all = lax.all_gather(field, "mp", axis=0)
    table = pltpu.VMEM((2, patches, tokens), BF)
    freq, base, xh1, inv1 = pl.pallas_call(
        functools.partial(norm_one_kernel, columns, padded),
        out_shape=[f32(patches, ch), f32(tokens, ch), f32(tokens, ch), f32(tokens, 1)],
        in_specs=[pl.BlockSpec(memory_space=pltpu.SMEM)]
        + [pl.BlockSpec(memory_space=pltpu.VMEM)] * 3
        + [pl.BlockSpec(memory_space=pl.ANY)] * 2,
        out_specs=[pl.BlockSpec(memory_space=pltpu.VMEM)] * 4,
        scratch_shapes=[
            pltpu.VMEM((mp, tokens, ch), F32),
            table,
            pltpu.SemaphoreType.DMA((2,)),
        ],
        compiler_params=pltpu.CompilerParams(vmem_limit_bytes=56 * 2**20),
    )(row_group, field_all, gain1, bias1, *lon)

    def to_other(values, rows_each):
        return lax.all_to_all(values.reshape(parts, rows_each, ch), "lat", 0, 0, tiled=True)

    z = to_other(freq, group).reshape(patches, ch)

    cos_mat, sin_mat = latitude_tables(row_group, row_valid)
    width = jnp.where(row_group == 0, LON_FINE, LON_COARSE).astype(jnp.int32)
    here = me * share + jnp.arange(share, dtype=jnp.int32)
    lone = (here[None, :] == 0) | (2 * here[None, :] == width[:, None])
    keep = (1.0 - lone.astype(F32)).reshape(rows * share, 1)
    lat = run(
        functools.partial(latitude_kernel, share),
        [bf(2 * patches, patches)] * 2,
        [
            jnp.concatenate([cos_mat, sin_mat], axis=1),
            *(jnp.asarray(t) for t in latitude_spread(rows, share)),
            keep,
        ],
    )
    spec = jnp.stack([spec_w1, spec_w2]).transpose(0, 1, 3, 2, 4).reshape(4, size, ch)
    spec_bias = jnp.concatenate([spec_b1.reshape(2, ch), spec_b2.reshape(2, ch)], axis=0)
    norms = lax.all_gather(jnp.stack([norm2_gain, norm2_bias]), "mp", axis=0)
    dy_all = lax.all_gather(cotangent, "mp", axis=0)
    z, norms, dy_all = lax.optimization_barrier((z, norms, dy_all))

    eo, s, h, slope, gate = run(
        functools.partial(filter_kernel, blocks, size),
        [bf(patches, ch), bf(2 * patches, ch), bf(2 * patches, ch), f32(2 * patches, ch), f32(2 * patches, ch)],
        [z, *lat, spec, spec_bias],
    )
    eo = to_other(eo, group).reshape(patches, ch)
    (x1,) = run(mix_kernel, [f32(tokens, ch)], [eo, *lon, base], (), (1, 2), choice)

    others = [
        lax.ppermute(x1, "mp", [((d + i) % mp, d) for d in range(mp)]) for i in range(1, mp)
    ]
    chunk = 256
    steps = hidden // chunk
    bits = [1 << b for b in range(parts.bit_length() - 1)]
    orders = [bits[i:3] + bits[:i] + bits[3:] for i in range(3)]
    pieces = len(orders)
    each = steps // pieces
    grad_specs = [
        pl.BlockSpec(
            (2, full_width // 2, chunk),
            functools.partial(lambda p, i: (0, 0, jnp.clip(i - p * each, 0, each - 1)), p),
        )
        for p in range(pieces)
        for _ in range(2)
    ]
    share_rows = full_width // parts
    places = np.stack(
        [np.arange(full_width) // share_rows, np.arange(full_width) % share_rows], axis=1
    ).astype(np.int32)
    send, *grads, g_fc1_bias = pl.pallas_call(
        functools.partial(mlp_kernel, columns, padded, orders),
        out_shape=[
            bf(mp, tokens, 2 * ch + 128),
            *[bf(2, full_width // 2, hidden // pieces)] * (2 * pieces),
            f32(1, hidden),
        ],
        grid=(steps,),
        in_specs=[
            whole(dy_all.shape),
            whole(norms.shape),
            whole((full_width, 2)),
            pl.BlockSpec((full_width, chunk), lambda i: (0, i)),
            pl.BlockSpec((1, chunk), lambda i: (0, i)),
            pl.BlockSpec((chunk, full_width), lambda i: (i, 0)),
            *[whole((tokens, ch))] * mp,
        ],
        out_specs=[
            whole((mp, tokens, 2 * ch + 128)),
            *grad_specs,
            pl.BlockSpec((1, chunk), lambda i: (0, i)),
        ],
        scratch_shapes=[
            pltpu.VMEM((tokens, full_width), BF),
            pltpu.VMEM((full_width, tokens), BF),
            pltpu.VMEM((tokens, full_width), BF),
            pltpu.VMEM((full_width, tokens), BF),
            pltpu.VMEM((mp, tokens, ch), F32),
            pltpu.VMEM((tokens, full_width), F32),
            pltpu.VMEM((tokens, full_width), F32),
            pltpu.VMEM((tokens, ch), F32),
        ],
        compiler_params=pltpu.CompilerParams(vmem_limit_bytes=56 * 2**20),
        cost_estimate=pl.CostEstimate(
            flops=12 * tokens * full_width * hidden, bytes_accessed=16 * 2**20, transcendentals=0
        ),
    )(
        dy_all,
        norms,
        jnp.asarray(places),
        fc1_weight,
        fc1_bias.reshape(1, hidden),
        fc2_weight,
        x1,
        *others,
    )
    got = lax.all_to_all(send, "mp", 0, 0, tiled=True)
    def exchange(states, turn):
        return [halve(*state, order[turn], parts) for state, order in zip(states, orders)]

    sums = exchange([grads[2 * p : 2 * p + 2] for p in range(pieces)], 0)

    out_field, dx1, dfreq, sums2 = run(
        functools.partial(back_mix_kernel, columns, padded),
        [bf(rows_dev, columns, ch), f32(tokens, ch), bf(patches, ch), f32(8, ch)],
        [got, cotangent, norm2_gain.reshape(1, ch), fc2_bias.reshape(1, ch), *lon, x1, *others],
        [pltpu.VMEM((tokens, ch), F32)],
        (4, 5),
        choice,
    )

    dz = to_other(dfreq, group).reshape(patches, ch)
    dz, sums = after(dz, sums)
    sums = exchange(sums, 1)
    spec_rows = 4 * size // parts
    send_rows = -(-(group + spec_rows + 2) // 8) * 8
    (sent,) = run(
        functools.partial(filter_back_kernel, blocks, size, group),
        [bf(parts, send_rows, ch)],
        [dz, *lat, spec, s, h, slope, gate, sums2, g_fc1_bias.reshape(-1, ch)],
        [
            pltpu.VMEM((parts, send_rows, ch), F32),
            pltpu.VMEM((4 * size, ch), F32),
            pltpu.VMEM((max(parts, 16), ch), F32),
        ],
    )
    sent, sums = after(sent, sums)
    sums = exchange(sums, 2)
    sent = lax.all_to_all(sent, "lat", 0, 0, tiled=True)
    sent, sums = after(sent, sums)
    kept, away = (jnp.concatenate([state[i] for state in sums], axis=2) for i in range(2))
    for bit in bits[3:-1]:
        kept, away = halve(kept, away, bit, parts)
    got_last = lax.ppermute(away, "lat", [(d, d ^ bits[-1]) for d in range(parts)])
    tail_rows = -(-(spec_rows + 6) // 16) * 16
    du, stat1, tail = run(
        functools.partial(back_norm_kernel, group, spec_rows),
        [f32(tokens, ch), f32(tokens, 2), bf(parts, tail_rows, ch)],
        [sent, *lon, dx1, xh1, gain1],
        [pltpu.VMEM((tail_rows, ch), F32)],
        (1, 2),
        choice,
    )
    stat1 = lax.psum(stat1, "mp")
    stat1, got_last = after(stat1, got_last)
    weights = kept + got_last.astype(F32)
    (grad_field,) = run(
        functools.partial(last_kernel, columns, padded, full_width),
        [f32(rows_dev, columns, ch)],
        [du, dx1, xh1, inv1, gain1, stat1],
    )

    tail = lax.all_to_all(tail, "lat", 0, 0, tiled=True).astype(F32)
    g_spec = tail[:, :spec_rows].reshape(2, 2, size, blocks, size).transpose(0, 1, 3, 2, 4)
    pairs = tail[:, spec_rows : spec_rows + 6].reshape(parts, 3, 2, ch).sum(axis=2)
    small = pairs[:, 0]
    norm1 = pairs[:, 1:].sum(axis=0)
    return (
        out_field,
        grad_field,
        norm1[0],
        norm1[1],
        g_spec[0],
        small[0:2].reshape(2, blocks, size),
        g_spec[1],
        small[2:4].reshape(2, blocks, size),
        small[4],
        small[5],
        weights[0],
        small[7 : 7 + hidden // ch].reshape(hidden),
        weights[1].T,
        small[6],
    )


def solution(mesh):
    placed = (
        P("lat", None, "mp"),
        P(),
        P(),
        P("mp"),
        P("mp"),
        P(None, "mp", None, None),
        P(None, "mp", None),
        P(None, "mp", None, None),
        P(None, "mp", None),
        P("mp"),
        P("mp"),
        P(None, "mp"),
        P("mp"),
        P("mp", None),
        P("mp"),
        P("lat", None, "mp"),
    )
    return jax.shard_map(
        body,
        mesh=mesh,
        in_specs=placed,
        out_specs=(
            P("lat", None, "mp"),
            P("lat", None, "mp"),
            P("mp"),
            P("mp"),
            P(None, "mp", None, None),
            P(None, "mp", None),
            P(None, "mp", None, None),
            P(None, "mp", None),
            P("mp"),
            P("mp"),
            P("lat", "mp"),
            P("mp"),
            P("mp", "lat"),
            P("mp"),
        ),
        check_vma=False,
    )
```

time: 323 us -> 174 us (0.54)
  the two profiles are of different devices: /device:TPU:14 before, /device:TPU:0 now
where the time goes in v2:
time: 174 us; the launch traced here: 173 us
  Pallas kernels  51.7 us (30%)
  starting transfers between devices  36.3 us (21%)
  waiting for transfers between devices  35.1 us (20%)
  local copies, waits for them, and re-layouts  19.4 us (11%)
  blocking collectives  18.7 us (11%)
  other arithmetic  9.03 us (5%)
  between operations  2.4 us (1%)
    pallas_call x4, Pallas kernels, run(): pl.pallas_call(kernel, out_shape=out_shape, in_specs=[pl.BlockSpec(memory...  20.5 us
    all_to_all x3, starting transfers between devices, to_other(): lax.all_to_all(values.reshape(parts, rows_each, ch), 'lat', 0, 0, tiled=T...  16.9 us
    pallas_call x1, Pallas kernels, body(): pl.pallas_call(functools.partial(mlp_kernel, columns, padded, orders), ou...  16.8 us
    all_to_all x3, waiting for transfers between devices, to_other(): lax.all_to_all(values.reshape(parts, rows_each, ch), 'lat', 0, 0, tiled=T...  16.5 us
    ppermute x9, waiting for transfers between devices, halve(): got = lax.ppermute(away, 'lat', [(d, d ^ bit) for d in range(parts)])  12.4 us
    pallas_call x3, Pallas kernels, run(): pl.pallas_call(kernel, out_shape=out_shape, grid_spec=pltpu.PrefetchScala...  10.6 us
    ppermute x9, starting transfers between devices, halve(): got = lax.ppermute(away, 'lat', [(d, d ^ bit) for d in range(parts)])  9.49 us
    unnamed x54, local copies, waits for them, and re-layouts  7.42 us
  transfers between devices with their start and end apart: 16, of which 9 were waited for; matrix products, arithmetic and copies ran while one was open for 10% of the time, Pallas kernels for 13%

profile of v2, /device:TPU:0, one launch (start us, length us, event | category | flops | bytes accessed | tf_op | source)
XLA Modules:
  0.0 172.7 jit_solution(1306992516508647731)
XLA Ops:
  0.7 1.3 reshape.194.gain
  1.9 1.0 copy.61
  2.9 2.4 %all-gather = bf16[4,180,384]{2,1,0:T(8,128)(2,1)} all-gather(bf16[2,180,384]{2,1,0:T(8,128)(2,1)S(1)} %copy.61), channel_id=2, replica_groups=mesh['lat'=16,'mp'=2] {'mp'}, dimensions={0}, use_global_device_ids=true | all-gather | bytes 829440 | tf_op jit(solution)/shard_map/all_gather | solution.py:538
  5.3 0.6 reshape.195.bias
  5.9 3.7 %shard_map.317 = (f32[384,384]{1,0:T(8,128)}, f32[384,384]{1,0:T(8,128)}, f32[384,384]{1,0:T(8,128)}, f32[384,1]{1,0:T(8,128)}) custom-call(s32[32]{0:T(128)} %groups.1, bf16[2,2,180,384]{3,2,1,0:T(8,128)(2,1)} %bitcast.36, f32[1,384]{1,0:T(1,128)} %reshape.194.gain, f32[1,384]{1,0:T(1,128)} %reshape.195.bias, bf16[4,384,384]{2,1,0:T(8,128)(2,1)} %constant.65.clone.high, ...), custom_call_target="tpu_custom_call" | custom-call | tf_op jit(solution)/shard_map/pallas_call | solution.py:540
  9.7 8.4 %all-to-all-start = ((f32[16,24,384]{2,1,0:T(8,128)}), f32[16,24,384]{2,1,0:T(8,128)S(1)}, u32[]{:S(2)}, u32[]{:S(2)}) async-start(f32[16,24,384]{2,1,0:T(8,128)} %bitcast.39), calls=%async_computation | async-start | bytes 1179648 | tf_op jit(solution)/shard_map/all_to_all | solution.py:556
  18.4 0.7 sub.23.keep
  19.6 1.0 reshape.199.weights
  21.3 0.7 pad_maximum_fusion.1.tables
  22.0 2.6 %shard_map.318 = (bf16[768,384]{1,0:T(8,128)(2,1)}, bf16[768,384]{1,0:T(8,128)(2,1)}) custom-call(f32[32,64]{1,0:T(8,128)} %pad_maximum_fusion.1.tables, bf16[192,32]{1,0:T(8,128)(2,1)} %constant.67.clone.left, bf16[4,64,384]{2,1,0:T(8,128)(2,1)} %constant.68.clone.right, bf16[192,384]{1,0:T(8,128)(2,1)} %constant.69.clone.same, f32[192,1]{1,0:T(8,128)} %sub.23.keep), custom_call_target="tpu_custom_call" | custom-call | bytes 1544960 | tf_op jit(solution)/shard_map/pallas_call | solution.py:454
  24.7 1.9 %all-gather.3.refs_1_ = f32[2,2,384]{2,1,0:T(2,128)} all-gather(f32[1,2,384]{2,1,0:T(2,128)S(1)} %maximum_bitcast_fusion.1), channel_id=3, replica_groups=mesh['lat'=16,'mp'=2] {'mp'}, dimensions={0}, use_global_device_ids=true | all-gather | bytes 9216 | tf_op jit(solution)/shard_map/all_gather | solution.py:576
  26.6 0.6 pad_maximum_fusion.2.biases
  27.2 2.3 %all-gather.2 = bf16[4,180,384]{2,1,0:T(8,128)(2,1)} all-gather(bf16[2,180,384]{2,1,0:T(8,128)(2,1)S(1)} %copy.62.dy), channel_id=4, replica_groups=mesh['lat'=16,'mp'=2] {'mp'}, dimensions={0}, use_global_device_ids=true | all-gather | bytes 829440 | tf_op jit(solution)/shard_map/all_gather | solution.py:577
  29.5 5.1 %all-to-all-done = f32[16,24,384]{2,1,0:T(8,128)S(1)} async-done(((f32[16,24,384]{2,1,0:T(8,128)}), f32[16,24,384]{2,1,0:T(8,128)S(1)}, u32[]{:S(2)}, u32[]{:S(2)}) %all-to-all-start) | async-done | bytes 589856 | tf_op jit(solution)/shard_map/all_to_all | solution.py:556
  34.6 0.8 copy-done.2
  35.4 6.7 %shard_map.319 = (bf16[384,384]{1,0:T(8,128)(2,1)}, bf16[768,384]{1,0:T(8,128)(2,1)}, bf16[768,384]{1,0:T(8,128)(2,1)}, f32[768,384]{1,0:T(8,128)}, f32[768,384]{1,0:T(8,128)}) custom-call(f32[384,384]{1,0:T(8,128)} %bitcast.35, bf16[768,384]{1,0:T(8,128)(2,1)} %get-tuple-element.70.high, bf16[768,384]{1,0:T(8,128)(2,1)} %get-tuple-element.71.low, ...), custom_call_target="tpu_custom_call" | custom-call | bytes 5904384 | tf_op jit(solution)/shard_map/pallas_call | solution.py:454
  42.1 4.2 %all-to-all-start.1 = ((bf16[16,24,384]{2,1,0:T(8,128)(2,1)}), bf16[16,24,384]{2,1,0:T(8,128)(2,1)S(1)}, u32[]{:S(2)}, u32[]{:S(2)}) async-start(bf16[16,24,384]{2,1,0:T(8,128)(2,1)} %bitcast.42), calls=%async_computation.1 | async-start | bytes 589824 | tf_op jit(solution)/shard_map/all_to_all | solution.py:556
  46.4 0.6 fusion.13
  48.3 7.9 %all-to-all-done.1 = bf16[16,24,384]{2,1,0:T(8,128)(2,1)S(1)} async-done(((bf16[16,24,384]{2,1,0:T(8,128)(2,1)}), bf16[16,24,384]{2,1,0:T(8,128)(2,1)S(1)}, u32[]{:S(2)}, u32[]{:S(2)}) %all-to-all-start.1) | async-done | bytes 294944 | tf_op jit(solution)/shard_map/all_to_all | solution.py:556
  56.2 0.7 copy-done.4
  56.9 2.7 %shard_map.320.refs_6_.own = f32[384,384]{1,0:T(8,128)} custom-call(s32[1]{0:T(128)S(6)} %add.90.choice, bf16[384,384]{1,0:T(8,128)(2,1)} %bitcast.38, bf16[4,384,384]{2,1,0:T(8,128)(2,1)} %constant.65.clone.high, bf16[4,384,384]{2,1,0:T(8,128)(2,1)} %constant.66.clone.low, f32[384,384]{1,0:T(8,128)} %get-tuple-element.73.base), custom_call_target="tpu_custom_call" | custom-call | bytes 3833856 | tf_op jit(solution)/shard_map/pallas_call | solution.py:467
  59.6 0.6 reshape.198.refs_4_
  60.2 1.6 collective-permute-done.refs_7_.refs_0_
  61.8 0.8 copy-done.9
  62.7 16.8 %shard_map.321 = (bf16[2,384,896]{2,1,0:T(8,128)(2,1)}, bf16[2,384,512]{2,1,0:T(8,128)(2,1)}, bf16[2,384,512]{2,1,0:T(8,128)(2,1)}, bf16[2,384,512]{2,1,0:T(8,12...) custom-call(bf16[2,2,180,384]{3,2,1,0:T(8,128)(2,1)} %bitcast.41, ...), custom_call_target="tpu_custom_call" | custom-call | flops 5435817984 | bytes 16777216 | tf_op jit(solution)/shard_map/pallas_call | solution.py:609
  79.5 1.0 collective-permute-start.3
  80.5 0.8 collective-permute-start.2
  81.9 0.6 reshape.204.bias2
  82.4 6.9 %all_to_all.30.got = bf16[2,384,896]{2,1,0:T(8,128)(2,1)} all-to-all(bf16[2,384,896]{2,1,0:T(8,128)(2,1)} %get-tuple-element.74), channel_id=1, replica_groups=mesh['lat'=16,'mp'=2] {'mp'}, dimensions={0} | all-to-all | bytes 2752512 | tf_op jit(solution)/shard_map/all_to_all | solution.py:655
  89.3 4.6 %shard_map.322 = (bf16[2,180,384]{2,1,0:T(8,128)(2,1)}, f32[384,384]{1,0:T(8,128)}, bf16[384,384]{1,0:T(8,128)(2,1)}, f32[8,384]{1,0:T(8,128)}) custom-call(s32[1]{0:T(128)S(6)} %add.90.choice, bf16[2,384,896]{2,1,0:T(8,128)(2,1)} %all_to_all.30.got, bf16[2,180,384]{2,1,0:T(8,128)(2,1)} %copy-done.1, f32[1,384]{1,0:T(1,128)} %copy-done.14, ...), custom_call_target="tpu_custom_call" | custom-call | bytes 6368256 | tf_op jit(solution)/shard_map/pallas_call | solution.py:467
  93.9 4.3 %all-to-all-start.3 = ((bf16[16,24,384]{2,1,0:T(8,128)(2,1)}), bf16[16,24,384]{2,1,0:T(8,128)(2,1)S(1)}, u32[]{:S(2)}, u32[]{:S(2)}) async-start(bf16[16,24,384]{2,1,0:T(8,128)(2,1)} %bitcast.43), calls=%async_computation.3 | async-start | bytes 589824 | tf_op jit(solution)/shard_map/all_to_all | solution.py:556
  98.1 1.2 collective-permute-done.3
  99.4 0.9 copy-done.8
  100.2 2.1 %add_convert_fusion = (bf16[2,192,512]{2,1,0:T(8,128)(2,1)}, f32[2,192,512]{2,1,0:T(8,128)S(1)}) fusion(bf16[2,384,512]{2,1,0:T(8,128)(2,1)} %copy-done.8, bf16[2,384,512]{2,1,0:T(8,128)(2,1)S(1)} %copy-done.7), kind=kLoop, calls=%fused_computation.1 | loop fusion | flops 1376256 | bytes 2752512 | tf_op jit(solution)/shard_map/convert_element_type | solution.py:485
  102.4 2.1 %add_convert_fusion.1 = (bf16[2,192,512]{2,1,0:T(8,128)(2,1)}, f32[2,192,512]{2,1,0:T(8,128)S(1)}) fusion(bf16[2,384,512]{2,1,0:T(8,128)(2,1)} %collective-permute-done.2, bf16[2,384,512]{2,1,0:T(8,128)(2,1)S(1)} %copy-done.6), kind=kLoop, calls=%fused_computation.3 | loop fusion | flops 1376256 | bytes 2752512 | tf_op jit(solution)/shard_map/convert_element_type | solution.py:485
  104.5 1.0 add_convert_fusion.2
  105.5 3.6 %all-to-all-done.3 = bf16[16,24,384]{2,1,0:T(8,128)(2,1)S(1)} async-done(((bf16[16,24,384]{2,1,0:T(8,128)(2,1)}), bf16[16,24,384]{2,1,0:T(8,128)(2,1)S(1)}, u32[]{:S(2)}, u32[]{:S(2)}) %all-to-all-start.3) | async-done | bytes 294944 | tf_op jit(solution)/shard_map/all_to_all | solution.py:556
  109.7 1.0 collective-permute-start.5
  110.7 0.6 reshape.207.hidden_sums
  111.3 0.8 collective-permute-start.4
  112.0 8.6 %shard_map.323 = bf16[16,56,384]{2,1,0:T(8,128)(2,1)} custom-call(bf16[384,384]{1,0:T(8,128)(2,1)} %bitcast.37, bf16[768,384]{1,0:T(8,128)(2,1)} %get-tuple-element.70.high, bf16[768,384]{1,0:T(8,128)(2,1)} %get-tuple-element.71.low, bf16[4,96,384]{2,1,0:T(8,128)(2,1)} %reshape.199.weights, bf16[768,384]{1,0:T(8,128)(2,1)} %get-tuple-element.84.s_ref, ...), custom_call_target="tpu_custom_call" | custom-call | bytes 6014976 | tf_op jit(solution)/shard_map/pallas_call | solution.py:454
  120.8 1.1 add_convert_fusion.4
  122.0 4.2 %all-to-all-start.4 = ((bf16[16,56,384]{2,1,0:T(8,128)(2,1)}), bf16[16,56,384]{2,1,0:T(8,128)(2,1)S(1)}, u32[]{:S(2)}, u32[]{:S(2)}) async-start(bf16[16,56,384]{2,1,0:T(8,128)(2,1)} %shard_map.323), calls=%async_computation.4 | async-start | bytes 1376256 | tf_op jit(solution)/shard_map/all_to_all | solution.py:687
  126.2 1.9 %collective-permute-start.9 = (bf16[2,96,512]{2,1,0:T(8,128)(2,1)S(1)}, bf16[2,96,512]{2,1,0:T(8,128)(2,1)S(1)}, u32[]{:S(2)}, u32[]{:S(2)}) collective-permute-start(bf16[2,96,512]{2,1,0:T(8,128)(2,1)S(1)} %get-tuple-element.102), channel_id=1, source_target_pairs={{0,4},{2,6},{4,0},{6,2},{8,12},{10,14},{12,8},{14,10},{16,20},{18,... | collective-permute-start | bytes 589832 | tf_op jit(solution)/shard_map/ppermute | solution.py:483
  128.2 1.5 collective-permute-start.8
  129.6 1.5 collective-permute-start.7
  131.1 5.3 %collective-permute-done.9 = bf16[2,96,512]{2,1,0:T(8,128)(2,1)S(1)} collective-permute-done((bf16[2,96,512]{2,1,0:T(8,128)(2,1)S(1)}, bf16[2,96,512]{2,1,0:T(8,128)(2,1)S(1)}, u32[]{:S(2)}, u32[]{:S(2)}) %collective-permute-start.9) | collective-permute-done | bytes 196640 | tf_op jit(solution)/shard_map/ppermute | solution.py:483
  136.6 5.9 %collective-permute-done.7 = bf16[2,96,512]{2,1,0:T(8,128)(2,1)S(1)} collective-permute-done((bf16[2,96,512]{2,1,0:T(8,128)(2,1)S(1)}, bf16[2,96,512]{2,1,0:T(8,128)(2,1)S(1)}, u32[]{:S(2)}, u32[]{:S(2)}) %collective-permute-start.7) | collective-permute-done | bytes 196640 | tf_op jit(solution)/shard_map/ppermute | solution.py:483
  142.5 0.8 all-to-all-done.4.got
  143.3 1.8 %collective-permute-start.10 = (bf16[2,48,1536]{2,1,0:T(8,128)(2,1)S(1)}, bf16[2,48,1536]{2,1,0:T(8,128)(2,1)S(1)}, u32[]{:S(2)}, u32[]{:S(2)}) collective-permute-start(bf16[2,48,1536]{2,1,0:T(8,128)(2,1)S(1)} %pad_maximum_fusion), channel_id=1, source_target_pairs={{0,16},{2,18},{4,20},{6,22},{8,24},{10,26},{12,28},{14,30},{16,0},... | collective-permute-start | bytes 884744 | tf_op jit(solution)/shard_map/ppermute | solution.py:692
  145.1 0.9 copy.69
  146.0 3.3 %shard_map.324 = (f32[384,384]{1,0:T(8,128)}, f32[384,2]{1,0:T(8,128)}, bf16[16,32,384]{2,1,0:T(8,128)(2,1)}) custom-call(s32[1]{0:T(128)S(6)} %add.90.choice, bf16[16,56,384]{2,1,0:T(8,128)(2,1)} %copy-done, bf16[4,384,384]{2,1,0:T(8,128)(2,1)} %constant.65.clone.high, bf16[4,384,384]{2,1,0:T(8,128)(2,1)} %constant.66.clone.low, ...), custom_call_target="tpu_custom_call" | custom-call | bytes 5214720 | tf_op jit(solution)/shard_map/pallas_call | solution.py:467
  149.3 4.0 %all-to-all-start.5 = ((bf16[16,32,384]{2,1,0:T(8,128)(2,1)}), bf16[16,32,384]{2,1,0:T(8,128)(2,1)S(1)}, u32[]{:S(2)}, u32[]{:S(2)}) async-start(bf16[16,32,384]{2,1,0:T(8,128)(2,1)} %get-tuple-element.113), calls=%async_computation.5 | async-start | bytes 786432 | tf_op jit(solution)/shard_map/all_to_all | solution.py:711
  153.3 5.2 %psum.7.stats = f32[384,2]{1,0:T(8,128)} all-reduce(f32[384,2]{1,0:T(8,128)} %get-tuple-element.108), channel_id=1, replica_groups=mesh['lat'=16,'mp'=2] {'mp'}, use_global_device_ids=true, to_apply=%region_4.5 | all-reduce | flops 768 | bytes 6144 | tf_op jit(solution)/shard_map/psum | solution.py:702
  158.5 3.8 %collective-permute-done.10 = bf16[2,48,1536]{2,1,0:T(8,128)(2,1)S(1)} collective-permute-done((bf16[2,48,1536]{2,1,0:T(8,128)(2,1)S(1)}, bf16[2,48,1536]{2,1,0:T(8,128)(2,1)S(1)}, u32[]{:S(2)}, u32[]{:S(2)}) %collective-permute-start.10) | collective-permute-done | bytes 294944 | tf_op jit(solution)/shard_map/ppermute | solution.py:692
  162.2 2.6 %shard_map.325 = f32[2,180,384]{2,1,0:T(8,128)} custom-call(f32[384,384]{1,0:T(8,128)} %get-tuple-element.106.du, f32[384,384]{1,0:T(8,128)} %get-tuple-element.104.dx1, f32[384,384]{1,0:T(8,128)} %get-tuple-element.105.xh, f32[384,1]{1,0:T(8,128)} %get-tuple-element.107.inverse, f32[1,384]{1,0:T(1,128)} %reshape.194.gain, f32[384,2]{1,0:T(8,128)} %psum.7.stats), custom_call_target="tpu_custom_call" | custom-call | bytes 2328576 | tf_op jit(solution)/shard_map/pallas_call | solution.py:454
  164.8 2.1 %copy.70 = f32[2,180,384]{2,0,1:T(2,128)} copy(f32[2,180,384]{2,1,0:T(8,128)} %shard_map.325) | data formatting | bytes 1105920
  167.0 0.8 slice_bitcast_fusion.2
  168.0 0.6 slice_reduce_fusion.1
  169.2 0.9 slice_bitcast_fusion
  170.1 0.6 reshape.212
  170.7 0.7 reshape.210
  171.4 0.7 reshape.211
  172.1 0.6 slice_reduce_fusion.4
  (94 shorter events, 3.8 us)
Async XLA Ops:
  0.6 4.7 %copy-start.21 = (f32[384]{0:T(512)S(1)}, f32[384]{0:T(512)}, u32[]{:S(2)}) copy-start(f32[384]{0:T(512)} %param.26) | copy-start | bytes 4612
  5.9 12.2 %copy-start.15 = (s32[32]{0:T(128)S(1)}, s32[32]{0:T(128)}, u32[]{:S(2)}) copy-start(s32[32]{0:T(128)} %groups.1) | copy-start | bytes 388
  5.9 12.2 %copy-start.20 = (s32[32]{0:T(128)S(1)}, s32[32]{0:T(128)}, u32[]{:S(2)}) copy-start(s32[32]{0:T(128)} %param.24) | copy-start | bytes 388
  9.6 9.5 %copy-start.11 = (bf16[2,180,384]{2,0,1:T(2,128)(2,1)S(1)}, bf16[2,180,384]{2,0,1:T(2,128)(2,1)}, u32[]{:S(2)}) copy-start(bf16[2,180,384]{2,0,1:T(2,128)(2,1)} %param.37) | copy-start | bytes 829444
  9.6 9.5 %copy-start.22 = (f32[384]{0:T(512)S(1)}, f32[384]{0:T(512)}, u32[]{:S(2)}) copy-start(f32[384]{0:T(512)} %param.31) | copy-start | bytes 4612
  9.7 9.6 %copy-start.23 = (f32[384]{0:T(512)S(1)}, f32[384]{0:T(512)}, u32[]{:S(2)}) copy-start(f32[384]{0:T(512)} %param.32) | copy-start | bytes 4612
  9.7 9.6 %copy-start.12 = (bf16[2,4,96,96]{3,2,1,0:T(8,128)(2,1)S(1)}, bf16[2,4,96,96]{3,2,1,0:T(8,128)(2,1)}, u32[]{:S(2)}) copy-start(bf16[2,4,96,96]{3,2,1,0:T(8,128)(2,1)} %param.29) | copy-start | bytes 442372
  9.7 9.6 %copy-start.13 = (bf16[2,4,96,96]{3,2,1,0:T(8,128)(2,1)S(1)}, bf16[2,4,96,96]{3,2,1,0:T(8,128)(2,1)}, u32[]{:S(2)}) copy-start(bf16[2,4,96,96]{3,2,1,0:T(8,128)(2,1)} %param.27) | copy-start | bytes 442372
  9.7 24.9 %all-to-all-start = ((f32[16,24,384]{2,1,0:T(8,128)}), f32[16,24,384]{2,1,0:T(8,128)S(1)}, u32[]{:S(2)}, u32[]{:S(2)}) async-start(f32[16,24,384]{2,1,0:T(8,128)} %bitcast.39), calls=%async_computation | async-start | bytes 1179648 | tf_op jit(solution)/shard_map/all_to_all | solution.py:556
  19.1 1.4 copy-start.18
  19.1 1.5 copy-start.19
  19.2 8.0 %copy-start.1 = (bf16[2,180,384]{2,1,0:T(8,128)(2,1)}, bf16[2,180,384]{2,1,0:T(8,128)(2,1)S(1)}, u32[]{:S(2)}) copy-start(bf16[2,180,384]{2,1,0:T(8,128)(2,1)S(1)} %copy.62.dy) | copy-start | bytes 829444
  19.2 5.4 %copy-start.14 = (f32[1,384]{1,0:T(1,128)}, f32[1,384]{1,0:T(1,128)S(1)}, u32[]{:S(2)}) copy-start(f32[1,384]{1,0:T(1,128)S(1)} %stack.18.gain) | copy-start | bytes 4612
  34.6 0.8 copy-start.2
  42.1 14.1 %all-to-all-start.1 = ((bf16[16,24,384]{2,1,0:T(8,128)(2,1)}), bf16[16,24,384]{2,1,0:T(8,128)(2,1)S(1)}, u32[]{:S(2)}, u32[]{:S(2)}) async-start(bf16[16,24,384]{2,1,0:T(8,128)(2,1)} %bitcast.42), calls=%async_computation.1 | async-start | bytes 589824 | tf_op jit(solution)/shard_map/all_to_all | solution.py:556
  56.2 0.7 copy-start.4
  56.9 2.7 %copy-start.16 = (f32[1536]{0:T(1024)S(1)}, f32[1536]{0:T(1024)}, u32[]{:S(2)}) copy-start(f32[1536]{0:T(1024)} %param.34) | copy-start | bytes 18436
  59.6 2.2 %collective-permute-start = (f32[384,384]{1,0:T(8,128)}, f32[384,384]{1,0:T(8,128)S(1)}, u32[]{:S(2)}, u32[]{:S(2)}) collective-permute-start(f32[384,384]{1,0:T(8,128)} %shard_map.320.refs_6_.own), channel_id=1, source_target_pairs={{1,0},{0,1},{3,2},{2,3},{5,4},{4,5},{7,6},{6,7},{9,8},{8,9},{11,10... | collective-permute-start | bytes 1769480 | tf_op jit(solution)/shard_map/ppermute | solution.py:589
  60.2 21.6 %copy-start.24 = (f32[384]{0:T(512)S(1)}, f32[384]{0:T(512)}, u32[]{:S(2)}) copy-start(f32[384]{0:T(512)} %param.36) | copy-start | bytes 4612
  61.8 0.8 copy-start.9
  79.5 19.9 %collective-permute-start.3 = (bf16[2,384,512]{2,1,0:T(8,128)(2,1)}, bf16[2,384,512]{2,1,0:T(8,128)(2,1)S(1)}, u32[]{:S(2)}, u32[]{:S(2)}) collective-permute-start(bf16[2,384,512]{2,1,0:T(8,128)(2,1)} %get-tuple-element.82), channel_id=1, source_target_pairs={{0,8},{2,10},{4,12},{6,14},{8,0},{10,2},{12,4},{14,6},{16,24},{18,... | collective-permute-start | bytes 2359304 | tf_op jit(solution)/shard_map/ppermute | solution.py:483
  80.5 21.8 %collective-permute-start.2 = (bf16[2,384,512]{2,1,0:T(8,128)(2,1)}, bf16[2,384,512]{2,1,0:T(8,128)(2,1)}, u32[]{:S(2)}, u32[]{:S(2)}) collective-permute-start(bf16[2,384,512]{2,1,0:T(8,128)(2,1)} %get-tuple-element.80), channel_id=1, source_target_pairs={{0,4},{2,6},{4,0},{6,2},{8,12},{10,14},{12,8},{14,10},{16,20},{18,... | collective-permute-start | bytes 2359304 | tf_op jit(solution)/shard_map/ppermute | solution.py:483
  81.3 23.2 %collective-permute-start.1 = (bf16[2,384,512]{2,1,0:T(8,128)(2,1)}, bf16[2,384,512]{2,1,0:T(8,128)(2,1)S(1)}, u32[]{:S(2)}, u32[]{:S(2)}) collective-permute-start(bf16[2,384,512]{2,1,0:T(8,128)(2,1)} %get-tuple-element.78), channel_id=1, source_target_pairs={{0,2},{2,0},{4,6},{6,4},{8,10},{10,8},{12,14},{14,12},{16,18},{18,... | collective-permute-start | bytes 2359304 | tf_op jit(solution)/shard_map/ppermute | solution.py:483
  89.3 11.0 %copy-start.7 = (bf16[2,384,512]{2,1,0:T(8,128)(2,1)S(1)}, bf16[2,384,512]{2,1,0:T(8,128)(2,1)}, u32[]{:S(2)}) copy-start(bf16[2,384,512]{2,1,0:T(8,128)(2,1)} %get-tuple-element.81) | copy-start | bytes 2359300
  93.9 15.2 %all-to-all-start.3 = ((bf16[16,24,384]{2,1,0:T(8,128)(2,1)}), bf16[16,24,384]{2,1,0:T(8,128)(2,1)S(1)}, u32[]{:S(2)}, u32[]{:S(2)}) async-start(bf16[16,24,384]{2,1,0:T(8,128)(2,1)} %bitcast.43), calls=%async_computation.3 | async-start | bytes 589824 | tf_op jit(solution)/shard_map/all_to_all | solution.py:556
  99.4 0.9 copy-start.8
  100.2 2.1 %copy-start.6 = (bf16[2,384,512]{2,1,0:T(8,128)(2,1)S(1)}, bf16[2,384,512]{2,1,0:T(8,128)(2,1)}, u32[]{:S(2)}) copy-start(bf16[2,384,512]{2,1,0:T(8,128)(2,1)} %get-tuple-element.79) | copy-start | bytes 2359300
  102.4 2.2 %copy-start.5 = (bf16[2,384,512]{2,1,0:T(8,128)(2,1)S(1)}, bf16[2,384,512]{2,1,0:T(8,128)(2,1)}, u32[]{:S(2)}) copy-start(bf16[2,384,512]{2,1,0:T(8,128)(2,1)} %get-tuple-element.77) | copy-start | bytes 2359300
  104.5 6.1 %copy-start.17 = (f32[1,1536]{1,0:T(1,128)S(1)}, f32[1,1536]{1,0:T(1,128)}, u32[]{:S(2)}) copy-start(f32[1,1536]{1,0:T(1,128)} %get-tuple-element.89) | copy-start | bytes 18436
  109.1 2.9 %copy-start.3 = (bf16[16,24,384]{2,1,0:T(8,128)(2,1)}, bf16[16,24,384]{2,1,0:T(8,128)(2,1)S(1)}, u32[]{:S(2)}) copy-start(bf16[16,24,384]{2,1,0:T(8,128)(2,1)S(1)} %all-to-all-done.3) | copy-start | bytes 884740
  109.1 11.5 %collective-permute-start.6 = (bf16[2,192,512]{2,1,0:T(8,128)(2,1)}, bf16[2,192,512]{2,1,0:T(8,128)(2,1)S(1)}, u32[]{:S(2)}, u32[]{:S(2)}) collective-permute-start(bf16[2,192,512]{2,1,0:T(8,128)(2,1)} %get-tuple-element.95), channel_id=1, source_target_pairs={{0,2},{2,0},{4,6},{6,4},{8,10},{10,8},{12,14},{14,12},{16,18},{18,... | collective-permute-start | bytes 1179656 | tf_op jit(solution)/shard_map/ppermute | solution.py:483
  109.7 11.1 %collective-permute-start.5 = (bf16[2,192,512]{2,1,0:T(8,128)(2,1)}, bf16[2,192,512]{2,1,0:T(8,128)(2,1)}, u32[]{:S(2)}, u32[]{:S(2)}) collective-permute-start(bf16[2,192,512]{2,1,0:T(8,128)(2,1)} %get-tuple-element.93), channel_id=1, source_target_pairs={{0,8},{2,10},{4,12},{6,14},{8,0},{10,2},{12,4},{14,6},{16,24},{18,... | collective-permute-start | bytes 1179656 | tf_op jit(solution)/shard_map/ppermute | solution.py:483
  111.3 10.6 %collective-permute-start.4 = (bf16[2,192,512]{2,1,0:T(8,128)(2,1)}, bf16[2,192,512]{2,1,0:T(8,128)(2,1)S(1)}, u32[]{:S(2)}, u32[]{:S(2)}) collective-permute-start(bf16[2,192,512]{2,1,0:T(8,128)(2,1)} %get-tuple-element.91), channel_id=1, source_target_pairs={{0,4},{2,6},{4,0},{6,2},{8,12},{10,14},{12,8},{14,10},{16,20},{18,... | collective-permute-start | bytes 1179656 | tf_op jit(solution)/shard_map/ppermute | solution.py:483
  122.0 21.2 %all-to-all-start.4 = ((bf16[16,56,384]{2,1,0:T(8,128)(2,1)}), bf16[16,56,384]{2,1,0:T(8,128)(2,1)S(1)}, u32[]{:S(2)}, u32[]{:S(2)}) async-start(bf16[16,56,384]{2,1,0:T(8,128)(2,1)} %shard_map.323), calls=%async_computation.4 | async-start | bytes 1376256 | tf_op jit(solution)/shard_map/all_to_all | solution.py:687
  126.2 10.2 %collective-permute-start.9 = (bf16[2,96,512]{2,1,0:T(8,128)(2,1)S(1)}, bf16[2,96,512]{2,1,0:T(8,128)(2,1)S(1)}, u32[]{:S(2)}, u32[]{:S(2)}) collective-permute-start(bf16[2,96,512]{2,1,0:T(8,128)(2,1)S(1)} %get-tuple-element.102), channel_id=1, source_target_pairs={{0,4},{2,6},{4,0},{6,2},{8,12},{10,14},{12,8},{14,10},{16,20},{18,... | collective-permute-start | bytes 589832 | tf_op jit(solution)/shard_map/ppermute | solution.py:483
  128.2 8.3 %collective-permute-start.8 = (bf16[2,96,512]{2,1,0:T(8,128)(2,1)S(1)}, bf16[2,96,512]{2,1,0:T(8,128)(2,1)S(1)}, u32[]{:S(2)}, u32[]{:S(2)}) collective-permute-start(bf16[2,96,512]{2,1,0:T(8,128)(2,1)S(1)} %get-tuple-element.100), channel_id=1, source_target_pairs={{0,2},{2,0},{4,6},{6,4},{8,10},{10,8},{12,14},{14,12},{16,18},{18,... | collective-permute-start | bytes 589832 | tf_op jit(solution)/shard_map/ppermute | solution.py:483
  129.6 12.8 %collective-permute-start.7 = (bf16[2,96,512]{2,1,0:T(8,128)(2,1)S(1)}, bf16[2,96,512]{2,1,0:T(8,128)(2,1)S(1)}, u32[]{:S(2)}, u32[]{:S(2)}) collective-permute-start(bf16[2,96,512]{2,1,0:T(8,128)(2,1)S(1)} %get-tuple-element.98), channel_id=1, source_target_pairs={{0,8},{2,10},{4,12},{6,14},{8,0},{10,2},{12,4},{14,6},{16,24},{18,... | collective-permute-start | bytes 589832 | tf_op jit(solution)/shard_map/ppermute | solution.py:483
  136.5 8.6 %copy-start.10 = (bf16[2,180,384]{2,1,0:T(8,128)(2,1)S(1)}, bf16[2,180,384]{2,1,0:T(8,128)(2,1)}, u32[]{:S(2)}) copy-start(bf16[2,180,384]{2,1,0:T(8,128)(2,1)} %get-tuple-element.160) | copy-start | bytes 829444
  143.3 2.7 %copy-start = (bf16[16,56,384]{2,1,0:T(8,128)(2,1)}, bf16[16,56,384]{2,1,0:T(8,128)(2,1)S(1)}, u32[]{:S(2)}) copy-start(bf16[16,56,384]{2,1,0:T(8,128)(2,1)S(1)} %all-to-all-done.4.got) | copy-start | bytes 2064388
  143.3 18.9 %collective-permute-start.10 = (bf16[2,48,1536]{2,1,0:T(8,128)(2,1)S(1)}, bf16[2,48,1536]{2,1,0:T(8,128)(2,1)S(1)}, u32[]{:S(2)}, u32[]{:S(2)}) collective-permute-start(bf16[2,48,1536]{2,1,0:T(8,128)(2,1)S(1)} %pad_maximum_fusion), channel_id=1, source_target_pairs={{0,16},{2,18},{4,20},{6,22},{8,24},{10,26},{12,28},{14,30},{16,0},... | collective-permute-start | bytes 884744 | tf_op jit(solution)/shard_map/ppermute | solution.py:692
  149.3 18.6 %all-to-all-start.5 = ((bf16[16,32,384]{2,1,0:T(8,128)(2,1)}), bf16[16,32,384]{2,1,0:T(8,128)(2,1)S(1)}, u32[]{:S(2)}, u32[]{:S(2)}) async-start(bf16[16,32,384]{2,1,0:T(8,128)(2,1)} %get-tuple-element.113), calls=%async_computation.5 | async-start | bytes 786432 | tf_op jit(solution)/shard_map/all_to_all | solution.py:711

commit v3 on v2

--- a/solution.py
+++ b/solution.py
@@ -5,6 +5,7 @@
 import jax.numpy as jnp
 import numpy as np
 from jax import lax
+from jax.experimental.layout import Layout, with_layout_constraint
 from jax.experimental import pallas as pl
 from jax.experimental.pallas import tpu as pltpu
 from jax.sharding import PartitionSpec as P
@@ -66,7 +67,7 @@
     return kept * jnp.cos(angles), kept * jnp.sin(angles)
 
 
-PIECES = 3
+CHUNK = 512
 GELU_A = math.sqrt(2.0 / math.pi)
 GELU_B = 0.044715
 
@@ -137,13 +138,10 @@
     return jnp.sum(values, axis=0, keepdims=True)
 
 
-def norm_one_kernel(columns, padded, groups, all_ref, gain, bias, high, low, freq, base, xh, inverse, pad, tables, sems):
+def norm_one_kernel(columns, padded, groups, all_ref, gain, bias, high, low, freq, xh, inverse, pad, tables, sems):
     mp, rows_dev = all_ref.shape[0], all_ref.shape[1]
     width = mp * all_ref.shape[3]
-    first = lax.axis_index("lat") * rows_dev
-    choice = jnp.int32(0)
-    for r in range(rows_dev):
-        choice = choice + jnp.where(groups[first + r] == 0, 1 << r, 0).astype(jnp.int32)
+    choice = width_choice(groups, rows_dev)
     copies = [
         pltpu.make_async_copy(src.at[choice], tables.at[i], sems.at[i])
         for i, src in enumerate((high, low))
@@ -163,7 +161,6 @@
     x = pad[lax.axis_index("mp")]
     hat = (x - average) * inv
     u = hat * gain[...] + bias[...]
-    base[...] = x + u
     xh[...] = hat
     inverse[...] = inv
     for copy in copies:
@@ -209,38 +206,57 @@
     return out
 
 
-def filter_kernel(blocks, size, z, high, low, weights, biases, eo, s_out, h_out, slope_out, gate_out):
+class Mover:
+    def __init__(self, sems):
+        self.sems, self.count, self.pending = sems, 0, []
+
+    def start(self, src, dst):
+        copy = pltpu.make_async_copy(src, dst, self.sems.at[self.count])
+        self.count += 1
+        copy.start()
+        return copy
+
+    def store(self, src, dst):
+        self.pending.append(self.start(src, dst))
+
+    def finish(self):
+        for copy in self.pending:
+            copy.wait()
+
+
+def filter_kernel(blocks, size, z, high, low, weights, biases, eo, s_h, h_h, slope_h, gate_h, s_s, h_s, slope_s, gate_s, sems):
+    move = Mover(sems)
     w1r, w1i, w2r, w2i = (diagonal(weights[i], blocks, size) for i in range(4))
     n = z.shape[0]
     s = times((high[...], low[...]), z[...]).astype(BF)
-    s_out[...] = s
+    s_s[...] = s
+    move.store(s_s, s_h)
     sr, si = s[:n], s[n:]
     a1r = mm(sr, w1r) - mm(si, w1i) + biases[0:1, :]
     a1i = mm(sr, w1i) + mm(si, w1r) + biases[1:2, :]
     hr, slope = gelu_pair(a1r)
     hr = hr.astype(BF)
-    slope_out[:n, :] = slope
+    slope_s[:n, :] = slope
     hi, slope = gelu_pair(a1i)
     hi = hi.astype(BF)
-    slope_out[n:, :] = slope
-    h_out[:n, :] = hr
-    h_out[n:, :] = hi
+    slope_s[n:, :] = slope
+    move.store(slope_s, slope_h)
+    h_s[:n, :] = hr
+    h_s[n:, :] = hi
+    move.store(h_s, h_h)
     a2r = mm(hr, w2r) - mm(hi, w2i) + biases[2:3, :]
     a2i = mm(hr, w2i) + mm(hi, w2r) + biases[3:4, :]
     tr = jnp.tanh(a2r * (1.0 / SHRINK))
     ti = jnp.tanh(a2i * (1.0 / SHRINK))
-    gate_out[:n, :] = tr * tr
-    gate_out[n:, :] = ti * ti
+    gate_s[:n, :] = tr * tr
+    gate_s[n:, :] = ti * ti
+    move.store(gate_s, gate_h)
     rh, rl = split_in(a2r - SHRINK * tr)
     ih, il = split_in(a2i - SHRINK * ti)
     out = mm_t(high[:n, :], rh) + mm_t(low[:n, :], rh) + mm_t(high[:n, :], rl)
     out += mm_t(high[n:, :], ih) + mm_t(low[n:, :], ih) + mm_t(high[n:, :], il)
     eo[...] = out.astype(BF)
-
-
-def mix_kernel(choice, eo, high, low, base, x1):
-    got = eo[...]
-    x1[...] = base[...] + mm_t(high[0], got) + mm_t(low[0], got)
+    move.finish()
 
 
 def second_norm(parts_of):
@@ -251,98 +267,160 @@
     return average, lax.rsqrt(spread / width + EPSILON)
 
 
-def mlp_kernel(columns, padded, orders, *refs):
-    mp, pieces = refs[0].shape[0], len(orders)
-    dy_all, norms, places, w1, b1, w2, own = refs[:7]
-    others = refs[7 : 6 + mp]
-    send = refs[6 + mp]
-    grads = refs[7 + mp : 7 + mp + 2 * pieces]
-    gb1, n_s, nt_s, dy_s, dyt_s, x1_s, out_acc, dn_acc, pad = refs[7 + mp + 2 * pieces :]
-    step, steps = pl.program_id(0), pl.num_programs(0)
-    ch, width = own.shape[1], w1.shape[0]
-    rows_dev = dy_all.shape[1]
-
-    @pl.when(step == 0)
+def swap_matrix(places):
+    width = places.shape[0]
+    lane = lax.broadcasted_iota(jnp.int32, (width, width), 1)
+    share = width // lax.axis_size("lat")
+    target = (places[:, 0:1] ^ lax.axis_index("lat")) * share + places[:, 1:2]
+    return jnp.where(lane == target, 1.0, 0.0).astype(BF)
+
+
+def cotangent_kernel(columns, padded, dy_all, places, field_all, vectors, w2, dyt, dact, base, pad, dy_s):
+    mp, rows_dev, ch = dy_all.shape[0], dy_all.shape[1], dy_all.shape[3]
+
+    @pl.when(pl.program_id(0) == 0)
     def _():
-        mine = lax.axis_index("mp")
-        x1_s[mine] = own[...]
-        for i, other in enumerate(others):
-            x1_s[lax.rem(mine + 1 + i, mp)] = other[...]
-        average, inv = second_norm([x1_s[m] for m in range(mp)])
         for m in range(mp):
-            lanes = slice(m * ch, (m + 1) * ch)
-            hat = (x1_s[m] - average) * inv
-            n_s[:, lanes] = (hat * norms[m, 0:1, :] + norms[m, 1:2, :]).astype(BF)
             pad[...] = jnp.zeros_like(pad)
             for r in range(rows_dev):
                 pad[r * padded : r * padded + columns, :] = dy_all[m, r].astype(F32)
-            dy_s[:, lanes] = pad[...].astype(BF)
-        me = lax.axis_index("lat")
-        lane = lax.broadcasted_iota(jnp.int32, (width, width), 1)
-        share = width // lax.axis_size("lat")
-        target = (places[:, 0:1] ^ me) * share + places[:, 1:2]
-        move = jnp.where(lane == target, 1.0, 0.0).astype(BF)
-        nt_s[...] = mm_nt(move, n_s[...]).astype(BF)
-        dyt_s[...] = mm_nt(move, dy_s[...]).astype(BF)
-        out_acc[...] = jnp.zeros_like(out_acc)
-        dn_acc[...] = jnp.zeros_like(dn_acc)
-
-    p = mm(n_s[...], w1[...]) + b1[...]
-    q, slope = gelu_pair(p)
-    q = q.astype(BF)
-    dp = (mm_nt(dy_s[...], w2[...]) * slope).astype(BF)
-    dn_acc[...] += mm_nt(dp, w1[...])
-    out_acc[...] += mm(q, w2[...])
-    gb1[...] = column_sum(dp.astype(F32))
-    both = (mm(nt_s[...], dp), mm(dyt_s[...], q))
+            dy_s[:, m * ch : (m + 1) * ch] = pad[...].astype(BF)
+        dyt[...] = mm_nt(swap_matrix(places), dy_s[...]).astype(BF)
+        for m in range(mp):
+            base[m] = jnp.zeros(base.shape[1:], F32)
+            for r in range(rows_dev):
+                base[m, r * padded : r * padded + columns, :] = field_all[m, r].astype(F32)
+        average, inv = second_norm([base[m] for m in range(mp)])
+        for m in range(mp):
+            x = base[m]
+            base[m] = x + (x - average) * inv * vectors[m, 0:1, :] + vectors[m, 1:2, :]
+
+    dact[...] = mm_nt(dy_s[...], w2[...])
+
+
+def width_choice(groups, rows_dev):
+    first = lax.axis_index("lat") * rows_dev
+    choice = jnp.int32(0)
+    for r in range(rows_dev):
+        choice = choice + jnp.where(groups[first + r] == 0, 1 << r, 0).astype(jnp.int32)
+    return choice
+
+
+def mlp_kernel(orders, rows_dev, groups, vectors, b1, places, eo_h, high_h, low_h, base_h, w1_h, dact_h, w2_h, dyt_h, *refs):
+    mp, pieces = vectors.shape[0], len(orders)
+    kept_h, away_h, gb1, norm_out, own_h = refs[:5]
+    grads_h = refs[5 : 5 + 2 * pieces]
+    eo, table, base, w1, dact, w2, dyt, kept_send, away_send = refs[5 + 2 * pieces : 14 + 2 * pieces]
+    grads = refs[14 + 2 * pieces : 14 + 4 * pieces]
+    n_s, nt_s, q_s, dp_s, sems = refs[14 + 4 * pieces :]
+    ch, width, hidden = base.shape[2], w1.shape[0], w1.shape[1]
+    chunk = hidden // pieces
+    mine = lax.axis_index("mp")
+    choice = width_choice(groups, rows_dev)
+    move = Mover(sems)
+    first = [
+        move.start(high_h.at[choice], table.at[0]),
+        move.start(low_h.at[choice], table.at[1]),
+        move.start(eo_h, eo),
+        move.start(base_h, base),
+    ]
+    spans = [slice(p * chunk, (p + 1) * chunk) for p in range(pieces)]
+    swap = swap_matrix(places)
+    for copy in first:
+        copy.wait()
+    loads = []
+    for p in range(pieces):
+        loads.append(
+            (
+                move.start(w1_h.at[:, spans[p]], w1.at[:, spans[p]]),
+                move.start(dact_h.at[:, spans[p]], dact.at[:, spans[p]]),
+            )
+        )
+    load_w2 = move.start(w2_h, w2)
+    load_dyt = move.start(dyt_h, dyt)
+    for m in range(mp):
+        base[m] = base[m] + mm_t(table[0], eo[m]) + mm_t(table[1], eo[m])
+    move.store(base.at[mine], own_h)
+    average, inv = second_norm([base[m] for m in range(mp)])
+    spot = lax.broadcasted_iota(jnp.int32, norm_out.shape, 1)
+    norm_out[...] = jnp.where(spot == 0, average, inv)
+    for m in range(mp):
+        hat = (base[m] - average) * inv
+        n_s[:, m * ch : (m + 1) * ch] = (hat * vectors[m, 2:3, :] + vectors[m, 3:4, :]).astype(BF)
+    nt_s[...] = mm_nt(swap, n_s[...]).astype(BF)
+
     for piece, bits in enumerate(orders):
+        span = spans[piece]
+        for copy in loads[piece]:
+            copy.wait()
+        q, slope = gelu_pair(mm(n_s[...], w1[:, span]) + b1[:, span])
+        q = q.astype(BF)
+        q_s[:, span] = q
+        dp = (dact[:, span] * slope).astype(BF)
+        dp_s[:, span] = dp
+        gb1[:, span] = column_sum(dp.astype(F32))
+
+    dn = mm_nt(dp_s[...], w1[...])
+    plain, cross = 0.0, 0.0
+    for m in range(mp):
+        scaled = dn[:, m * ch : (m + 1) * ch] * vectors[m, 2:3, :]
+        plain += jnp.sum(scaled, axis=1, keepdims=True)
+        cross += jnp.sum(scaled * ((base[m] - average) * inv), axis=1, keepdims=True)
+    spot = lax.broadcasted_iota(jnp.int32, (plain.shape[0], 128), 1)
+    stat = jnp.zeros(spot.shape, F32)
+    for at, value in ((0, plain), (3, cross)):
+        for i in range(3):
+            term = value.astype(BF).astype(F32)
+            value = value - term
+            stat = jnp.where(spot == at + i, term, stat)
+    stat = stat.astype(BF)
+    load_w2.wait()
+    out = mm(q_s[...], w2[...])
+    for m in range(mp):
+        lanes = slice(m * ch, (m + 1) * ch)
+
+        def put(ref):
+            ref[:, :ch] = out[:, lanes].astype(BF)
+            ref[:, ch : 2 * ch] = dn[:, lanes].astype(BF)
+            ref[:, 2 * ch :] = stat
+
+        @pl.when(mine == m)
+        def _():
+            put(kept_send)
+
+        for other in range(mp):
+            if other != m:
+
+                @pl.when(mine == other)
+                def _():
+                    put(away_send.at[(m - other) % mp - 1])
+
+    move.store(away_send, away_h)
+    move.store(kept_send, kept_h)
+    load_dyt.wait()
+    for piece, bits in enumerate(orders):
+        span = spans[piece]
         kept, away = grads[2 * piece : 2 * piece + 2]
         count = len(bits)
         rows = width >> count
-
-        @pl.when((step * pieces) // steps == piece)
-        def _():
-            for i, grad in enumerate(both):
-                for spot in range(2**count):
-                    who = sum(((spot >> (count - 1 - b)) & 1) * bit for b, bit in enumerate(bits))
-                    block = grad[who * rows : (who + 1) * rows, :].astype(BF)
-                    at = (spot % 2 ** (count - 1)) * rows
-                    (away if spot >> (count - 1) else kept)[i, at : at + rows, :] = block
-
-    @pl.when(step == steps - 1)
-    def _():
-        halves = [x1_s[m] for m in range(mp)]
-        average, inv = second_norm(halves)
-        plain, cross = 0.0, 0.0
-        for m in range(mp):
-            lanes = slice(m * ch, (m + 1) * ch)
-            part = dn_acc[:, lanes]
-            scaled = part * norms[m, 0:1, :]
-            plain += jnp.sum(scaled, axis=1, keepdims=True)
-            cross += jnp.sum(scaled * ((halves[m] - average) * inv), axis=1, keepdims=True)
-            send[m, :, :ch] = out_acc[:, lanes].astype(BF)
-            send[m, :, ch : 2 * ch] = part.astype(BF)
-        spot = lax.broadcasted_iota(jnp.int32, (plain.shape[0], 128), 1)
-        stat = jnp.zeros(spot.shape, BF)
-        for first, value in ((0, plain), (3, cross)):
-            for i in range(3):
-                term = value.astype(BF)
-                value = value - term.astype(F32)
-                stat = jnp.where(spot == first + i, term.astype(F32), stat.astype(F32)).astype(BF)
-        for m in range(mp):
-            send[m, :, 2 * ch :] = stat
-
-
-def back_mix_kernel(columns, padded, choice, got, dy, gain, bias2, high, low, own, *refs):
-    mp, ch = got.shape[0], own.shape[1]
-    others = refs[: mp - 1]
-    out_field, dx1, freq, sums, pad = refs[mp - 1 :]
-    rows_dev = dy.shape[0]
-    width = mp * ch
+        for i, grad in enumerate((mm(nt_s[...], dp_s[:, span]), mm(dyt[...], q_s[:, span]))):
+            for place in range(2**count):
+                who = sum(((place >> (count - 1 - b)) & 1) * bit for b, bit in enumerate(bits))
+                block = grad[who * rows : (who + 1) * rows, :].astype(BF)
+                at = (place % 2 ** (count - 1)) * rows
+                (away if place >> (count - 1) else kept)[i, at : at + rows, :] = block
+            move.store(away.at[i], grads_h[2 * piece + 1].at[i])
+            move.store(kept.at[i], grads_h[2 * piece].at[i])
+    move.finish()
+
+
+def back_mix_kernel(columns, padded, width, choice, dy, gain, bias2, high, low, norm_in, own, *refs):
+    got, (out_field, dx1, freq, sums, pad) = refs[:-5], refs[-5:]
+    ch, rows_dev = own.shape[1], dy.shape[0]
     x1 = own[...]
-    average, inv = second_norm([x1] + [other[...] for other in others])
+    average, inv = norm_in[:, 0:1], norm_in[:, 1:2]
     hat = (x1 - average) * inv
-    total = sum(got[m].astype(F32) for m in range(mp))
+    total = sum(piece[...].astype(F32) for piece in got)
     out = x1 + total[:, :ch] + bias2[...]
     dn = total[:, ch : 2 * ch]
     pad[...] = jnp.zeros_like(pad)
@@ -405,7 +483,7 @@
     send[...] = rows[...].astype(BF)
 
 
-def back_norm_kernel(group, share, choice, got, high, low, dx1, xh, gain, du_out, stat, tail, tail_s):
+def back_norm_kernel(group, share, shares, choice, got, high, low, dx1, xh, inverse, gain, du_out, stat, tail, tail_s):
     parts, _, ch = got.shape
     every = got[...].astype(F32)
     deo = every[:, :group, :].reshape(parts * group, ch).astype(BF)
@@ -418,11 +496,9 @@
     hat = xh[...]
     scaled = du * gain[...]
     spot = lax.broadcasted_iota(jnp.int32, stat.shape, 1)
-    stat[...] = jnp.where(
-        spot == 0,
-        jnp.sum(scaled, axis=1, keepdims=True),
-        jnp.sum(scaled * hat, axis=1, keepdims=True),
-    )
+    plain = jnp.sum(scaled, axis=1, keepdims=True)
+    cross = jnp.sum(scaled * hat, axis=1, keepdims=True)
+    stat[...] = jnp.where(spot == 0, plain, jnp.where(spot == 1, cross, inverse[...] / shares))
     for i, row in enumerate((total, column_sum(du * hat), column_sum(du))):
         first = row.astype(BF).astype(F32)
         tail_s[share + 2 * i : share + 2 * i + 1, :] = first
@@ -432,12 +508,29 @@
         tail[d] = whole_tail
 
 
-def last_kernel(columns, padded, width, du, dx1, xh, inverse, gain, stats, out):
-    plain = stats[:, 0:1] / width
-    cross = stats[:, 1:2] / width
-    value = dx1[...] + inverse[...] * (du[...] * gain[...] - plain - xh[...] * cross)
-    for r in range(out.shape[0]):
-        out[r] = value[r * padded : r * padded + columns, :]
+def close_kernel(share, blocks, size, tail, n1g, n1b, w1, b1, w2, b2, n2g, n2b, gb1, gb2, rows):
+    parts = tail.shape[0]
+    for d in range(parts):
+        rows[d * share : (d + 1) * share, :] = tail[d, :share, :].astype(F32)
+    for i, out in enumerate((w1, w1, w2, w2)):
+        for n in range(blocks):
+            out[i % 2, n] = rows[i * size : (i + 1) * size, n * size : (n + 1) * size]
+
+    def pair(d, i):
+        both = tail[d, share + 2 * i : share + 2 * i + 2, :].astype(F32)
+        return both[0:1] + both[1:2]
+
+    for i, out in enumerate((b1, b1, b2, b2)):
+        row = pair(i, 0)
+        for n in range(blocks):
+            out[i % 2, n : n + 1, :] = row[:, n * size : (n + 1) * size]
+    n2g[...] = pair(4, 0)[0]
+    n2b[...] = pair(5, 0)[0]
+    gb2[...] = pair(6, 0)[0]
+    for i in range(gb1.shape[0]):
+        gb1[i : i + 1, :] = pair(7 + i, 0)
+    n1g[...] = sum(pair(d, 1) for d in range(parts))[0]
+    n1b[...] = sum(pair(d, 2) for d in range(parts))[0]
 
 
 def whole(shape, extra=0):
@@ -479,16 +572,26 @@
     )(choice, *args)
 
 
-def halve(kept, away, bit, parts):
-    got = lax.ppermute(away, "lat", [(d, d ^ bit) for d in range(parts)])
+def added(terms):
+    return sum(term.astype(F32) for term in terms)
+
+
+def swapped(away, bit, parts):
+    return lax.ppermute(away, "lat", [(d, d ^ bit) for d in range(parts)])
+
+
+def folded(kept, got):
     half = kept.shape[1] // 2
     away = (kept[:, half:].astype(F32) + got[:, half:].astype(F32)).astype(BF)
-    kept = kept[:, :half].astype(F32) + got[:, :half].astype(F32)
-    return kept, away
-
-
-def after(value, arrays):
-    return lax.optimization_barrier((value, arrays))
+    return kept[:, :half].astype(F32) + got[:, :half].astype(F32), away
+
+
+def halve(kept, away, bit, parts):
+    return folded(kept, swapped(away, bit, parts))
+
+
+def tied(value, states):
+    return lax.optimization_barrier((value, states))
 
 
 def body(
@@ -533,24 +636,23 @@
     choice = sum(
         jnp.where(local_group[r] == 0, 1 << r, 0) for r in range(rows_dev)
     ).astype(jnp.int32).reshape(1)
-    gain1, bias1 = norm1_gain.reshape(1, ch), norm1_bias.reshape(1, ch)
 
     field_all = lax.all_gather(field, "mp", axis=0)
     table = pltpu.VMEM((2, patches, tokens), BF)
-    freq, base, xh1, inv1 = pl.pallas_call(
+    freq, xh1, inv1 = pl.pallas_call(
         functools.partial(norm_one_kernel, columns, padded),
-        out_shape=[f32(patches, ch), f32(tokens, ch), f32(tokens, ch), f32(tokens, 1)],
+        out_shape=[f32(patches, ch), f32(tokens, ch), f32(tokens, 1)],
         in_specs=[pl.BlockSpec(memory_space=pltpu.SMEM)]
         + [pl.BlockSpec(memory_space=pltpu.VMEM)] * 3
         + [pl.BlockSpec(memory_space=pl.ANY)] * 2,
-        out_specs=[pl.BlockSpec(memory_space=pltpu.VMEM)] * 4,
+        out_specs=[pl.BlockSpec(memory_space=pltpu.VMEM)] * 3,
         scratch_shapes=[
             pltpu.VMEM((mp, tokens, ch), F32),
             table,
             pltpu.SemaphoreType.DMA((2,)),
         ],
         compiler_params=pltpu.CompilerParams(vmem_limit_bytes=56 * 2**20),
-    )(row_group, field_all, gain1, bias1, *lon)
+    )(row_group, field_all, norm1_gain, norm1_bias, *lon)
 
     def to_other(values, rows_each):
         return lax.all_to_all(values.reshape(parts, rows_each, ch), "lat", 0, 0, tiled=True)
@@ -573,103 +675,141 @@
     )
     spec = jnp.stack([spec_w1, spec_w2]).transpose(0, 1, 3, 2, 4).reshape(4, size, ch)
     spec_bias = jnp.concatenate([spec_b1.reshape(2, ch), spec_b2.reshape(2, ch)], axis=0)
-    norms = lax.all_gather(jnp.stack([norm2_gain, norm2_bias]), "mp", axis=0)
+    vectors = jnp.concatenate([norm1_gain, norm1_bias, norm2_gain, norm2_bias]).reshape(4, ch)
+    vectors_all = lax.all_gather(vectors, "mp", axis=0)
     dy_all = lax.all_gather(cotangent, "mp", axis=0)
-    z, norms, dy_all = lax.optimization_barrier((z, norms, dy_all))
-
-    eo, s, h, slope, gate = run(
+    z, vectors_all, dy_all = lax.optimization_barrier((z, vectors_all, dy_all))
+
+    saved = [bf(2 * patches, ch), bf(2 * patches, ch), f32(2 * patches, ch), f32(2 * patches, ch)]
+    vmem, hbm = pl.BlockSpec(memory_space=pltpu.VMEM), pl.BlockSpec(memory_space=pl.ANY)
+    eo, s, h, slope, gate = pl.pallas_call(
         functools.partial(filter_kernel, blocks, size),
-        [bf(patches, ch), bf(2 * patches, ch), bf(2 * patches, ch), f32(2 * patches, ch), f32(2 * patches, ch)],
-        [z, *lat, spec, spec_bias],
-    )
-    eo = to_other(eo, group).reshape(patches, ch)
-    (x1,) = run(mix_kernel, [f32(tokens, ch)], [eo, *lon, base], (), (1, 2), choice)
-
-    others = [
-        lax.ppermute(x1, "mp", [((d + i) % mp, d) for d in range(mp)]) for i in range(1, mp)
-    ]
-    chunk = 256
+        out_shape=[bf(patches, ch), *saved],
+        in_specs=[vmem] * 5,
+        out_specs=[vmem] + [hbm] * 4,
+        scratch_shapes=[pltpu.VMEM(a.shape, a.dtype) for a in saved]
+        + [pltpu.SemaphoreType.DMA((4,))],
+        compiler_params=pltpu.CompilerParams(vmem_limit_bytes=56 * 2**20),
+    )(z, *lat, spec, spec_bias)
+    chunk = CHUNK if hidden % (3 * CHUNK) == 0 else 256
     steps = hidden // chunk
     bits = [1 << b for b in range(parts.bit_length() - 1)]
     orders = [bits[i:3] + bits[:i] + bits[3:] for i in range(3)]
     pieces = len(orders)
-    each = steps // pieces
-    grad_specs = [
-        pl.BlockSpec(
-            (2, full_width // 2, chunk),
-            functools.partial(lambda p, i: (0, 0, jnp.clip(i - p * each, 0, each - 1)), p),
-        )
-        for p in range(pieces)
-        for _ in range(2)
-    ]
     share_rows = full_width // parts
     places = np.stack(
         [np.arange(full_width) // share_rows, np.arange(full_width) % share_rows], axis=1
     ).astype(np.int32)
-    send, *grads, g_fc1_bias = pl.pallas_call(
-        functools.partial(mlp_kernel, columns, padded, orders),
-        out_shape=[
-            bf(mp, tokens, 2 * ch + 128),
-            *[bf(2, full_width // 2, hidden // pieces)] * (2 * pieces),
-            f32(1, hidden),
-        ],
+    dyt, dact, base = pl.pallas_call(
+        functools.partial(cotangent_kernel, columns, padded),
+        out_shape=[bf(full_width, tokens), f32(tokens, hidden), f32(mp, tokens, ch)],
         grid=(steps,),
         in_specs=[
             whole(dy_all.shape),
-            whole(norms.shape),
-            whole((full_width, 2)),
-            pl.BlockSpec((full_width, chunk), lambda i: (0, i)),
-            pl.BlockSpec((1, chunk), lambda i: (0, i)),
+            whole(places.shape),
+            whole(field_all.shape),
+            whole(vectors_all.shape),
             pl.BlockSpec((chunk, full_width), lambda i: (i, 0)),
-            *[whole((tokens, ch))] * mp,
         ],
         out_specs=[
-            whole((mp, tokens, 2 * ch + 128)),
-            *grad_specs,
-            pl.BlockSpec((1, chunk), lambda i: (0, i)),
+            whole((full_width, tokens)),
+            pl.BlockSpec((tokens, chunk), lambda i: (0, i)),
+            whole((mp, tokens, ch)),
         ],
+        scratch_shapes=[pltpu.VMEM((tokens, ch), F32), pltpu.VMEM((tokens, full_width), BF)],
+        compiler_params=pltpu.CompilerParams(vmem_limit_bytes=56 * 2**20),
+    )(dy_all, jnp.asarray(places), field_all, vectors_all, fc2_weight)
+    eo = to_other(eo, group).reshape(patches, ch)
+    eo, dyt, dact, base = lax.optimization_barrier((eo, dyt, dact, base))
+    eo = lax.all_gather(eo, "mp", axis=0)
+
+    send_lanes = 2 * ch + 128
+    piece_shape = (2, full_width // 2, hidden // pieces)
+    kept_send, away_send, g_fc1_bias, norm2, x1, *grads = pl.pallas_call(
+        functools.partial(mlp_kernel, orders, rows_dev),
+        out_shape=[
+            bf(tokens, send_lanes),
+            bf(mp - 1, tokens, send_lanes),
+            f32(1, hidden),
+            f32(tokens, 2),
+            f32(tokens, ch),
+            *[bf(*piece_shape)] * (2 * pieces),
+        ],
+        in_specs=[pl.BlockSpec(memory_space=pltpu.SMEM), vmem, vmem, vmem] + [hbm] * 8,
+        out_specs=[hbm, hbm, vmem, vmem, hbm] + [hbm] * (2 * pieces),
         scratch_shapes=[
+            pltpu.VMEM(eo.shape, BF),
+            table,
+            pltpu.VMEM(base.shape, F32),
+            pltpu.VMEM(fc1_weight.shape, BF),
+            pltpu.VMEM(dact.shape, F32),
+            pltpu.VMEM(fc2_weight.shape, BF),
+            pltpu.VMEM(dyt.shape, BF),
+            pltpu.VMEM((tokens, send_lanes), BF),
+            pltpu.VMEM((mp - 1, tokens, send_lanes), BF),
+            *[pltpu.VMEM(piece_shape, BF)] * (2 * pieces),
             pltpu.VMEM((tokens, full_width), BF),
             pltpu.VMEM((full_width, tokens), BF),
-            pltpu.VMEM((tokens, full_width), BF),
-            pltpu.VMEM((full_width, tokens), BF),
-            pltpu.VMEM((mp, tokens, ch), F32),
-            pltpu.VMEM((tokens, full_width), F32),
-            pltpu.VMEM((tokens, full_width), F32),
-            pltpu.VMEM((tokens, ch), F32),
+            pltpu.VMEM((tokens, hidden), BF),
+            pltpu.VMEM((tokens, hidden), BF),
+            pltpu.SemaphoreType.DMA((16 + 8 * pieces,)),
         ],
         compiler_params=pltpu.CompilerParams(vmem_limit_bytes=56 * 2**20),
         cost_estimate=pl.CostEstimate(
-            flops=12 * tokens * full_width * hidden, bytes_accessed=16 * 2**20, transcendentals=0
+            flops=10 * tokens * full_width * hidden, bytes_accessed=16 * 2**20, transcendentals=0
         ),
     )(
-        dy_all,
-        norms,
+        row_group,
+        vectors_all,
+        fc1_bias.reshape(1, hidden),
         jnp.asarray(places),
+        eo,
+        *lon,
+        base,
         fc1_weight,
-        fc1_bias.reshape(1, hidden),
+        dact,
         fc2_weight,
-        x1,
-        *others,
-    )
-    got = lax.all_to_all(send, "mp", 0, 0, tiled=True)
+        dyt,
+    )
+    got = [
+        lax.ppermute(away_send[i - 1], "mp", [(d, (d + i) % mp) for d in range(mp)])
+        for i in range(1, mp)
+    ]
+
     def exchange(states, turn):
         return [halve(*state, order[turn], parts) for state, order in zip(states, orders)]
 
-    sums = exchange([grads[2 * p : 2 * p + 2] for p in range(pieces)], 0)
+    def received(states, turn):
+        return [
+            (kept, swapped(away, order[turn], parts)) for (kept, away), order in zip(states, orders)
+        ]
+
+    states = [(grads[2 * p], grads[2 * p + 1]) for p in range(pieces)]
+    states = exchange(states, 0)
 
     out_field, dx1, dfreq, sums2 = run(
-        functools.partial(back_mix_kernel, columns, padded),
+        functools.partial(back_mix_kernel, columns, padded, full_width),
         [bf(rows_dev, columns, ch), f32(tokens, ch), bf(patches, ch), f32(8, ch)],
-        [got, cotangent, norm2_gain.reshape(1, ch), fc2_bias.reshape(1, ch), *lon, x1, *others],
+        [
+            cotangent,
+            norm2_gain,
+            fc2_bias,
+            *lon,
+            norm2,
+            x1,
+            kept_send,
+            *got,
+        ],
         [pltpu.VMEM((tokens, ch), F32)],
-        (4, 5),
+        (3, 4),
         choice,
     )
 
     dz = to_other(dfreq, group).reshape(patches, ch)
-    dz, sums = after(dz, sums)
-    sums = exchange(sums, 1)
+    dz, out_field = lax.optimization_barrier(
+        (dz, with_layout_constraint(out_field, Layout(major_to_minor=(1, 0, 2))))
+    )
+    dz, states = tied(dz, states)
     spec_rows = 4 * size // parts
     send_rows = -(-(group + spec_rows + 2) // 8) * 8
     (sent,) = run(
@@ -682,52 +822,54 @@
             pltpu.VMEM((max(parts, 16), ch), F32),
         ],
     )
-    sent, sums = after(sent, sums)
-    sums = exchange(sums, 2)
+    sent, states = tied(sent, received(states, 1))
+    states = exchange([folded(*state) for state in states], 2)
     sent = lax.all_to_all(sent, "lat", 0, 0, tiled=True)
-    sent, sums = after(sent, sums)
-    kept, away = (jnp.concatenate([state[i] for state in sums], axis=2) for i in range(2))
+    sent, states = tied(sent, states)
+    kept, away = (jnp.concatenate([state[i] for state in states], axis=2) for i in range(2))
     for bit in bits[3:-1]:
         kept, away = halve(kept, away, bit, parts)
     got_last = lax.ppermute(away, "lat", [(d, d ^ bits[-1]) for d in range(parts)])
     tail_rows = -(-(spec_rows + 6) // 16) * 16
     du, stat1, tail = run(
-        functools.partial(back_norm_kernel, group, spec_rows),
-        [f32(tokens, ch), f32(tokens, 2), bf(parts, tail_rows, ch)],
-        [sent, *lon, dx1, xh1, gain1],
+        functools.partial(back_norm_kernel, group, spec_rows, mp),
+        [f32(tokens, ch), f32(tokens, 3), bf(parts, tail_rows, ch)],
+        [sent, *lon, dx1, xh1, inv1, norm1_gain],
         [pltpu.VMEM((tail_rows, ch), F32)],
         (1, 2),
         choice,
     )
     stat1 = lax.psum(stat1, "mp")
-    stat1, got_last = after(stat1, got_last)
+    stat1, got_last = lax.optimization_barrier((stat1, got_last))
     weights = kept + got_last.astype(F32)
-    (grad_field,) = run(
-        functools.partial(last_kernel, columns, padded, full_width),
-        [f32(rows_dev, columns, ch)],
-        [du, dx1, xh1, inv1, gain1, stat1],
-    )
-
-    tail = lax.all_to_all(tail, "lat", 0, 0, tiled=True).astype(F32)
-    g_spec = tail[:, :spec_rows].reshape(2, 2, size, blocks, size).transpose(0, 1, 3, 2, 4)
-    pairs = tail[:, spec_rows : spec_rows + 6].reshape(parts, 3, 2, ch).sum(axis=2)
-    small = pairs[:, 0]
-    norm1 = pairs[:, 1:].sum(axis=0)
+    grad_field = dx1 + stat1[:, 2:] * (
+        du * norm1_gain - (stat1[:, :1] + xh1 * stat1[:, 1:2]) * (1.0 / full_width)
+    )
+    grad_field = grad_field.reshape(rows_dev, padded, ch)[:, :columns]
+
+    tail = lax.all_to_all(tail, "lat", 0, 0, tiled=True)
+    vector, weight, bias = f32(ch), f32(2, blocks, size, size), f32(2, blocks, size)
+    g_n1g, g_n1b, g_w1, g_b1, g_w2, g_b2, g_n2g, g_n2b, g_fc1b, g_fc2b = run(
+        functools.partial(close_kernel, spec_rows, blocks, size),
+        [vector, vector, weight, bias, weight, bias, vector, vector, f32(hidden // ch, ch), vector],
+        [tail],
+        [pltpu.VMEM((4 * size, ch), F32)],
+    )
     return (
         out_field,
         grad_field,
-        norm1[0],
-        norm1[1],
-        g_spec[0],
-        small[0:2].reshape(2, blocks, size),
-        g_spec[1],
-        small[2:4].reshape(2, blocks, size),
-        small[4],
-        small[5],
+        g_n1g,
+        g_n1b,
+        g_w1,
+        g_b1,
+        g_w2,
+        g_b2,
+        g_n2g,
+        g_n2b,
         weights[0],
-        small[7 : 7 + hidden // ch].reshape(hidden),
+        g_fc1b.reshape(hidden),
         weights[1].T,
-        small[6],
+        g_fc2b,
     )
 
 

time: 174 us -> 161 us (0.925)
  waiting for transfers between devices: 35.1 us -> 27.8 us
  local copies, waits for them, and re-layouts: 19.4 us -> 13.9 us
  blocking collectives: 18.7 us -> 13.8 us
  starting transfers between devices: 36.3 us -> 38.8 us
    pallas_call x1 -> x3, Pallas kernels: 16.8 us -> 28.2 us  [the longest x1 15.1 us: body(): pl.pallas_call(functools.partial(mlp_kernel, orders, rows_dev), out_shape...]
    all_to_all x3, waiting for transfers between devices: 16.5 us -> 9.03 us  [to_other(): lax.all_to_all(values.reshape(parts, rows_each, ch), 'lat', 0, 0, tiled=T...]
    pallas_call x4 -> x3, Pallas kernels: 20.5 us -> 13.3 us  [run(): pl.pallas_call(kernel, out_shape=out_shape, in_specs=[pl.BlockSpec(memory...]
    all_to_all x1 -> x0, blocking collectives: 6.86 us -> none  [body(): got = lax.all_to_all(send, 'mp', 0, 0, tiled=True)]
    reshape x8 -> x1, local copies, waits for them, and re-layouts: 4.87 us -> 1.3 us  [body(): g_fc1b.reshape(hidden)]
    pallas_call x3 -> x2, Pallas kernels: 10.6 us -> 7.22 us  [run(): pl.pallas_call(kernel, out_shape=out_shape, grid_spec=pltpu.PrefetchScala...]
    all_gather x1 -> x2, blocking collectives: 1.92 us -> 4.46 us  [the longest x1 2.53 us: body(): eo = lax.all_gather(eo, 'mp', axis=0)]
    unnamed x54 -> x61, local copies, waits for them, and re-layouts: 7.42 us -> 5.37 us
  transfers between devices with their start and end apart: 16 -> 16, of which waited for: 9 -> 8; matrix products, arithmetic and copies ran while one was open for 10% -> 12% of each run, Pallas kernels for 13% -> 16%
where the time goes in v3:
time: 161 us; the launch traced here: 159 us
  Pallas kernels  52.4 us (33%)
  starting transfers between devices  38.8 us (24%)
  waiting for transfers between devices  27.8 us (17%)
  local copies, waits for them, and re-layouts  13.9 us (9%)
  blocking collectives  13.8 us (9%)
  other arithmetic  10.2 us (6%)
  between operations  2.48 us (2%)
    all_to_all x3, starting transfers between devices, to_other(): lax.all_to_all(values.reshape(parts, rows_each, ch), 'lat', 0, 0, tiled=T...  17 us
    pallas_call x1, Pallas kernels, body(): pl.pallas_call(functools.partial(mlp_kernel, orders, rows_dev), out_shape...  15.1 us
    ppermute x9, waiting for transfers between devices, swapped(): return lax.ppermute(away, 'lat', [(d, d ^ bit) for d in range(parts)])  15 us
    pallas_call x3, Pallas kernels, run(): pl.pallas_call(kernel, out_shape=out_shape, in_specs=[pl.BlockSpec(memory...  13.3 us
    ppermute x9, starting transfers between devices, swapped(): return lax.ppermute(away, 'lat', [(d, d ^ bit) for d in range(parts)])  10 us
    all_to_all x3, waiting for transfers between devices, to_other(): lax.all_to_all(values.reshape(parts, rows_each, ch), 'lat', 0, 0, tiled=T...  9.03 us
    pallas_call x2, Pallas kernels, run(): pl.pallas_call(kernel, out_shape=out_shape, grid_spec=pltpu.PrefetchScala...  7.22 us
    convert_element_type x9, other arithmetic, folded(): away = (kept[:, half:].astype(F32) + got[:, half:].astype(F32)).astype(BF)  6.8 us
  transfers between devices with their start and end apart: 16, of which 8 were waited for; matrix products, arithmetic and copies ran while one was open for 12% of the time, Pallas kernels for 16%

profile of v3, /device:TPU:0, one launch (start us, length us, event | category | flops | bytes accessed | tf_op | source)
XLA Modules:
  0.0 159.4 jit_solution(5620934849732617777)
XLA Ops:
  0.6 1.0 copy.56
  1.6 2.4 %all-gather = bf16[4,180,384]{2,1,0:T(8,128)(2,1)} all-gather(bf16[2,180,384]{2,1,0:T(8,128)(2,1)S(1)} %copy.56), channel_id=2, replica_groups=mesh['lat'=16,'mp'=2] {'mp'}, dimensions={0}, use_global_device_ids=true | all-gather | bytes 829440 | tf_op jit(solution)/shard_map/all_gather | solution.py:640
  4.1 3.7 %shard_map.317 = (f32[384,384]{1,0:T(8,128)}, f32[384,384]{1,0:T(8,128)}, f32[384,1]{1,0:T(8,128)}) custom-call(s32[32]{0:T(128)} %groups.3, bf16[2,2,180,384]{3,2,1,0:T(8,128)(2,1)} %bitcast.21, f32[384]{0:T(512)} %gain.5, f32[384]{0:T(512)} %bias.1, bf16[4,384,384]{2,1,0:T(8,128)(2,1)} %constant.66.clone.high.high_h, ...), custom_call_target="tpu_custom_call" | custom-call | tf_op jit(solution)/shard_map/pallas_call | solution.py:642
  7.9 8.4 %all-to-all-start = ((f32[16,24,384]{2,1,0:T(8,128)}), f32[16,24,384]{2,1,0:T(8,128)S(1)}, u32[]{:S(2)}, u32[]{:S(2)}) async-start(f32[16,24,384]{2,1,0:T(8,128)} %bitcast.28), calls=%async_computation | async-start | bytes 1179648 | tf_op jit(solution)/shard_map/all_to_all | solution.py:658
  16.9 0.7 sub.27.keep
  17.8 0.2 copy.60
  18.0 1.0 reshape.167.weights
  19.0 0.2 fusion.3
  19.2 0.3 select_multiply_fusion.1
  19.5 0.7 pad_maximum_fusion.1.tables
  20.2 2.6 %shard_map.318 = (bf16[768,384]{1,0:T(8,128)(2,1)}, bf16[768,384]{1,0:T(8,128)(2,1)}) custom-call(f32[32,64]{1,0:T(8,128)} %pad_maximum_fusion.1.tables, bf16[192,32]{1,0:T(8,128)(2,1)} %constant.68.clone.left, bf16[4,64,384]{2,1,0:T(8,128)(2,1)} %constant.69.clone.right, bf16[192,384]{1,0:T(8,128)(2,1)} %constant.70.clone.same, f32[192,1]{1,0:T(8,128)} %sub.27.keep), custom_call_target="tpu_custom_call" | custom-call | bytes 1544960 | tf_op jit(solution)/shard_map/pallas_call | solution.py:547
  22.9 1.9 %all_gather.23.vectors = f32[2,4,384]{2,1,0:T(4,128)} all-gather(f32[1,4,384]{2,1,0:T(4,128)S(1)} %all_gather_reshape.3), channel_id=1, replica_groups=mesh['lat'=16,'mp'=2] {'mp'}, dimensions={0}, use_global_device_ids=true | all-gather | bytes 18432 | tf_op jit(solution)/shard_map/all_gather | solution.py:679
  24.8 0.6 pad_maximum_fusion.3.biases
  25.4 2.3 %all-gather.1 = bf16[4,180,384]{2,1,0:T(8,128)(2,1)} all-gather(bf16[2,180,384]{2,1,0:T(8,128)(2,1)S(1)} %copy.61.dy), channel_id=3, replica_groups=mesh['lat'=16,'mp'=2] {'mp'}, dimensions={0}, use_global_device_ids=true | all-gather | bytes 829440 | tf_op jit(solution)/shard_map/all_gather | solution.py:680
  27.8 5.1 %all-to-all-done = f32[16,24,384]{2,1,0:T(8,128)S(1)} async-done(((f32[16,24,384]{2,1,0:T(8,128)}), f32[16,24,384]{2,1,0:T(8,128)S(1)}, u32[]{:S(2)}, u32[]{:S(2)}) %all-to-all-start) | async-done | bytes 589856 | tf_op jit(solution)/shard_map/all_to_all | solution.py:658
  32.8 0.8 copy-done.2
  33.6 6.7 %shard_map.319 = (bf16[384,384]{1,0:T(8,128)(2,1)}, bf16[768,384]{1,0:T(8,128)(2,1)}, bf16[768,384]{1,0:T(8,128)(2,1)}, f32[768,384]{1,0:T(8,128)}, f32[768,384]{1,0:T(8,128)}) custom-call(f32[384,384]{1,0:T(8,128)} %bitcast.23, bf16[768,384]{1,0:T(8,128)(2,1)} %get-tuple-element.90.high, bf16[768,384]{1,0:T(8,128)(2,1)} %get-tuple-element.91.low, ...), custom_call_target="tpu_custom_call" | custom-call | tf_op jit(solution)/shard_map/pallas_call | solution.py:685
  40.4 4.2 %all-to-all-start.1 = ((bf16[16,24,384]{2,1,0:T(8,128)(2,1)}), bf16[16,24,384]{2,1,0:T(8,128)(2,1)S(1)}, u32[]{:S(2)}, u32[]{:S(2)}) async-start(bf16[16,24,384]{2,1,0:T(8,128)(2,1)} %bitcast.31), calls=%async_computation.1 | async-start | bytes 589824 | tf_op jit(solution)/shard_map/all_to_all | solution.py:658
  44.6 0.6 reshape.166.b1
  45.2 6.3 %shard_map.320 = (bf16[768,384]{1,0:T(8,128)(2,1)}, f32[384,1536]{1,0:T(8,128)}, f32[2,384,384]{2,1,0:T(8,128)}) custom-call(bf16[2,2,180,384]{3,2,1,0:T(8,128)(2,1)} %bitcast.25, s32[768,2]{1,0:T(8,128)} %constant.71.clone.places, bf16[2,2,180,384]{3,2,1,0:T(8,128)(2,1)} %bitcast.22, f32[2,4,384]{2,1,0:T(4,128)} %all_gather.23.vectors, bf16[1536,768]{1,0:T(8,128)(2,1)} %w2_h.1), custom_call_target="tpu_custom_call" | custom-call | tf_op jit(solution)/shard_map/pallas_call | solution.py:703
  51.5 3.0 %all-to-all-done.1 = bf16[16,24,384]{2,1,0:T(8,128)(2,1)S(1)} async-done(((bf16[16,24,384]{2,1,0:T(8,128)(2,1)}), bf16[16,24,384]{2,1,0:T(8,128)(2,1)S(1)}, u32[]{:S(2)}, u32[]{:S(2)}) %all-to-all-start.1) | async-done | bytes 294944 | tf_op jit(solution)/shard_map/all_to_all | solution.py:658
  54.5 2.5 %all-gather.2 = bf16[768,384]{1,0:T(8,128)(2,1)} all-gather(bf16[384,384]{1,0:T(8,128)(2,1)S(1)} %bitcast.27), channel_id=4, replica_groups=mesh['lat'=16,'mp'=2] {'mp'}, dimensions={0}, use_global_device_ids=true | all-gather | bytes 884736 | tf_op jit(solution)/shard_map/all_gather | solution.py:724
  57.0 15.1 %shard_map.321 = (bf16[384,896]{1,0:T(8,128)(2,1)}, bf16[1,384,896]{2,1,0:T(8,128)(2,1)}, f32[1,1536]{1,0:T(1,128)}, f32[384,2]{1,0:T(8,128)}, f32[384,384]{1,0:...) custom-call(s32[32]{0:T(128)} %groups.3, ...), custom_call_target="tpu_custom_call" | custom-call | flops 4529848320 | bytes 16777216 | tf_op jit(solution)/shard_map/pallas_call | solution.py:728
  72.1 0.6 collective-permute-start.1
  72.8 0.8 collective-permute-start.2
  73.5 1.0 collective-permute-start.3
  74.6 0.6 fusion.15
  76.5 0.8 copy-done.10
  77.3 3.9 %shard_map.322 = (bf16[2,180,384]{2,1,0:T(8,128)(2,1)}, f32[384,384]{1,0:T(8,128)}, bf16[384,384]{1,0:T(8,128)(2,1)}, f32[8,384]{1,0:T(8,128)}) custom-call(s32[1]{0:T(128)S(6)} %add.103.choice, bf16[2,180,384]{2,1,0:T(8,128)(2,1)} %copy-done.1, f32[384]{0:T(512)} %gain.4, f32[384]{0:T(512)} %bias2.1, bf16[4,384,384]{2,1,0:T(8,128)(2,1)} %constant.66.clone.high.high_h, ...), custom_call_target="tpu_custom_call" | custom-call | bytes 5781504 | tf_op jit(solution)/shard_map/pallas_call | solution.py:560
  81.2 4.4 %all-to-all-start.2 = ((bf16[16,24,384]{2,1,0:T(8,128)(2,1)}), bf16[16,24,384]{2,1,0:T(8,128)(2,1)S(1)}, u32[]{:S(2)}, u32[]{:S(2)}) async-start(bf16[16,24,384]{2,1,0:T(8,128)(2,1)} %bitcast.30), calls=%async_computation.2 | async-start | bytes 589824 | tf_op jit(solution)/shard_map/all_to_all | solution.py:658
  85.6 1.9 %copy.62 = bf16[2,180,384]{2,0,1:T(2,128)(2,1)} copy(bf16[2,180,384]{2,1,0:T(8,128)(2,1)} %get-tuple-element.106) | data formatting | bytes 552960 | tf_op jit(solution)/shard_map/pallas_call | solution.py:560
  87.4 5.8 %collective-permute-done.1 = bf16[2,384,512]{2,1,0:T(8,128)(2,1)} collective-permute-done((bf16[2,384,512]{2,1,0:T(8,128)(2,1)}, bf16[2,384,512]{2,1,0:T(8,128)(2,1)}, u32[]{:S(2)}, u32[]{:S(2)}) %collective-permute-start.1) | collective-permute-done | bytes 786464 | tf_op jit(solution)/shard_map/ppermute | solution.py:580
  93.3 2.1 %add_convert_fusion.2 = (bf16[2,192,512]{2,1,0:T(8,128)(2,1)}, f32[2,192,512]{2,1,0:T(8,128)S(1)}) fusion(bf16[2,384,512]{2,1,0:T(8,128)(2,1)} %collective-permute-done.1, bf16[2,384,512]{2,1,0:T(8,128)(2,1)S(1)} %copy-done.9), kind=kLoop, calls=%fused_computation.4 | loop fusion | flops 1376256 | bytes 2752512 | tf_op jit(solution)/shard_map/convert_element_type | solution.py:585
  95.4 2.1 %add_convert_fusion.1 = (bf16[2,192,512]{2,1,0:T(8,128)(2,1)}, f32[2,192,512]{2,1,0:T(8,128)S(1)}) fusion(bf16[2,384,512]{2,1,0:T(8,128)(2,1)} %collective-permute-done.2, bf16[2,384,512]{2,1,0:T(8,128)(2,1)S(1)} %copy-done.8), kind=kLoop, calls=%fused_computation.2 | loop fusion | flops 1376256 | bytes 2752512 | tf_op jit(solution)/shard_map/convert_element_type | solution.py:585
  97.6 1.0 add_convert_fusion
  98.5 1.0 all-to-all-done.2
  99.6 1.0 collective-permute-start.4
  100.5 0.3 collective-permute-start.5
  100.9 1.3 collective-permute-start.6
  102.2 0.6 reshape.174.hidden_sums
  102.8 8.6 %shard_map.323 = bf16[16,56,384]{2,1,0:T(8,128)(2,1)} custom-call(bf16[384,384]{1,0:T(8,128)(2,1)} %bitcast.26, bf16[768,384]{1,0:T(8,128)(2,1)} %get-tuple-element.90.high, bf16[768,384]{1,0:T(8,128)(2,1)} %get-tuple-element.91.low, bf16[4,96,384]{2,1,0:T(8,128)(2,1)} %reshape.167.weights, bf16[768,384]{1,0:T(8,128)(2,1)} %get-tuple-element.117.s_ref, ...), custom_call_target="tpu_custom_call" | custom-call | bytes 6014976 | tf_op jit(solution)/shard_map/pallas_call | solution.py:547
  111.4 0.7 copy-done.12
  112.2 4.8 %all-to-all-start.3 = ((bf16[16,56,384]{2,1,0:T(8,128)(2,1)}), bf16[16,56,384]{2,1,0:T(8,128)(2,1)S(1)}, u32[]{:S(2)}, u32[]{:S(2)}) async-start(bf16[16,56,384]{2,1,0:T(8,128)(2,1)} %shard_map.323), calls=%async_computation.3 | async-start | bytes 1376256 | tf_op jit(solution)/shard_map/all_to_all | solution.py:827
  117.0 1.2 add_convert_fusion.5
  118.2 2.0 %collective-permute-start.7 = (bf16[2,96,512]{2,1,0:T(8,128)(2,1)S(1)}, bf16[2,96,512]{2,1,0:T(8,128)(2,1)S(1)}, u32[]{:S(2)}, u32[]{:S(2)}) collective-permute-start(bf16[2,96,512]{2,1,0:T(8,128)(2,1)S(1)} %get-tuple-element.175), channel_id=1, source_target_pairs={{0,8},{2,10},{4,12},{6,14},{8,0},{10,2},{12,4},{14,6},{16,24},{18,... | collective-permute-start | bytes 589832 | tf_op jit(solution)/shard_map/ppermute | solution.py:580
  120.2 0.1 add_convert_fusion.4
  120.3 1.5 collective-permute-start.8
  121.9 1.5 collective-permute-start.9
  123.5 9.2 %collective-permute-done.7 = bf16[2,96,512]{2,1,0:T(8,128)(2,1)S(1)} collective-permute-done((bf16[2,96,512]{2,1,0:T(8,128)(2,1)S(1)}, bf16[2,96,512]{2,1,0:T(8,128)(2,1)S(1)}, u32[]{:S(2)}, u32[]{:S(2)}) %collective-permute-start.7) | collective-permute-done | bytes 196640 | tf_op jit(solution)/shard_map/ppermute | solution.py:580
  132.8 0.8 all-to-all-done.3.got
  133.6 2.8 %collective-permute-start.10 = (bf16[2,48,1536]{2,1,0:T(8,128)(2,1)S(1)}, bf16[2,48,1536]{2,1,0:T(8,128)(2,1)}, u32[]{:S(2)}, u32[]{:S(2)}) collective-permute-start(bf16[2,48,1536]{2,1,0:T(8,128)(2,1)S(1)} %pad_maximum_fusion), channel_id=1, source_target_pairs={{0,16},{2,18},{4,20},{6,22},{8,24},{10,26},{12,28},{14,30},{16,0},... | collective-permute-start | bytes 884744 | tf_op jit(solution)/shard_map/ppermute | solution.py:832
  136.5 3.4 %shard_map.324 = (f32[384,384]{1,0:T(8,128)}, f32[384,3]{1,0:T(8,128)}, bf16[16,32,384]{2,1,0:T(8,128)(2,1)}) custom-call(s32[1]{0:T(128)S(6)} %add.103.choice, bf16[16,56,384]{2,1,0:T(8,128)(2,1)} %copy-done, bf16[4,384,384]{2,1,0:T(8,128)(2,1)} %constant.66.clone.high.high_h, bf16[4,384,384]{2,1,0:T(8,128)(2,1)} %constant.67.clone.low.low_h, ...), custom_call_target="tpu_custom_call" | custom-call | bytes 5217792 | tf_op jit(solution)/shard_map/pallas_call | solution.py:560
  139.9 4.2 %all-to-all-start.4 = ((bf16[16,32,384]{2,1,0:T(8,128)(2,1)}), bf16[16,32,384]{2,1,0:T(8,128)(2,1)S(1)}, u32[]{:S(2)}, u32[]{:S(2)}) async-start(bf16[16,32,384]{2,1,0:T(8,128)(2,1)} %get-tuple-element.145), calls=%async_computation.4 | async-start | bytes 786432 | tf_op jit(solution)/shard_map/all_to_all | solution.py:850
  144.0 4.6 %psum.7 = f32[384,3]{1,0:T(8,128)S(1)} all-reduce(f32[384,3]{1,0:T(8,128)} %get-tuple-element.139), channel_id=1, replica_groups=mesh['lat'=16,'mp'=2] {'mp'}, use_global_device_ids=true, to_apply=%region_4.5 | all-reduce | flops 1152 | bytes 9216 | tf_op jit(solution)/shard_map/psum | solution.py:842
  148.7 2.4 %collective-permute-done.10 = bf16[2,48,1536]{2,1,0:T(8,128)(2,1)} collective-permute-done((bf16[2,48,1536]{2,1,0:T(8,128)(2,1)S(1)}, bf16[2,48,1536]{2,1,0:T(8,128)(2,1)}, u32[]{:S(2)}, u32[]{:S(2)}) %collective-permute-start.10) | collective-permute-done | bytes 294944 | tf_op jit(solution)/shard_map/ppermute | solution.py:832
  151.1 0.4 slice_reduce_fusion.2
  151.5 0.2 multiply_add_fusion
  151.8 1.1 copy.64
  152.9 1.0 maximum_add_fusion
  153.9 0.8 slice_bitcast_fusion
  154.8 0.6 all-to-all-done.4.tail
  155.3 0.7 copy-done.5
  156.0 2.1 %shard_map.325 = (f32[384]{0:T(512)}, f32[384]{0:T(512)}, f32[2,4,96,96]{3,2,1,0:T(8,128)}, f32[2,4,96]{2,1,0:T(4,128)}, f32[2,4,96,96]{3,2,1,0:T(8,128)}, /*ind...) custom-call(bf16[16,32,384]{2,1,0:T(8,128)(2,1)} %copy-done.5), custom_call_target="tpu_custom_call" | custom-call | bytes 1003008 | tf_op jit(solution)/shard_map/pallas_call | solution.py:547
  158.1 1.3 reshape.176
  (87 shorter events, 1.2 us)
Async XLA Ops:
  7.8 8.5 %copy-start.19 = (s32[32]{0:T(128)S(1)}, s32[32]{0:T(128)}, u32[]{:S(2)}) copy-start(s32[32]{0:T(128)} %groups.3) | copy-start | bytes 388
  7.8 8.6 %copy-start.27 = (s32[32]{0:T(128)S(1)}, s32[32]{0:T(128)}, u32[]{:S(2)}) copy-start(s32[32]{0:T(128)} %param.24) | copy-start | bytes 388
  7.8 8.7 %copy-start.25 = (f32[2,4,96]{2,1,0:T(4,128)S(1)}, f32[2,4,96]{2,1,0:T(4,128)}, u32[]{:S(2)}) copy-start(f32[2,4,96]{2,1,0:T(4,128)} %param.28) | copy-start | bytes 9220
  7.8 8.8 %copy-start.26 = (f32[2,4,96]{2,1,0:T(4,128)S(1)}, f32[2,4,96]{2,1,0:T(4,128)}, u32[]{:S(2)}) copy-start(f32[2,4,96]{2,1,0:T(4,128)} %param.30) | copy-start | bytes 9220
  7.8 8.8 %copy-start.17 = (f32[384]{0:T(512)S(1)}, f32[384]{0:T(512)}, u32[]{:S(2)}) copy-start(f32[384]{0:T(512)} %gain.5) | copy-start | bytes 4612
  7.8 8.8 %copy-start.21 = (f32[384]{0:T(512)S(1)}, f32[384]{0:T(512)}, u32[]{:S(2)}) copy-start(f32[384]{0:T(512)} %gain.4) | copy-start | bytes 4612
  7.8 8.8 %copy-start.22 = (f32[384]{0:T(512)S(1)}, f32[384]{0:T(512)}, u32[]{:S(2)}) copy-start(f32[384]{0:T(512)} %bias.1) | copy-start | bytes 4612
  7.8 8.8 %copy-start.28 = (f32[384]{0:T(512)S(1)}, f32[384]{0:T(512)}, u32[]{:S(2)}) copy-start(f32[384]{0:T(512)} %param.32) | copy-start | bytes 4612
  7.9 9.7 %copy-start.14 = (bf16[2,180,384]{2,0,1:T(2,128)(2,1)S(1)}, bf16[2,180,384]{2,0,1:T(2,128)(2,1)}, u32[]{:S(2)}) copy-start(bf16[2,180,384]{2,0,1:T(2,128)(2,1)} %param.37) | copy-start | bytes 829444
  7.9 9.8 %copy-start.15 = (bf16[2,4,96,96]{3,2,1,0:T(8,128)(2,1)S(1)}, bf16[2,4,96,96]{3,2,1,0:T(8,128)(2,1)}, u32[]{:S(2)}) copy-start(bf16[2,4,96,96]{3,2,1,0:T(8,128)(2,1)} %param.29) | copy-start | bytes 442372
  7.9 9.8 %copy-start.16 = (bf16[2,4,96,96]{3,2,1,0:T(8,128)(2,1)S(1)}, bf16[2,4,96,96]{3,2,1,0:T(8,128)(2,1)}, u32[]{:S(2)}) copy-start(bf16[2,4,96,96]{3,2,1,0:T(8,128)(2,1)} %param.27) | copy-start | bytes 442372
  7.9 24.9 %all-to-all-start = ((f32[16,24,384]{2,1,0:T(8,128)}), f32[16,24,384]{2,1,0:T(8,128)S(1)}, u32[]{:S(2)}, u32[]{:S(2)}) async-start(f32[16,24,384]{2,1,0:T(8,128)} %bitcast.28), calls=%async_computation | async-start | bytes 1179648 | tf_op jit(solution)/shard_map/all_to_all | solution.py:658
  17.6 7.8 %copy-start.1 = (bf16[2,180,384]{2,1,0:T(8,128)(2,1)}, bf16[2,180,384]{2,1,0:T(8,128)(2,1)S(1)}, u32[]{:S(2)}) copy-start(bf16[2,180,384]{2,1,0:T(8,128)(2,1)S(1)} %copy.61.dy) | copy-start | bytes 829444
  32.8 0.8 copy-start.2
  33.6 11.0 %copy-start.23 = (f32[1536]{0:T(1024)S(1)}, f32[1536]{0:T(1024)}, u32[]{:S(2)}) copy-start(f32[1536]{0:T(1024)} %param.34) | copy-start | bytes 18436
  40.4 14.1 %all-to-all-start.1 = ((bf16[16,24,384]{2,1,0:T(8,128)(2,1)}), bf16[16,24,384]{2,1,0:T(8,128)(2,1)S(1)}, u32[]{:S(2)}, u32[]{:S(2)}) async-start(bf16[16,24,384]{2,1,0:T(8,128)(2,1)} %bitcast.31), calls=%async_computation.1 | async-start | bytes 589824 | tf_op jit(solution)/shard_map/all_to_all | solution.py:658
  57.0 17.5 %copy-start.20 = (s32[32]{0:T(128)S(1)}, s32[32]{0:T(128)}, u32[]{:S(2)}) copy-start(s32[32]{0:T(128)} %groups.3) | copy-start | bytes 388
  72.1 21.1 %collective-permute-start.1 = (bf16[2,384,512]{2,1,0:T(8,128)(2,1)}, bf16[2,384,512]{2,1,0:T(8,128)(2,1)}, u32[]{:S(2)}, u32[]{:S(2)}) collective-permute-start(bf16[2,384,512]{2,1,0:T(8,128)(2,1)} %get-tuple-element.111), channel_id=1, source_target_pairs={{0,2},{2,0},{4,6},{6,4},{8,10},{10,8},{12,14},{14,12},{16,18},{18,... | collective-permute-start | bytes 2359304 | tf_op jit(solution)/shard_map/ppermute | solution.py:580
  72.8 3.7 %collective-permute-start = (bf16[384,896]{1,0:T(8,128)(2,1)}, bf16[384,896]{1,0:T(8,128)(2,1)S(1)}, u32[]{:S(2)}, u32[]{:S(2)}) collective-permute-start(bf16[384,896]{1,0:T(8,128)(2,1)} %bitcast.34), channel_id=1, source_target_pairs={{0,1},{1,0},{2,3},{3,2},{4,5},{5,4},{6,7},{7,6},{8,9},{9,8},{10,11... | collective-permute-start | bytes 2064392 | tf_op jit(solution)/shard_map/ppermute | solution.py:775
  72.8 22.7 %collective-permute-start.2 = (bf16[2,384,512]{2,1,0:T(8,128)(2,1)}, bf16[2,384,512]{2,1,0:T(8,128)(2,1)}, u32[]{:S(2)}, u32[]{:S(2)}) collective-permute-start(bf16[2,384,512]{2,1,0:T(8,128)(2,1)} %get-tuple-element.113), channel_id=1, source_target_pairs={{0,4},{2,6},{4,0},{6,2},{8,12},{10,14},{12,8},{14,10},{16,20},{18,... | collective-permute-start | bytes 2359304 | tf_op jit(solution)/shard_map/ppermute | solution.py:580
  73.5 24.1 %collective-permute-start.3 = (bf16[2,384,512]{2,1,0:T(8,128)(2,1)}, bf16[2,384,512]{2,1,0:T(8,128)(2,1)S(1)}, u32[]{:S(2)}, u32[]{:S(2)}) collective-permute-start(bf16[2,384,512]{2,1,0:T(8,128)(2,1)} %get-tuple-element.115), channel_id=1, source_target_pairs={{0,8},{2,10},{4,12},{6,14},{8,0},{10,2},{12,4},{14,6},{16,24},{18,... | collective-permute-start | bytes 2359304 | tf_op jit(solution)/shard_map/ppermute | solution.py:580
  76.5 0.8 copy-start.10
  81.2 12.1 %copy-start.9 = (bf16[2,384,512]{2,1,0:T(8,128)(2,1)S(1)}, bf16[2,384,512]{2,1,0:T(8,128)(2,1)}, u32[]{:S(2)}) copy-start(bf16[2,384,512]{2,1,0:T(8,128)(2,1)} %get-tuple-element.110) | copy-start | bytes 2359300
  81.2 18.4 %all-to-all-start.2 = ((bf16[16,24,384]{2,1,0:T(8,128)(2,1)}), bf16[16,24,384]{2,1,0:T(8,128)(2,1)S(1)}, u32[]{:S(2)}, u32[]{:S(2)}) async-start(bf16[16,24,384]{2,1,0:T(8,128)(2,1)} %bitcast.30), calls=%async_computation.2 | async-start | bytes 589824 | tf_op jit(solution)/shard_map/all_to_all | solution.py:658
  93.3 2.1 %copy-start.8 = (bf16[2,384,512]{2,1,0:T(8,128)(2,1)S(1)}, bf16[2,384,512]{2,1,0:T(8,128)(2,1)}, u32[]{:S(2)}) copy-start(bf16[2,384,512]{2,1,0:T(8,128)(2,1)} %get-tuple-element.112) | copy-start | bytes 2359300
  95.4 2.2 %copy-start.7 = (bf16[2,384,512]{2,1,0:T(8,128)(2,1)S(1)}, bf16[2,384,512]{2,1,0:T(8,128)(2,1)}, u32[]{:S(2)}) copy-start(bf16[2,384,512]{2,1,0:T(8,128)(2,1)} %get-tuple-element.114) | copy-start | bytes 2359300
  97.6 4.6 %copy-start.24 = (f32[1,1536]{1,0:T(1,128)S(1)}, f32[1,1536]{1,0:T(1,128)}, u32[]{:S(2)}) copy-start(f32[1,1536]{1,0:T(1,128)} %get-tuple-element.122) | copy-start | bytes 18436
  99.5 3.2 %copy-start.6 = (bf16[16,24,384]{2,1,0:T(8,128)(2,1)}, bf16[16,24,384]{2,1,0:T(8,128)(2,1)S(1)}, u32[]{:S(2)}) copy-start(bf16[16,24,384]{2,1,0:T(8,128)(2,1)S(1)} %all-to-all-done.2) | copy-start | bytes 884740
  99.6 11.8 %collective-permute-start.4 = (bf16[2,192,512]{2,1,0:T(8,128)(2,1)}, bf16[2,192,512]{2,1,0:T(8,128)(2,1)}, u32[]{:S(2)}, u32[]{:S(2)}) collective-permute-start(bf16[2,192,512]{2,1,0:T(8,128)(2,1)} %get-tuple-element.124), channel_id=1, source_target_pairs={{0,4},{2,6},{4,0},{6,2},{8,12},{10,14},{12,8},{14,10},{16,20},{18,... | collective-permute-start | bytes 1179656 | tf_op jit(solution)/shard_map/ppermute | solution.py:580
  100.5 10.9 %collective-permute-start.5 = (bf16[2,192,512]{2,1,0:T(8,128)(2,1)}, bf16[2,192,512]{2,1,0:T(8,128)(2,1)S(1)}, u32[]{:S(2)}, u32[]{:S(2)}) collective-permute-start(bf16[2,192,512]{2,1,0:T(8,128)(2,1)} %get-tuple-element.126), channel_id=1, source_target_pairs={{0,8},{2,10},{4,12},{6,14},{8,0},{10,2},{12,4},{14,6},{16,24},{18,... | collective-permute-start | bytes 1179656 | tf_op jit(solution)/shard_map/ppermute | solution.py:580
  100.9 10.6 %collective-permute-start.6 = (bf16[2,192,512]{2,1,0:T(8,128)(2,1)}, bf16[2,192,512]{2,1,0:T(8,128)(2,1)S(1)}, u32[]{:S(2)}, u32[]{:S(2)}) collective-permute-start(bf16[2,192,512]{2,1,0:T(8,128)(2,1)} %get-tuple-element.128), channel_id=1, source_target_pairs={{0,2},{2,0},{4,6},{6,4},{8,10},{10,8},{12,14},{14,12},{16,18},{18,... | collective-permute-start | bytes 1179656 | tf_op jit(solution)/shard_map/ppermute | solution.py:580
  111.4 0.7 copy-start.12
  112.2 21.5 %all-to-all-start.3 = ((bf16[16,56,384]{2,1,0:T(8,128)(2,1)}), bf16[16,56,384]{2,1,0:T(8,128)(2,1)S(1)}, u32[]{:S(2)}, u32[]{:S(2)}) async-start(bf16[16,56,384]{2,1,0:T(8,128)(2,1)} %shard_map.323), calls=%async_computation.3 | async-start | bytes 1376256 | tf_op jit(solution)/shard_map/all_to_all | solution.py:827
  117.0 3.2 %copy-start.13 = (bf16[2,192,512]{2,1,0:T(8,128)(2,1)S(1)}, bf16[2,192,512]{2,1,0:T(8,128)(2,1)}, u32[]{:S(2)}) copy-start(bf16[2,192,512]{2,1,0:T(8,128)(2,1)} %copy-done.12) | copy-start | bytes 1179652
  118.2 14.4 %collective-permute-start.7 = (bf16[2,96,512]{2,1,0:T(8,128)(2,1)S(1)}, bf16[2,96,512]{2,1,0:T(8,128)(2,1)S(1)}, u32[]{:S(2)}, u32[]{:S(2)}) collective-permute-start(bf16[2,96,512]{2,1,0:T(8,128)(2,1)S(1)} %get-tuple-element.175), channel_id=1, source_target_pairs={{0,8},{2,10},{4,12},{6,14},{8,0},{10,2},{12,4},{14,6},{16,24},{18,... | collective-permute-start | bytes 589832 | tf_op jit(solution)/shard_map/ppermute | solution.py:580
  120.3 12.4 %collective-permute-start.8 = (bf16[2,96,512]{2,1,0:T(8,128)(2,1)S(1)}, bf16[2,96,512]{2,1,0:T(8,128)(2,1)S(1)}, u32[]{:S(2)}, u32[]{:S(2)}) collective-permute-start(bf16[2,96,512]{2,1,0:T(8,128)(2,1)S(1)} %get-tuple-element.173), channel_id=1, source_target_pairs={{0,2},{2,0},{4,6},{6,4},{8,10},{10,8},{12,14},{14,12},{16,18},{18,... | collective-permute-start | bytes 589832 | tf_op jit(solution)/shard_map/ppermute | solution.py:580
  121.9 10.8 %collective-permute-start.9 = (bf16[2,96,512]{2,1,0:T(8,128)(2,1)S(1)}, bf16[2,96,512]{2,1,0:T(8,128)(2,1)S(1)}, u32[]{:S(2)}, u32[]{:S(2)}) collective-permute-start(bf16[2,96,512]{2,1,0:T(8,128)(2,1)S(1)} %get-tuple-element.171), channel_id=1, source_target_pairs={{0,4},{2,6},{4,0},{6,2},{8,12},{10,14},{12,8},{14,10},{16,20},{18,... | collective-permute-start | bytes 589832 | tf_op jit(solution)/shard_map/ppermute | solution.py:580
  133.6 2.9 %copy-start = (bf16[16,56,384]{2,1,0:T(8,128)(2,1)}, bf16[16,56,384]{2,1,0:T(8,128)(2,1)S(1)}, u32[]{:S(2)}) copy-start(bf16[16,56,384]{2,1,0:T(8,128)(2,1)S(1)} %all-to-all-done.3.got) | copy-start | bytes 2064388
  133.6 17.5 %collective-permute-start.10 = (bf16[2,48,1536]{2,1,0:T(8,128)(2,1)S(1)}, bf16[2,48,1536]{2,1,0:T(8,128)(2,1)}, u32[]{:S(2)}, u32[]{:S(2)}) collective-permute-start(bf16[2,48,1536]{2,1,0:T(8,128)(2,1)S(1)} %pad_maximum_fusion), channel_id=1, source_target_pairs={{0,16},{2,18},{4,20},{6,22},{8,24},{10,26},{12,28},{14,30},{16,0},... | collective-permute-start | bytes 884744 | tf_op jit(solution)/shard_map/ppermute | solution.py:832
  139.9 11.6 %copy-start.3 = (f32[384,384]{1,0:T(8,128)S(1)}, f32[384,384]{1,0:T(8,128)}, u32[]{:S(2)}) copy-start(f32[384,384]{1,0:T(8,128)} %get-tuple-element.137.xh) | copy-start | bytes 1769476
  139.9 11.6 %copy-start.4 = (f32[384,384]{1,0:T(8,128)S(1)}, f32[384,384]{1,0:T(8,128)}, u32[]{:S(2)}) copy-start(f32[384,384]{1,0:T(8,128)} %get-tuple-element.108.dx1) | copy-start | bytes 1769476
  139.9 11.6 %copy-start.11 = (f32[384,384]{1,0:T(8,128)S(1)}, f32[384,384]{1,0:T(8,128)}, u32[]{:S(2)}) copy-start(f32[384,384]{1,0:T(8,128)} %get-tuple-element.144) | copy-start | bytes 1769476
  139.9 11.6 %copy-start.18 = (f32[384]{0:T(512)S(1)}, f32[384]{0:T(512)}, u32[]{:S(2)}) copy-start(f32[384]{0:T(512)} %gain.5) | copy-start | bytes 4612
  139.9 15.4 %all-to-all-start.4 = ((bf16[16,32,384]{2,1,0:T(8,128)(2,1)}), bf16[16,32,384]{2,1,0:T(8,128)(2,1)S(1)}, u32[]{:S(2)}, u32[]{:S(2)}) async-start(bf16[16,32,384]{2,1,0:T(8,128)(2,1)} %get-tuple-element.145), calls=%async_computation.4 | async-start | bytes 786432 | tf_op jit(solution)/shard_map/all_to_all | solution.py:850
  155.3 0.7 copy-start.5

commit v4 on v3

--- a/solution.py
+++ b/solution.py
@@ -114,12 +114,16 @@
 
 def times(pair, values):
     high, low = split_in(values)
-    return mm(pair[0], high) + mm(pair[1], high) + mm(pair[0], low)
+    width = values.shape[1]
+    both = mm(pair[0], jnp.concatenate([high, low], axis=1))
+    return both[:, :width] + both[:, width:] + mm(pair[1], high)
 
 
 def times_t(pair, values):
     high, low = split_in(values)
-    return mm_t(pair[0], high) + mm_t(pair[1], high) + mm_t(pair[0], low)
+    width = values.shape[1]
+    both = mm_t(pair[0], jnp.concatenate([high, low], axis=1))
+    return both[:, :width] + both[:, width:] + mm_t(pair[1], high)
 
 
 def gelu_pair(v):
@@ -224,38 +228,41 @@
             copy.wait()
 
 
+def complex_blocks(real, imag, blocks, size):
+    real, imag = diagonal(real, blocks, size), diagonal(imag, blocks, size)
+    return jnp.concatenate(
+        [jnp.concatenate([real, imag], axis=1), jnp.concatenate([-imag, real], axis=1)], axis=0
+    )
+
+
+def side_by_side(values):
+    half = values.shape[0] // 2
+    return jnp.concatenate([values[:half], values[half:]], axis=1)
+
+
+def one_below(values):
+    half = values.shape[1] // 2
+    return jnp.concatenate([values[:, :half], values[:, half:]], axis=0)
+
+
 def filter_kernel(blocks, size, z, high, low, weights, biases, eo, s_h, h_h, slope_h, gate_h, s_s, h_s, slope_s, gate_s, sems):
     move = Mover(sems)
-    w1r, w1i, w2r, w2i = (diagonal(weights[i], blocks, size) for i in range(4))
-    n = z.shape[0]
-    s = times((high[...], low[...]), z[...]).astype(BF)
+    first = complex_blocks(weights[0], weights[1], blocks, size)
+    second = complex_blocks(weights[2], weights[3], blocks, size)
+    s = side_by_side(times((high[...], low[...]), z[...]).astype(BF))
     s_s[...] = s
     move.store(s_s, s_h)
-    sr, si = s[:n], s[n:]
-    a1r = mm(sr, w1r) - mm(si, w1i) + biases[0:1, :]
-    a1i = mm(sr, w1i) + mm(si, w1r) + biases[1:2, :]
-    hr, slope = gelu_pair(a1r)
-    hr = hr.astype(BF)
-    slope_s[:n, :] = slope
-    hi, slope = gelu_pair(a1i)
-    hi = hi.astype(BF)
-    slope_s[n:, :] = slope
+    h, slope = gelu_pair(mm(s, first) + biases[0:1, :])
+    h = h.astype(BF)
+    slope_s[...] = slope
     move.store(slope_s, slope_h)
-    h_s[:n, :] = hr
-    h_s[n:, :] = hi
+    h_s[...] = h
     move.store(h_s, h_h)
-    a2r = mm(hr, w2r) - mm(hi, w2i) + biases[2:3, :]
-    a2i = mm(hr, w2i) + mm(hi, w2r) + biases[3:4, :]
-    tr = jnp.tanh(a2r * (1.0 / SHRINK))
-    ti = jnp.tanh(a2i * (1.0 / SHRINK))
-    gate_s[:n, :] = tr * tr
-    gate_s[n:, :] = ti * ti
+    a2 = mm(h, second) + biases[1:2, :]
+    tanh = jnp.tanh(a2 * (1.0 / SHRINK))
+    gate_s[...] = tanh * tanh
     move.store(gate_s, gate_h)
-    rh, rl = split_in(a2r - SHRINK * tr)
-    ih, il = split_in(a2i - SHRINK * ti)
-    out = mm_t(high[:n, :], rh) + mm_t(low[:n, :], rh) + mm_t(high[:n, :], rl)
-    out += mm_t(high[n:, :], ih) + mm_t(low[n:, :], ih) + mm_t(high[n:, :], il)
-    eo[...] = out.astype(BF)
+    eo[...] = times_t((high[...], low[...]), one_below(a2 - SHRINK * tanh)).astype(BF)
     move.finish()
 
 
@@ -338,8 +345,10 @@
         )
     load_w2 = move.start(w2_h, w2)
     load_dyt = move.start(dyt_h, dyt)
+    every = jnp.concatenate([eo[m] for m in range(mp)], axis=1)
+    filtered = mm_t(table[0], every) + mm_t(table[1], every)
     for m in range(mp):
-        base[m] = base[m] + mm_t(table[0], eo[m]) + mm_t(table[1], eo[m])
+        base[m] = base[m] + filtered[:, m * ch : (m + 1) * ch]
     move.store(base.at[mine], own_h)
     average, inv = second_norm([base[m] for m in range(mp)])
     spot = lax.broadcasted_iota(jnp.int32, norm_out.shape, 1)
@@ -416,7 +425,8 @@
 
 def back_mix_kernel(columns, padded, width, choice, dy, gain, bias2, high, low, norm_in, own, *refs):
     got, (out_field, dx1, freq, sums, pad) = refs[:-5], refs[-5:]
-    ch, rows_dev = own.shape[1], dy.shape[0]
+    ch, rows_dev = own.shape[1], dy.shape[1]
+    mine = lax.axis_index("mp")
     x1 = own[...]
     average, inv = norm_in[:, 0:1], norm_in[:, 1:2]
     hat = (x1 - average) * inv
@@ -426,7 +436,7 @@
     pad[...] = jnp.zeros_like(pad)
     for r in range(rows_dev):
         out_field[r] = out[r * padded : r * padded + columns, :].astype(BF)
-        put_rows(pad, dy[r].astype(F32), r, padded)
+        put_rows(pad, dy[mine, r].astype(F32), r, padded)
     grad = pad[...]
     sums[0:1, :] = column_sum(dn * hat)
     sums[1:2, :] = column_sum(dn)
@@ -441,35 +451,30 @@
 
 
 def filter_back_kernel(blocks, size, group, dz, high, low, weights, s_ref, h_ref, slope_ref, gate_ref, mlp_sums, hidden_sums, send, rows, grads_s, sums_s):
-    w1r, w1i, w2r, w2i = (diagonal(weights[i], blocks, size) for i in range(4))
-    n = dz.shape[0]
+    first = complex_blocks(weights[0], weights[1], blocks, size)
+    second = complex_blocks(weights[2], weights[3], blocks, size)
+    ch = dz.shape[1]
     dsh = mm(high[...], dz[...]) + mm(low[...], dz[...])
-    da = dsh * gate_ref[...]
-    dar, dai = da[:n].astype(BF), da[n:].astype(BF)
-    hr, hi = h_ref[:n, :], h_ref[n:, :]
-    dcr = ((mm_nt(dar, w2r) + mm_nt(dai, w2i)) * slope_ref[:n, :]).astype(BF)
-    dci = ((mm_nt(dai, w2r) - mm_nt(dar, w2i)) * slope_ref[n:, :]).astype(BF)
-    rh, rl = split_in(mm_nt(dcr, w1r) + mm_nt(dci, w1i))
-    ih, il = split_in(mm_nt(dci, w1r) - mm_nt(dcr, w1i))
-    out = mm_t(high[:n, :], rh) + mm_t(low[:n, :], rh) + mm_t(high[:n, :], rl)
-    out += mm_t(high[n:, :], ih) + mm_t(low[n:, :], ih) + mm_t(high[n:, :], il)
+    da = (side_by_side(dsh) * gate_ref[...]).astype(BF)
+    dc = (mm_nt(da, second) * slope_ref[...]).astype(BF)
+    out = times_t((high[...], low[...]), one_below(mm_nt(dc, first)))
     parts = rows.shape[0]
     for d in range(parts):
         rows[d, :group, :] = out[d * group : (d + 1) * group, :]
-    sr, si = s_ref[:n, :], s_ref[n:, :]
-    grads = (
-        mm_t(sr, dcr) + mm_t(si, dci),
-        mm_t(sr, dci) - mm_t(si, dcr),
-        mm_t(hr, dar) + mm_t(hi, dai),
-        mm_t(hr, dai) - mm_t(hi, dar),
-    )
-    for i, grad in enumerate(grads):
-        grads_s[i * size : (i + 1) * size, :] = gather_blocks(grad, blocks, size)
+    for i, (left, right) in enumerate(((s_ref, dc), (h_ref, da))):
+        outer = mm_t(left[...], right)
+        pair = (outer[:ch, :ch] + outer[ch:, ch:], outer[:ch, ch:] - outer[ch:, :ch])
+        for k, grad in enumerate(pair):
+            at = (2 * i + k) * size
+            grads_s[at : at + size, :] = gather_blocks(grad, blocks, size)
     sums_s[...] = jnp.zeros_like(sums_s)
-    for i, grad in enumerate((dcr, dci, dar, dai)):
-        sums_s[i : i + 1, :] = column_sum(grad.astype(F32))
+    for i, grad in enumerate((dc, da)):
+        total = column_sum(grad.astype(F32))
+        sums_s[2 * i : 2 * i + 1, :] = total[:, :ch]
+        sums_s[2 * i + 1 : 2 * i + 2, :] = total[:, ch:]
     sums_s[4:7, :] = mlp_sums[0:3, :]
-    sums_s[7 : 7 + hidden_sums.shape[0], :] = hidden_sums[...]
+    for i in range(hidden_sums.shape[1] // ch):
+        sums_s[7 + i : 8 + i, :] = hidden_sums[:, i * ch : (i + 1) * ch]
     share = grads_s.shape[0] // parts
     at = group + share
     for d in range(parts):
@@ -527,8 +532,13 @@
     n2g[...] = pair(4, 0)[0]
     n2b[...] = pair(5, 0)[0]
     gb2[...] = pair(6, 0)[0]
-    for i in range(gb1.shape[0]):
-        gb1[i : i + 1, :] = pair(7 + i, 0)
+    ch = tail.shape[2]
+    for i in range(math.prod(gb1.shape) // ch):
+        row = pair(7 + i, 0)
+        if gb1.ndim == 1:
+            gb1[i * ch : (i + 1) * ch] = row[0]
+        else:
+            gb1[i : i + 1, :] = row
     n1g[...] = sum(pair(d, 1) for d in range(parts))[0]
     n1b[...] = sum(pair(d, 2) for d in range(parts))[0]
 
@@ -580,18 +590,16 @@
     return lax.ppermute(away, "lat", [(d, d ^ bit) for d in range(parts)])
 
 
-def folded(kept, got):
-    half = kept.shape[1] // 2
-    away = (kept[:, half:].astype(F32) + got[:, half:].astype(F32)).astype(BF)
-    return kept[:, :half].astype(F32) + got[:, :half].astype(F32), away
-
-
-def halve(kept, away, bit, parts):
-    return folded(kept, swapped(away, bit, parts))
-
-
-def tied(value, states):
-    return lax.optimization_barrier((value, states))
+def added(terms, first, end):
+    return sum(t[:, first:end].astype(F32) for t in terms)
+
+
+def later(value, arrays):
+    return lax.optimization_barrier((value, arrays))[0]
+
+
+def together(value, arrays):
+    return lax.optimization_barrier((value, arrays))
 
 
 def body(
@@ -674,13 +682,13 @@
         ],
     )
     spec = jnp.stack([spec_w1, spec_w2]).transpose(0, 1, 3, 2, 4).reshape(4, size, ch)
-    spec_bias = jnp.concatenate([spec_b1.reshape(2, ch), spec_b2.reshape(2, ch)], axis=0)
+    spec_bias = jnp.concatenate([spec_b1.reshape(1, 2 * ch), spec_b2.reshape(1, 2 * ch)], axis=0)
     vectors = jnp.concatenate([norm1_gain, norm1_bias, norm2_gain, norm2_bias]).reshape(4, ch)
     vectors_all = lax.all_gather(vectors, "mp", axis=0)
     dy_all = lax.all_gather(cotangent, "mp", axis=0)
     z, vectors_all, dy_all = lax.optimization_barrier((z, vectors_all, dy_all))
 
-    saved = [bf(2 * patches, ch), bf(2 * patches, ch), f32(2 * patches, ch), f32(2 * patches, ch)]
+    saved = [bf(patches, 2 * ch), bf(patches, 2 * ch), f32(patches, 2 * ch), f32(patches, 2 * ch)]
     vmem, hbm = pl.BlockSpec(memory_space=pltpu.VMEM), pl.BlockSpec(memory_space=pl.ANY)
     eo, s, h, slope, gate = pl.pallas_call(
         functools.partial(filter_kernel, blocks, size),
@@ -776,22 +784,20 @@
         for i in range(1, mp)
     ]
 
-    def exchange(states, turn):
-        return [halve(*state, order[turn], parts) for state, order in zip(states, orders)]
-
-    def received(states, turn):
-        return [
-            (kept, swapped(away, order[turn], parts)) for (kept, away), order in zip(states, orders)
-        ]
-
-    states = [(grads[2 * p], grads[2 * p + 1]) for p in range(pieces)]
-    states = exchange(states, 0)
+    def exchanged(away, turn):
+        return [swapped(a, order[turn], parts) for a, order in zip(away, orders)]
+
+    rows_each = full_width // 4
+    streams = [[kept] for kept in grads[0::2]]
+    got_rows = exchanged(grads[1::2], 0)
+    streams = [[*terms, part] for terms, part in zip(streams, got_rows)]
+    away = [added(terms, rows_each, 2 * rows_each).astype(BF) for terms in streams]
 
     out_field, dx1, dfreq, sums2 = run(
         functools.partial(back_mix_kernel, columns, padded, full_width),
         [bf(rows_dev, columns, ch), f32(tokens, ch), bf(patches, ch), f32(8, ch)],
         [
-            cotangent,
+            dy_all,
             norm2_gain,
             fc2_bias,
             *lon,
@@ -806,30 +812,39 @@
     )
 
     dz = to_other(dfreq, group).reshape(patches, ch)
-    dz, out_field = lax.optimization_barrier(
-        (dz, with_layout_constraint(out_field, Layout(major_to_minor=(1, 0, 2))))
-    )
-    dz, states = tied(dz, states)
+    dz = later(dz, away)
+    got_rows = exchanged(away, 1)
     spec_rows = 4 * size // parts
     send_rows = -(-(group + spec_rows + 2) // 8) * 8
     (sent,) = run(
         functools.partial(filter_back_kernel, blocks, size, group),
         [bf(parts, send_rows, ch)],
-        [dz, *lat, spec, s, h, slope, gate, sums2, g_fc1_bias.reshape(-1, ch)],
+        [dz, *lat, spec, s, h, slope, gate, sums2, g_fc1_bias],
         [
             pltpu.VMEM((parts, send_rows, ch), F32),
             pltpu.VMEM((4 * size, ch), F32),
             pltpu.VMEM((max(parts, 16), ch), F32),
         ],
     )
-    sent, states = tied(sent, received(states, 1))
-    states = exchange([folded(*state) for state in states], 2)
+    sent, got_rows, out_field = lax.optimization_barrier((sent, got_rows, out_field))
+    out_field = with_layout_constraint(out_field, Layout(major_to_minor=(1, 0, 2)))
+    streams = [[*terms, part] for terms, part in zip(streams, got_rows)]
+    half = rows_each // 2
+    kept = [added(terms, 0, half) for terms in streams]
+    got_rows = exchanged([added(terms, half, rows_each).astype(BF) for terms in streams], 2)
+    quarter = half // 2
+    pairs = list(zip(kept, got_rows))
+    away = [added(pair, quarter, half).astype(BF) for pair in pairs]
+    kept = [added(pair, 0, quarter) for pair in pairs]
     sent = lax.all_to_all(sent, "lat", 0, 0, tiled=True)
-    sent, states = tied(sent, states)
-    kept, away = (jnp.concatenate([state[i] for state in states], axis=2) for i in range(2))
+    sent, out_field = together(sent, out_field)
+    sent, kept, away = lax.optimization_barrier((sent, kept, away))
+    kept, away = (jnp.concatenate(arrays, axis=2) for arrays in (kept, away))
     for bit in bits[3:-1]:
-        kept, away = halve(kept, away, bit, parts)
-    got_last = lax.ppermute(away, "lat", [(d, d ^ bits[-1]) for d in range(parts)])
+        pair = (kept, swapped(away, bit, parts))
+        quarter //= 2
+        kept, away = added(pair, 0, quarter), added(pair, quarter, 2 * quarter).astype(BF)
+    got_last = swapped(away, bits[-1], parts)
     tail_rows = -(-(spec_rows + 6) // 16) * 16
     du, stat1, tail = run(
         functools.partial(back_norm_kernel, group, spec_rows, mp),
@@ -840,7 +855,7 @@
         choice,
     )
     stat1 = lax.psum(stat1, "mp")
-    stat1, got_last = lax.optimization_barrier((stat1, got_last))
+    stat1, got_last = together(stat1, got_last)
     weights = kept + got_last.astype(F32)
     grad_field = dx1 + stat1[:, 2:] * (
         du * norm1_gain - (stat1[:, :1] + xh1 * stat1[:, 1:2]) * (1.0 / full_width)
@@ -848,10 +863,11 @@
     grad_field = grad_field.reshape(rows_dev, padded, ch)[:, :columns]
 
     tail = lax.all_to_all(tail, "lat", 0, 0, tiled=True)
+    hidden_bias = f32(hidden) if ch % 128 == 0 else f32(hidden // ch, ch)
     vector, weight, bias = f32(ch), f32(2, blocks, size, size), f32(2, blocks, size)
     g_n1g, g_n1b, g_w1, g_b1, g_w2, g_b2, g_n2g, g_n2b, g_fc1b, g_fc2b = run(
         functools.partial(close_kernel, spec_rows, blocks, size),
-        [vector, vector, weight, bias, weight, bias, vector, vector, f32(hidden // ch, ch), vector],
+        [vector, vector, weight, bias, weight, bias, vector, vector, hidden_bias, vector],
         [tail],
         [pltpu.VMEM((4 * size, ch), F32)],
     )

time: 161 us -> 156 us (0.969)
  local copies, waits for them, and re-layouts: 13.9 us -> 11 us
  other arithmetic: 10.2 us -> 12.2 us
  Pallas kernels: 52.4 us -> 50.6 us
    ppermute x9 -> x10, waiting for transfers between devices: 15 us -> 19.2 us  [swapped(): return lax.ppermute(away, 'lat', [(d, d ^ bit) for d in range(parts)])]
    ppermute x1 -> x0, starting transfers between devices: 2.84 us -> none  [body(): lax.ppermute(away, 'lat', [(d, d ^ bits[-1]) for d in range(parts)])]
    ppermute x1 -> x0, waiting for transfers between devices: 2.45 us -> none  [body(): lax.ppermute(away, 'lat', [(d, d ^ bits[-1]) for d in range(parts)])]
    ppermute x9 -> x10, starting transfers between devices: 10 us -> 12.2 us  [swapped(): return lax.ppermute(away, 'lat', [(d, d ^ bit) for d in range(parts)])]
    convert_element_type x9, other arithmetic: 6.8 us -> 8.77 us  [the longest x3 4.52 us: body(): added(terms, rows_each, 2 * rows_each).astype(BF)]
    reshape x4 -> x2, local copies, waits for them, and re-layouts: 2.07 us -> 0.16 us  [the longest x1 0.08 us: body(): spec_b1.reshape(1, 2 * ch)]
    pallas_call x1 -> x0, local copies, waits for them, and re-layouts: 1.88 us -> none  [run(): pl.pallas_call(kernel, out_shape=out_shape, grid_spec=pltpu.PrefetchScala...]
    unnamed x61 -> x57, local copies, waits for them, and re-layouts: 5.37 us -> 5.34 us
  transfers between devices with their start and end apart: 16 -> 16, of which waited for: 8 -> 7; matrix products, arithmetic and copies ran while one was open for 12% -> 12% of each run, Pallas kernels for 16% -> 15%
where the time goes in v4:
time: 156 us; the launch traced here: 155 us
  Pallas kernels  50.6 us (32%)
  starting transfers between devices  37.2 us (24%)
  waiting for transfers between devices  28 us (18%)
  blocking collectives  13.8 us (9%)
  other arithmetic  12.2 us (8%)
  local copies, waits for them, and re-layouts  11 us (7%)
  between operations  2.45 us (2%)
    ppermute x10, waiting for transfers between devices, swapped(): return lax.ppermute(away, 'lat', [(d, d ^ bit) for d in range(parts)])  19.2 us
    all_to_all x3, starting transfers between devices, to_other(): lax.all_to_all(values.reshape(parts, rows_each, ch), 'lat', 0, 0, tiled=T...  17 us
    pallas_call x1, Pallas kernels, body(): pl.pallas_call(functools.partial(mlp_kernel, orders, rows_dev), out_shape...  15.4 us
    ppermute x10, starting transfers between devices, swapped(): return lax.ppermute(away, 'lat', [(d, d ^ bit) for d in range(parts)])  12.2 us
    pallas_call x3, Pallas kernels, run(): pl.pallas_call(kernel, out_shape=out_shape, in_specs=[pl.BlockSpec(memory...  12 us
    all_to_all x3, waiting for transfers between devices, to_other(): lax.all_to_all(values.reshape(parts, rows_each, ch), 'lat', 0, 0, tiled=T...  8.02 us
    pallas_call x2, Pallas kernels, run(): pl.pallas_call(kernel, out_shape=out_shape, grid_spec=pltpu.PrefetchScala...  7.31 us
    pallas_call x1, Pallas kernels, body(): pl.pallas_call(functools.partial(cotangent_kernel, columns, padded), out_...  6.3 us
  transfers between devices with their start and end apart: 16, of which 7 were waited for; matrix products, arithmetic and copies ran while one was open for 12% of the time, Pallas kernels for 15%

profile of v4, /device:TPU:0, one launch (start us, length us, event | category | flops | bytes accessed | tf_op | source)
XLA Modules:
  0.0 155.2 jit_solution(4492775322125240988)
XLA Ops:
  0.6 1.0 copy.53
  1.6 2.4 %all-gather = bf16[4,180,384]{2,1,0:T(8,128)(2,1)} all-gather(bf16[2,180,384]{2,1,0:T(8,128)(2,1)S(1)} %copy.53), channel_id=2, replica_groups=mesh['lat'=16,'mp'=2] {'mp'}, dimensions={0}, use_global_device_ids=true | all-gather | bytes 829440 | tf_op jit(solution)/shard_map/all_gather | solution.py:648
  4.1 3.6 %shard_map.317 = (f32[384,384]{1,0:T(8,128)}, f32[384,384]{1,0:T(8,128)}, f32[384,1]{1,0:T(8,128)}) custom-call(s32[32]{0:T(128)} %groups.3, bf16[2,2,180,384]{3,2,1,0:T(8,128)(2,1)} %bitcast.21, f32[384]{0:T(512)} %gain.5, f32[384]{0:T(512)} %bias.1, bf16[4,384,384]{2,1,0:T(8,128)(2,1)} %constant.66.clone.high.high_h, ...), custom_call_target="tpu_custom_call" | custom-call | tf_op jit(solution)/shard_map/pallas_call | solution.py:650
  7.8 8.4 %all-to-all-start = ((f32[16,24,384]{2,1,0:T(8,128)}), f32[16,24,384]{2,1,0:T(8,128)S(1)}, u32[]{:S(2)}, u32[]{:S(2)}) async-start(f32[16,24,384]{2,1,0:T(8,128)} %bitcast.29), calls=%async_computation | async-start | bytes 1179648 | tf_op jit(solution)/shard_map/all_to_all | solution.py:666
  16.3 0.1 fusion.11
  16.7 0.1 copy.55
  16.8 0.7 sub.27.keep
  17.7 0.2 copy.57
  17.9 1.0 reshape.161.weights
  19.0 0.2 fusion.3
  19.2 0.3 select_multiply_fusion.1
  19.5 0.7 pad_maximum_fusion.1.tables
  20.2 2.6 %shard_map.318 = (bf16[768,384]{1,0:T(8,128)(2,1)}, bf16[768,384]{1,0:T(8,128)(2,1)}) custom-call(f32[32,64]{1,0:T(8,128)} %pad_maximum_fusion.1.tables, bf16[192,32]{1,0:T(8,128)(2,1)} %constant.68.clone.left, bf16[4,64,384]{2,1,0:T(8,128)(2,1)} %constant.69.clone.right, bf16[192,384]{1,0:T(8,128)(2,1)} %constant.70.clone.same, f32[192,1]{1,0:T(8,128)} %sub.27.keep), custom_call_target="tpu_custom_call" | custom-call | bytes 1544960 | tf_op jit(solution)/shard_map/pallas_call | solution.py:557
  22.8 1.9 %all_gather.23.vectors = f32[2,4,384]{2,1,0:T(4,128)} all-gather(f32[1,4,384]{2,1,0:T(4,128)S(1)} %all_gather_reshape.3), channel_id=1, replica_groups=mesh['lat'=16,'mp'=2] {'mp'}, dimensions={0}, use_global_device_ids=true | all-gather | bytes 18432 | tf_op jit(solution)/shard_map/all_gather | solution.py:687
  24.7 0.6 pad_maximum_fusion.3.biases
  25.4 2.3 %all-gather.1 = bf16[4,180,384]{2,1,0:T(8,128)(2,1)} all-gather(bf16[2,180,384]{2,1,0:T(8,128)(2,1)S(1)} %copy.54), channel_id=3, replica_groups=mesh['lat'=16,'mp'=2] {'mp'}, dimensions={0}, use_global_device_ids=true | all-gather | bytes 829440 | tf_op jit(solution)/shard_map/all_gather | solution.py:688
  27.7 5.1 %all-to-all-done = f32[16,24,384]{2,1,0:T(8,128)S(1)} async-done(((f32[16,24,384]{2,1,0:T(8,128)}), f32[16,24,384]{2,1,0:T(8,128)S(1)}, u32[]{:S(2)}, u32[]{:S(2)}) %all-to-all-start) | async-done | bytes 589856 | tf_op jit(solution)/shard_map/all_to_all | solution.py:666
  32.8 0.8 copy-done.1
  33.6 6.0 %shard_map.319 = (bf16[384,384]{1,0:T(8,128)(2,1)}, bf16[384,768]{1,0:T(8,128)(2,1)}, bf16[384,768]{1,0:T(8,128)(2,1)}, f32[384,768]{1,0:T(8,128)}, f32[384,768]{1,0:T(8,128)}) custom-call(f32[384,384]{1,0:T(8,128)} %bitcast.25, bf16[768,384]{1,0:T(8,128)(2,1)} %get-tuple-element.83.high, bf16[768,384]{1,0:T(8,128)(2,1)} %get-tuple-element.84.low, ...), custom_call_target="tpu_custom_call" | custom-call | tf_op jit(solution)/shard_map/pallas_call | solution.py:693
  39.6 4.2 %all-to-all-start.1 = ((bf16[16,24,384]{2,1,0:T(8,128)(2,1)}), bf16[16,24,384]{2,1,0:T(8,128)(2,1)S(1)}, u32[]{:S(2)}, u32[]{:S(2)}) async-start(bf16[16,24,384]{2,1,0:T(8,128)(2,1)} %bitcast.32), calls=%async_computation.1 | async-start | bytes 589824 | tf_op jit(solution)/shard_map/all_to_all | solution.py:666
  43.8 0.6 reshape.160.b1
  44.4 6.3 %shard_map.320 = (bf16[768,384]{1,0:T(8,128)(2,1)}, f32[384,1536]{1,0:T(8,128)}, f32[2,384,384]{2,1,0:T(8,128)}) custom-call(bf16[2,2,180,384]{3,2,1,0:T(8,128)(2,1)} %bitcast.23, s32[768,2]{1,0:T(8,128)} %constant.71.clone.places, bf16[2,2,180,384]{3,2,1,0:T(8,128)(2,1)} %bitcast.22, f32[2,4,384]{2,1,0:T(4,128)} %all_gather.23.vectors, bf16[1536,768]{1,0:T(8,128)(2,1)} %w2_h.1), custom_call_target="tpu_custom_call" | custom-call | tf_op jit(solution)/shard_map/pallas_call | solution.py:711
  50.7 2.9 %all-to-all-done.1 = bf16[16,24,384]{2,1,0:T(8,128)(2,1)S(1)} async-done(((bf16[16,24,384]{2,1,0:T(8,128)(2,1)}), bf16[16,24,384]{2,1,0:T(8,128)(2,1)S(1)}, u32[]{:S(2)}, u32[]{:S(2)}) %all-to-all-start.1) | async-done | bytes 294944 | tf_op jit(solution)/shard_map/all_to_all | solution.py:666
  53.6 2.5 %all-gather.2 = bf16[768,384]{1,0:T(8,128)(2,1)} all-gather(bf16[384,384]{1,0:T(8,128)(2,1)S(1)} %bitcast.28), channel_id=4, replica_groups=mesh['lat'=16,'mp'=2] {'mp'}, dimensions={0}, use_global_device_ids=true | all-gather | bytes 884736 | tf_op jit(solution)/shard_map/all_gather | solution.py:732
  56.2 15.4 %shard_map.321 = (bf16[384,896]{1,0:T(8,128)(2,1)}, bf16[1,384,896]{2,1,0:T(8,128)(2,1)}, f32[1,1536]{1,0:T(1,128)}, f32[384,2]{1,0:T(8,128)}, f32[384,384]{1,0:...) custom-call(s32[32]{0:T(128)} %groups.3, ...), custom_call_target="tpu_custom_call" | custom-call | flops 4529848320 | bytes 16777216 | tf_op jit(solution)/shard_map/pallas_call | solution.py:736
  71.6 0.6 collective-permute-start.1
  72.2 0.8 collective-permute-start.2
  72.9 1.0 collective-permute-start.3
  74.0 0.6 fusion.15
  75.9 0.8 copy-done.10
  76.7 3.9 %shard_map.322 = (bf16[2,180,384]{2,1,0:T(8,128)(2,1)}, f32[384,384]{1,0:T(8,128)}, bf16[384,384]{1,0:T(8,128)(2,1)}, f32[8,384]{1,0:T(8,128)}) custom-call(s32[1]{0:T(128)S(6)} %add.112.choice, bf16[2,2,180,384]{3,2,1,0:T(8,128)(2,1)} %bitcast.24, f32[384]{0:T(512)} %gain.4, f32[384]{0:T(512)} %bias2.1, bf16[4,384,384]{2,1,0:T(8,128)(2,1)} %constant.66.clone.high.high_h, ...), custom_call_target="tpu_custom_call" | custom-call | bytes 6057984 | tf_op jit(solution)/shard_map/pallas_call | solution.py:570
  80.7 4.4 %all-to-all-start.2 = ((bf16[16,24,384]{2,1,0:T(8,128)(2,1)}), bf16[16,24,384]{2,1,0:T(8,128)(2,1)S(1)}, u32[]{:S(2)}, u32[]{:S(2)}) async-start(bf16[16,24,384]{2,1,0:T(8,128)(2,1)} %bitcast.31), calls=%async_computation.2 | async-start | bytes 589824 | tf_op jit(solution)/shard_map/all_to_all | solution.py:666
  85.1 7.5 %collective-permute-done.1 = bf16[2,384,512]{2,1,0:T(8,128)(2,1)S(1)} collective-permute-done((bf16[2,384,512]{2,1,0:T(8,128)(2,1)}, bf16[2,384,512]{2,1,0:T(8,128)(2,1)S(1)}, u32[]{:S(2)}, u32[]{:S(2)}) %collective-permute-start.1) | collective-permute-done | bytes 786464 | tf_op jit(solution)/shard_map/ppermute | solution.py:590
  92.6 0.8 add_convert_fusion.2
  93.5 0.4 collective-permute-start.4
  93.8 1.8 %add_convert_fusion.1 = bf16[2,192,512]{2,1,0:T(8,128)(2,1)} fusion(bf16[2,384,512]{2,1,0:T(8,128)(2,1)} %collective-permute-done.2, bf16[2,384,512]{2,1,0:T(8,128)(2,1)S(1)} %copy-done.7), kind=kLoop, calls=%fused_computation.1 | loop fusion | flops 786432 | bytes 1179648 | tf_op jit(solution)/shard_map/convert_element_type | solution.py:794
  95.7 1.2 collective-permute-start.5
  96.8 1.8 %add_convert_fusion = bf16[2,192,512]{2,1,0:T(8,128)(2,1)} fusion(bf16[2,384,512]{2,1,0:T(8,128)(2,1)} %collective-permute-done.3, bf16[2,384,512]{2,1,0:T(8,128)(2,1)S(1)} %copy-done.6), kind=kLoop, calls=%fused_computation | loop fusion | flops 786432 | bytes 1179648 | tf_op jit(solution)/shard_map/convert_element_type | solution.py:794
  98.7 1.5 collective-permute-start.6
  100.1 0.7 copy-done.5
  100.9 7.3 %shard_map.323 = bf16[16,56,384]{2,1,0:T(8,128)(2,1)} custom-call(bf16[384,384]{1,0:T(8,128)(2,1)} %bitcast.27, bf16[768,384]{1,0:T(8,128)(2,1)} %get-tuple-element.83.high, bf16[768,384]{1,0:T(8,128)(2,1)} %get-tuple-element.84.low, bf16[4,96,384]{2,1,0:T(8,128)(2,1)} %reshape.161.weights, bf16[384,768]{1,0:T(8,128)(2,1)} %get-tuple-element.105.s_ref, ...), custom_call_target="tpu_custom_call" | custom-call | bytes 6014976 | tf_op jit(solution)/shard_map/pallas_call | solution.py:557
  108.2 0.9 collective-permute-done.6
  109.1 3.9 %all-to-all-start.3 = ((bf16[16,56,384]{2,1,0:T(8,128)(2,1)}), bf16[16,56,384]{2,1,0:T(8,128)(2,1)S(1)}, u32[]{:S(2)}, u32[]{:S(2)}) async-start(bf16[16,56,384]{2,1,0:T(8,128)(2,1)} %shard_map.323), calls=%async_computation.3 | async-start | bytes 1376256 | tf_op jit(solution)/shard_map/all_to_all | solution.py:839
  113.0 1.4 add_convert_fusion.5
  114.4 2.0 %collective-permute-start.7 = (bf16[2,96,512]{2,1,0:T(8,128)(2,1)S(1)}, bf16[2,96,512]{2,1,0:T(8,128)(2,1)S(1)}, u32[]{:S(2)}, u32[]{:S(2)}) collective-permute-start(bf16[2,96,512]{2,1,0:T(8,128)(2,1)S(1)} %get-tuple-element.153), channel_id=1, source_target_pairs={{0,8},{2,10},{4,12},{6,14},{8,0},{10,2},{12,4},{14,6},{16,24},{18,... | collective-permute-start | bytes 589832 | tf_op jit(solution)/shard_map/ppermute | solution.py:590
  116.4 1.4 add_convert_fusion.4
  117.7 1.5 collective-permute-start.8
  119.3 1.4 add_convert_fusion.3
  120.6 1.5 collective-permute-start.9
  122.2 0.9 copy.58
  123.1 5.9 %collective-permute-done.7 = bf16[2,96,512]{2,1,0:T(8,128)(2,1)S(1)} collective-permute-done((bf16[2,96,512]{2,1,0:T(8,128)(2,1)S(1)}, bf16[2,96,512]{2,1,0:T(8,128)(2,1)S(1)}, u32[]{:S(2)}, u32[]{:S(2)}) %collective-permute-start.7) | collective-permute-done | bytes 196640 | tf_op jit(solution)/shard_map/ppermute | solution.py:590
  129.2 0.7 all-to-all-done.3.got
  130.0 1.8 %collective-permute-start.10 = (bf16[2,48,1536]{2,1,0:T(8,128)(2,1)S(1)}, bf16[2,48,1536]{2,1,0:T(8,128)(2,1)}, u32[]{:S(2)}, u32[]{:S(2)}) collective-permute-start(bf16[2,48,1536]{2,1,0:T(8,128)(2,1)S(1)} %pad_maximum_fusion), channel_id=1, source_target_pairs={{0,16},{2,18},{4,20},{6,22},{8,24},{10,26},{12,28},{14,30},{16,0},... | collective-permute-start | bytes 884744 | tf_op jit(solution)/shard_map/ppermute | solution.py:590
  131.8 3.4 %shard_map.324 = (f32[384,384]{1,0:T(8,128)}, f32[384,3]{1,0:T(8,128)}, bf16[16,32,384]{2,1,0:T(8,128)(2,1)}) custom-call(s32[1]{0:T(128)S(6)} %add.112.choice, bf16[16,56,384]{2,1,0:T(8,128)(2,1)} %copy-done, bf16[4,384,384]{2,1,0:T(8,128)(2,1)} %constant.66.clone.high.high_h, bf16[4,384,384]{2,1,0:T(8,128)(2,1)} %constant.67.clone.low.low_h, ...), custom_call_target="tpu_custom_call" | custom-call | bytes 5217792 | tf_op jit(solution)/shard_map/pallas_call | solution.py:570
  135.2 4.1 %all-to-all-start.4 = ((bf16[16,32,384]{2,1,0:T(8,128)(2,1)}), bf16[16,32,384]{2,1,0:T(8,128)(2,1)S(1)}, u32[]{:S(2)}, u32[]{:S(2)}) async-start(bf16[16,32,384]{2,1,0:T(8,128)(2,1)} %get-tuple-element.129), calls=%async_computation.4 | async-start | bytes 786432 | tf_op jit(solution)/shard_map/all_to_all | solution.py:865
  139.3 4.6 %psum.7 = f32[384,3]{1,0:T(8,128)S(1)} all-reduce(f32[384,3]{1,0:T(8,128)} %get-tuple-element.123), channel_id=1, replica_groups=mesh['lat'=16,'mp'=2] {'mp'}, use_global_device_ids=true, to_apply=%region_4.5 | all-reduce | flops 1152 | bytes 9216 | tf_op jit(solution)/shard_map/psum | solution.py:857
  143.9 4.8 %collective-permute-done.10 = bf16[2,48,1536]{2,1,0:T(8,128)(2,1)} collective-permute-done((bf16[2,48,1536]{2,1,0:T(8,128)(2,1)S(1)}, bf16[2,48,1536]{2,1,0:T(8,128)(2,1)}, u32[]{:S(2)}, u32[]{:S(2)}) %collective-permute-start.10) | collective-permute-done | bytes 294944 | tf_op jit(solution)/shard_map/ppermute | solution.py:590
  148.7 0.4 slice_reduce_fusion.2
  149.1 0.2 multiply_add_fusion
  149.4 1.1 copy.60
  150.5 1.0 maximum_add_fusion
  151.5 0.8 slice_bitcast_fusion
  152.3 0.7 copy-done.4
  153.1 2.1 %shard_map.325 = (f32[384]{0:T(512)}, f32[384]{0:T(512)}, f32[2,4,96,96]{3,2,1,0:T(8,128)}, f32[2,4,96]{2,1,0:T(4,128)}, f32[2,4,96,96]{3,2,1,0:T(8,128)}, /*ind...) custom-call(bf16[16,32,384]{2,1,0:T(8,128)(2,1)} %copy-done.4), custom_call_target="tpu_custom_call" | custom-call | bytes 1003008 | tf_op jit(solution)/shard_map/pallas_call | solution.py:557
  (80 shorter events, 0.9 us)
Async XLA Ops:
  7.7 8.5 %copy-start.18 = (s32[32]{0:T(128)S(1)}, s32[32]{0:T(128)}, u32[]{:S(2)}) copy-start(s32[32]{0:T(128)} %groups.3) | copy-start | bytes 388
  7.7 8.6 %copy-start.25 = (s32[32]{0:T(128)S(1)}, s32[32]{0:T(128)}, u32[]{:S(2)}) copy-start(s32[32]{0:T(128)} %param.24) | copy-start | bytes 388
  7.7 8.7 %copy-start.23 = (f32[2,4,96]{2,1,0:T(4,128)S(1)}, f32[2,4,96]{2,1,0:T(4,128)}, u32[]{:S(2)}) copy-start(f32[2,4,96]{2,1,0:T(4,128)} %param.28) | copy-start | bytes 9220
  7.7 8.7 %copy-start.24 = (f32[2,4,96]{2,1,0:T(4,128)S(1)}, f32[2,4,96]{2,1,0:T(4,128)}, u32[]{:S(2)}) copy-start(f32[2,4,96]{2,1,0:T(4,128)} %param.30) | copy-start | bytes 9220
  7.8 8.8 %copy-start.16 = (f32[384]{0:T(512)S(1)}, f32[384]{0:T(512)}, u32[]{:S(2)}) copy-start(f32[384]{0:T(512)} %gain.5) | copy-start | bytes 4612
  7.8 8.8 %copy-start.20 = (f32[384]{0:T(512)S(1)}, f32[384]{0:T(512)}, u32[]{:S(2)}) copy-start(f32[384]{0:T(512)} %bias.1) | copy-start | bytes 4612
  7.8 8.8 %copy-start.21 = (f32[384]{0:T(512)S(1)}, f32[384]{0:T(512)}, u32[]{:S(2)}) copy-start(f32[384]{0:T(512)} %gain.4) | copy-start | bytes 4612
  7.8 8.8 %copy-start.26 = (f32[384]{0:T(512)S(1)}, f32[384]{0:T(512)}, u32[]{:S(2)}) copy-start(f32[384]{0:T(512)} %param.32) | copy-start | bytes 4612
  7.8 9.7 %copy-start.13 = (bf16[2,180,384]{2,0,1:T(2,128)(2,1)S(1)}, bf16[2,180,384]{2,0,1:T(2,128)(2,1)}, u32[]{:S(2)}) copy-start(bf16[2,180,384]{2,0,1:T(2,128)(2,1)} %param.37) | copy-start | bytes 829444
  7.8 9.8 %copy-start.14 = (bf16[2,4,96,96]{3,2,1,0:T(8,128)(2,1)S(1)}, bf16[2,4,96,96]{3,2,1,0:T(8,128)(2,1)}, u32[]{:S(2)}) copy-start(bf16[2,4,96,96]{3,2,1,0:T(8,128)(2,1)} %param.29) | copy-start | bytes 442372
  7.8 9.8 %copy-start.15 = (bf16[2,4,96,96]{3,2,1,0:T(8,128)(2,1)S(1)}, bf16[2,4,96,96]{3,2,1,0:T(8,128)(2,1)}, u32[]{:S(2)}) copy-start(bf16[2,4,96,96]{3,2,1,0:T(8,128)(2,1)} %param.27) | copy-start | bytes 442372
  7.8 24.9 %all-to-all-start = ((f32[16,24,384]{2,1,0:T(8,128)}), f32[16,24,384]{2,1,0:T(8,128)S(1)}, u32[]{:S(2)}, u32[]{:S(2)}) async-start(f32[16,24,384]{2,1,0:T(8,128)} %bitcast.29), calls=%async_computation | async-start | bytes 1179648 | tf_op jit(solution)/shard_map/all_to_all | solution.py:666
  32.8 0.8 copy-start.1
  33.6 10.2 %copy-start.22 = (f32[1536]{0:T(1024)S(1)}, f32[1536]{0:T(1024)}, u32[]{:S(2)}) copy-start(f32[1536]{0:T(1024)} %param.34) | copy-start | bytes 18436
  39.6 14.1 %all-to-all-start.1 = ((bf16[16,24,384]{2,1,0:T(8,128)(2,1)}), bf16[16,24,384]{2,1,0:T(8,128)(2,1)S(1)}, u32[]{:S(2)}, u32[]{:S(2)}) async-start(bf16[16,24,384]{2,1,0:T(8,128)(2,1)} %bitcast.32), calls=%async_computation.1 | async-start | bytes 589824 | tf_op jit(solution)/shard_map/all_to_all | solution.py:666
  56.2 17.7 %copy-start.19 = (s32[32]{0:T(128)S(1)}, s32[32]{0:T(128)}, u32[]{:S(2)}) copy-start(s32[32]{0:T(128)} %groups.3) | copy-start | bytes 388
  71.6 21.0 %collective-permute-start.1 = (bf16[2,384,512]{2,1,0:T(8,128)(2,1)}, bf16[2,384,512]{2,1,0:T(8,128)(2,1)S(1)}, u32[]{:S(2)}, u32[]{:S(2)}) collective-permute-start(bf16[2,384,512]{2,1,0:T(8,128)(2,1)} %get-tuple-element.99), channel_id=1, source_target_pairs={{0,2},{2,0},{4,6},{6,4},{8,10},{10,8},{12,14},{14,12},{16,18},{18,... | collective-permute-start | bytes 2359304 | tf_op jit(solution)/shard_map/ppermute | solution.py:590
  72.2 3.7 %collective-permute-start = (bf16[384,896]{1,0:T(8,128)(2,1)}, bf16[384,896]{1,0:T(8,128)(2,1)S(1)}, u32[]{:S(2)}, u32[]{:S(2)}) collective-permute-start(bf16[384,896]{1,0:T(8,128)(2,1)} %bitcast.35), channel_id=1, source_target_pairs={{0,1},{1,0},{2,3},{3,2},{4,5},{5,4},{6,7},{7,6},{8,9},{9,8},{10,11... | collective-permute-start | bytes 2064392 | tf_op jit(solution)/shard_map/ppermute | solution.py:783
  72.2 21.7 %collective-permute-start.2 = (bf16[2,384,512]{2,1,0:T(8,128)(2,1)}, bf16[2,384,512]{2,1,0:T(8,128)(2,1)}, u32[]{:S(2)}, u32[]{:S(2)}) collective-permute-start(bf16[2,384,512]{2,1,0:T(8,128)(2,1)} %get-tuple-element.101), channel_id=1, source_target_pairs={{0,4},{2,6},{4,0},{6,2},{8,12},{10,14},{12,8},{14,10},{16,20},{18,... | collective-permute-start | bytes 2359304 | tf_op jit(solution)/shard_map/ppermute | solution.py:590
  72.9 23.9 %collective-permute-start.3 = (bf16[2,384,512]{2,1,0:T(8,128)(2,1)}, bf16[2,384,512]{2,1,0:T(8,128)(2,1)}, u32[]{:S(2)}, u32[]{:S(2)}) collective-permute-start(bf16[2,384,512]{2,1,0:T(8,128)(2,1)} %get-tuple-element.103), channel_id=1, source_target_pairs={{0,8},{2,10},{4,12},{6,14},{8,0},{10,2},{12,4},{14,6},{16,24},{18,... | collective-permute-start | bytes 2359304 | tf_op jit(solution)/shard_map/ppermute | solution.py:590
  75.9 0.8 copy-start.10
  76.7 15.9 %copy-start.8 = (bf16[2,384,512]{2,1,0:T(8,128)(2,1)S(1)}, bf16[2,384,512]{2,1,0:T(8,128)(2,1)}, u32[]{:S(2)}) copy-start(bf16[2,384,512]{2,1,0:T(8,128)(2,1)} %get-tuple-element.98) | copy-start | bytes 2359300
  80.7 13.2 %copy-start.7 = (bf16[2,384,512]{2,1,0:T(8,128)(2,1)S(1)}, bf16[2,384,512]{2,1,0:T(8,128)(2,1)}, u32[]{:S(2)}) copy-start(bf16[2,384,512]{2,1,0:T(8,128)(2,1)} %get-tuple-element.100) | copy-start | bytes 2359300
  80.7 19.5 %all-to-all-start.2 = ((bf16[16,24,384]{2,1,0:T(8,128)(2,1)}), bf16[16,24,384]{2,1,0:T(8,128)(2,1)S(1)}, u32[]{:S(2)}, u32[]{:S(2)}) async-start(bf16[16,24,384]{2,1,0:T(8,128)(2,1)} %bitcast.31), calls=%async_computation.2 | async-start | bytes 589824 | tf_op jit(solution)/shard_map/all_to_all | solution.py:666
  92.6 15.6 %copy-start.9 = (bf16[2,384,512]{2,1,0:T(8,128)(2,1)}, bf16[2,384,512]{2,1,0:T(8,128)(2,1)S(1)}, u32[]{:S(2)}) copy-start(bf16[2,384,512]{2,1,0:T(8,128)(2,1)S(1)} %collective-permute-done.1) | copy-start | bytes 2359300
  92.6 4.2 %copy-start.6 = (bf16[2,384,512]{2,1,0:T(8,128)(2,1)S(1)}, bf16[2,384,512]{2,1,0:T(8,128)(2,1)}, u32[]{:S(2)}) copy-start(bf16[2,384,512]{2,1,0:T(8,128)(2,1)} %get-tuple-element.102) | copy-start | bytes 2359300
  93.5 14.7 %collective-permute-start.4 = (bf16[2,192,512]{2,1,0:T(8,128)(2,1)}, bf16[2,192,512]{2,1,0:T(8,128)(2,1)}, u32[]{:S(2)}, u32[]{:S(2)}) collective-permute-start(bf16[2,192,512]{2,1,0:T(8,128)(2,1)} %add_convert_fusion.2), channel_id=1, source_target_pairs={{0,4},{2,6},{4,0},{6,2},{8,12},{10,14},{12,8},{14,10},{16,20},{18,... | collective-permute-start | bytes 1179656 | tf_op jit(solution)/shard_map/ppermute | solution.py:590
  95.7 12.5 %collective-permute-start.5 = (bf16[2,192,512]{2,1,0:T(8,128)(2,1)}, bf16[2,192,512]{2,1,0:T(8,128)(2,1)}, u32[]{:S(2)}, u32[]{:S(2)}) collective-permute-start(bf16[2,192,512]{2,1,0:T(8,128)(2,1)} %add_convert_fusion.1), channel_id=1, source_target_pairs={{0,8},{2,10},{4,12},{6,14},{8,0},{10,2},{12,4},{14,6},{16,24},{18,... | collective-permute-start | bytes 1179656 | tf_op jit(solution)/shard_map/ppermute | solution.py:590
  98.7 10.4 %collective-permute-start.6 = (bf16[2,192,512]{2,1,0:T(8,128)(2,1)}, bf16[2,192,512]{2,1,0:T(8,128)(2,1)}, u32[]{:S(2)}, u32[]{:S(2)}) collective-permute-start(bf16[2,192,512]{2,1,0:T(8,128)(2,1)} %add_convert_fusion), channel_id=1, source_target_pairs={{0,2},{2,0},{4,6},{6,4},{8,10},{10,8},{12,14},{14,12},{16,18},{18,... | collective-permute-start | bytes 1179656 | tf_op jit(solution)/shard_map/ppermute | solution.py:590
  100.1 0.7 copy-start.5
  109.1 20.9 %all-to-all-start.3 = ((bf16[16,56,384]{2,1,0:T(8,128)(2,1)}), bf16[16,56,384]{2,1,0:T(8,128)(2,1)S(1)}, u32[]{:S(2)}, u32[]{:S(2)}) async-start(bf16[16,56,384]{2,1,0:T(8,128)(2,1)} %shard_map.323), calls=%async_computation.3 | async-start | bytes 1376256 | tf_op jit(solution)/shard_map/all_to_all | solution.py:839
  114.4 14.6 %collective-permute-start.7 = (bf16[2,96,512]{2,1,0:T(8,128)(2,1)S(1)}, bf16[2,96,512]{2,1,0:T(8,128)(2,1)S(1)}, u32[]{:S(2)}, u32[]{:S(2)}) collective-permute-start(bf16[2,96,512]{2,1,0:T(8,128)(2,1)S(1)} %get-tuple-element.153), channel_id=1, source_target_pairs={{0,8},{2,10},{4,12},{6,14},{8,0},{10,2},{12,4},{14,6},{16,24},{18,... | collective-permute-start | bytes 589832 | tf_op jit(solution)/shard_map/ppermute | solution.py:590
  117.7 4.4 %copy-start.12 = (bf16[2,180,384]{2,1,0:T(8,128)(2,1)S(1)}, bf16[2,180,384]{2,1,0:T(8,128)(2,1)}, u32[]{:S(2)}) copy-start(bf16[2,180,384]{2,1,0:T(8,128)(2,1)} %get-tuple-element.113) | copy-start | bytes 829444
  117.7 11.3 %collective-permute-start.8 = (bf16[2,96,512]{2,1,0:T(8,128)(2,1)S(1)}, bf16[2,96,512]{2,1,0:T(8,128)(2,1)S(1)}, u32[]{:S(2)}, u32[]{:S(2)}) collective-permute-start(bf16[2,96,512]{2,1,0:T(8,128)(2,1)S(1)} %get-tuple-element.151), channel_id=1, source_target_pairs={{0,2},{2,0},{4,6},{6,4},{8,10},{10,8},{12,14},{14,12},{16,18},{18,... | collective-permute-start | bytes 589832 | tf_op jit(solution)/shard_map/ppermute | solution.py:590
  120.6 8.5 %collective-permute-start.9 = (bf16[2,96,512]{2,1,0:T(8,128)(2,1)S(1)}, bf16[2,96,512]{2,1,0:T(8,128)(2,1)S(1)}, u32[]{:S(2)}, u32[]{:S(2)}) collective-permute-start(bf16[2,96,512]{2,1,0:T(8,128)(2,1)S(1)} %get-tuple-element.149), channel_id=1, source_target_pairs={{0,4},{2,6},{4,0},{6,2},{8,12},{10,14},{12,8},{14,10},{16,20},{18,... | collective-permute-start | bytes 589832 | tf_op jit(solution)/shard_map/ppermute | solution.py:590
  130.0 1.8 %copy-start = (bf16[16,56,384]{2,1,0:T(8,128)(2,1)}, bf16[16,56,384]{2,1,0:T(8,128)(2,1)S(1)}, u32[]{:S(2)}) copy-start(bf16[16,56,384]{2,1,0:T(8,128)(2,1)S(1)} %all-to-all-done.3.got) | copy-start | bytes 2064388
  130.0 18.7 %collective-permute-start.10 = (bf16[2,48,1536]{2,1,0:T(8,128)(2,1)S(1)}, bf16[2,48,1536]{2,1,0:T(8,128)(2,1)}, u32[]{:S(2)}, u32[]{:S(2)}) collective-permute-start(bf16[2,48,1536]{2,1,0:T(8,128)(2,1)S(1)} %pad_maximum_fusion), channel_id=1, source_target_pairs={{0,16},{2,18},{4,20},{6,22},{8,24},{10,26},{12,28},{14,30},{16,0},... | collective-permute-start | bytes 884744 | tf_op jit(solution)/shard_map/ppermute | solution.py:590
  135.2 13.9 %copy-start.2 = (f32[384,384]{1,0:T(8,128)S(1)}, f32[384,384]{1,0:T(8,128)}, u32[]{:S(2)}) copy-start(f32[384,384]{1,0:T(8,128)} %get-tuple-element.121.xh) | copy-start | bytes 1769476
  135.2 13.9 %copy-start.3 = (f32[384,384]{1,0:T(8,128)S(1)}, f32[384,384]{1,0:T(8,128)}, u32[]{:S(2)}) copy-start(f32[384,384]{1,0:T(8,128)} %get-tuple-element.115.dx1) | copy-start | bytes 1769476
  135.2 13.9 %copy-start.11 = (f32[384,384]{1,0:T(8,128)S(1)}, f32[384,384]{1,0:T(8,128)}, u32[]{:S(2)}) copy-start(f32[384,384]{1,0:T(8,128)} %get-tuple-element.128) | copy-start | bytes 1769476
  135.2 13.9 %copy-start.17 = (f32[384]{0:T(512)S(1)}, f32[384]{0:T(512)}, u32[]{:S(2)}) copy-start(f32[384]{0:T(512)} %gain.5) | copy-start | bytes 4612
  135.2 17.2 %all-to-all-start.4 = ((bf16[16,32,384]{2,1,0:T(8,128)(2,1)}), bf16[16,32,384]{2,1,0:T(8,128)(2,1)S(1)}, u32[]{:S(2)}, u32[]{:S(2)}) async-start(bf16[16,32,384]{2,1,0:T(8,128)(2,1)} %get-tuple-element.129), calls=%async_computation.4 | async-start | bytes 786432 | tf_op jit(solution)/shard_map/all_to_all | solution.py:865
  152.3 0.7 copy-start.4

commit v5 on v4

--- a/solution.py
+++ b/solution.py
@@ -282,27 +282,23 @@
     return jnp.where(lane == target, 1.0, 0.0).astype(BF)
 
 
-def cotangent_kernel(columns, padded, dy_all, places, field_all, vectors, w2, dyt, dact, base, pad, dy_s):
+def cotangent_kernel(columns, padded, dy_all, places, field_all, vectors, dyt, dy_s, base, pad):
     mp, rows_dev, ch = dy_all.shape[0], dy_all.shape[1], dy_all.shape[3]
 
-    @pl.when(pl.program_id(0) == 0)
-    def _():
-        for m in range(mp):
-            pad[...] = jnp.zeros_like(pad)
-            for r in range(rows_dev):
-                pad[r * padded : r * padded + columns, :] = dy_all[m, r].astype(F32)
-            dy_s[:, m * ch : (m + 1) * ch] = pad[...].astype(BF)
-        dyt[...] = mm_nt(swap_matrix(places), dy_s[...]).astype(BF)
-        for m in range(mp):
-            base[m] = jnp.zeros(base.shape[1:], F32)
-            for r in range(rows_dev):
-                base[m, r * padded : r * padded + columns, :] = field_all[m, r].astype(F32)
-        average, inv = second_norm([base[m] for m in range(mp)])
-        for m in range(mp):
-            x = base[m]
-            base[m] = x + (x - average) * inv * vectors[m, 0:1, :] + vectors[m, 1:2, :]
-
-    dact[...] = mm_nt(dy_s[...], w2[...])
+    for m in range(mp):
+        pad[...] = jnp.zeros_like(pad)
+        for r in range(rows_dev):
+            pad[r * padded : r * padded + columns, :] = dy_all[m, r].astype(F32)
+        dy_s[:, m * ch : (m + 1) * ch] = pad[...].astype(BF)
+    dyt[...] = mm_nt(swap_matrix(places), dy_s[...]).astype(BF)
+    for m in range(mp):
+        base[m] = jnp.zeros(base.shape[1:], F32)
+        for r in range(rows_dev):
+            base[m, r * padded : r * padded + columns, :] = field_all[m, r].astype(F32)
+    average, inv = second_norm([base[m] for m in range(mp)])
+    for m in range(mp):
+        x = base[m]
+        base[m] = x + (x - average) * inv * vectors[m, 0:1, :] + vectors[m, 1:2, :]
 
 
 def width_choice(groups, rows_dev):
@@ -313,11 +309,11 @@
     return choice
 
 
-def mlp_kernel(orders, rows_dev, groups, vectors, b1, places, eo_h, high_h, low_h, base_h, w1_h, dact_h, w2_h, dyt_h, *refs):
+def mlp_kernel(orders, rows_dev, groups, vectors, b1, places, eo_h, high_h, low_h, base_h, w1_h, dy_h, w2_h, dyt_h, *refs):
     mp, pieces = vectors.shape[0], len(orders)
     kept_h, away_h, gb1, norm_out, own_h = refs[:5]
     grads_h = refs[5 : 5 + 2 * pieces]
-    eo, table, base, w1, dact, w2, dyt, kept_send, away_send = refs[5 + 2 * pieces : 14 + 2 * pieces]
+    eo, table, base, w1, dy, w2, dyt, kept_send, away_send = refs[5 + 2 * pieces : 14 + 2 * pieces]
     grads = refs[14 + 2 * pieces : 14 + 4 * pieces]
     n_s, nt_s, q_s, dp_s, sems = refs[14 + 4 * pieces :]
     ch, width, hidden = base.shape[2], w1.shape[0], w1.shape[1]
@@ -335,15 +331,14 @@
     swap = swap_matrix(places)
     for copy in first:
         copy.wait()
-    loads = []
-    for p in range(pieces):
-        loads.append(
-            (
-                move.start(w1_h.at[:, spans[p]], w1.at[:, spans[p]]),
-                move.start(dact_h.at[:, spans[p]], dact.at[:, spans[p]]),
-            )
+    load_dy = move.start(dy_h, dy)
+    loads = [
+        (
+            move.start(w1_h.at[:, span], w1.at[:, span]),
+            move.start(w2_h.at[span, :], w2.at[span, :]),
         )
-    load_w2 = move.start(w2_h, w2)
+        for span in spans
+    ]
     load_dyt = move.start(dyt_h, dyt)
     every = jnp.concatenate([eo[m] for m in range(mp)], axis=1)
     filtered = mm_t(table[0], every) + mm_t(table[1], every)
@@ -362,10 +357,13 @@
         span = spans[piece]
         for copy in loads[piece]:
             copy.wait()
+        if piece == 0:
+            load_dy.wait()
+        dact = mm_nt(dy[...], w2[span, :])
         q, slope = gelu_pair(mm(n_s[...], w1[:, span]) + b1[:, span])
         q = q.astype(BF)
         q_s[:, span] = q
-        dp = (dact[:, span] * slope).astype(BF)
+        dp = (dact * slope).astype(BF)
         dp_s[:, span] = dp
         gb1[:, span] = column_sum(dp.astype(F32))
 
@@ -383,7 +381,6 @@
             value = value - term
             stat = jnp.where(spot == at + i, term, stat)
     stat = stat.astype(BF)
-    load_w2.wait()
     out = mm(q_s[...], w2[...])
     for m in range(mp):
         lanes = slice(m * ch, (m + 1) * ch)
@@ -708,27 +705,14 @@
     places = np.stack(
         [np.arange(full_width) // share_rows, np.arange(full_width) % share_rows], axis=1
     ).astype(np.int32)
-    dyt, dact, base = pl.pallas_call(
+    dyt, dy_pad, base = run(
         functools.partial(cotangent_kernel, columns, padded),
-        out_shape=[bf(full_width, tokens), f32(tokens, hidden), f32(mp, tokens, ch)],
-        grid=(steps,),
-        in_specs=[
-            whole(dy_all.shape),
-            whole(places.shape),
-            whole(field_all.shape),
-            whole(vectors_all.shape),
-            pl.BlockSpec((chunk, full_width), lambda i: (i, 0)),
-        ],
-        out_specs=[
-            whole((full_width, tokens)),
-            pl.BlockSpec((tokens, chunk), lambda i: (0, i)),
-            whole((mp, tokens, ch)),
-        ],
-        scratch_shapes=[pltpu.VMEM((tokens, ch), F32), pltpu.VMEM((tokens, full_width), BF)],
-        compiler_params=pltpu.CompilerParams(vmem_limit_bytes=56 * 2**20),
-    )(dy_all, jnp.asarray(places), field_all, vectors_all, fc2_weight)
+        [bf(full_width, tokens), bf(tokens, full_width), f32(mp, tokens, ch)],
+        [dy_all, jnp.asarray(places), field_all, vectors_all],
+        [pltpu.VMEM((tokens, ch), F32)],
+    )
     eo = to_other(eo, group).reshape(patches, ch)
-    eo, dyt, dact, base = lax.optimization_barrier((eo, dyt, dact, base))
+    eo, dyt, dy_pad, base = lax.optimization_barrier((eo, dyt, dy_pad, base))
     eo = lax.all_gather(eo, "mp", axis=0)
 
     send_lanes = 2 * ch + 128
@@ -750,7 +734,7 @@
             table,
             pltpu.VMEM(base.shape, F32),
             pltpu.VMEM(fc1_weight.shape, BF),
-            pltpu.VMEM(dact.shape, F32),
+            pltpu.VMEM(dy_pad.shape, BF),
             pltpu.VMEM(fc2_weight.shape, BF),
             pltpu.VMEM(dyt.shape, BF),
             pltpu.VMEM((tokens, send_lanes), BF),
@@ -775,7 +759,7 @@
         *lon,
         base,
         fc1_weight,
-        dact,
+        dy_pad,
         fc2_weight,
         dyt,
     )
@@ -870,6 +854,7 @@
         [vector, vector, weight, bias, weight, bias, vector, vector, hidden_bias, vector],
         [tail],
         [pltpu.VMEM((4 * size, ch), F32)],
+        limit=24,
     )
     return (
         out_field,

time: 156 us -> 154 us (0.987)
  Pallas kernels: 50.6 us -> 47.3 us
  waiting for transfers between devices: 28 us -> 30.1 us
    pallas_call x1 -> x0, Pallas kernels: 6.3 us -> none  [body(): pl.pallas_call(functools.partial(cotangent_kernel, columns, padded), out_...]
    pallas_call x3 -> x4, Pallas kernels: 12 us -> 14.9 us  [run(): pl.pallas_call(kernel, out_shape=out_shape, in_specs=[pl.BlockSpec(memory...]
    all_to_all x3, waiting for transfers between devices: 8.02 us -> 10.5 us  [to_other(): lax.all_to_all(values.reshape(parts, rows_each, ch), 'lat', 0, 0, tiled=T...]
    unnamed x57 -> x55, local copies, waits for them, and re-layouts: 5.34 us -> 4.6 us
  transfers between devices with their start and end apart: 16 -> 16, of which waited for: 7 -> 7; matrix products, arithmetic and copies ran while one was open for 12% -> 12% of each run, Pallas kernels for 15% -> 14%
where the time goes in v5:
time: 154 us; the launch traced here: 153 us
  Pallas kernels  47.3 us (31%)
  starting transfers between devices  37.2 us (24%)
  waiting for transfers between devices  30.1 us (20%)
  blocking collectives  13.8 us (9%)
  other arithmetic  12.2 us (8%)
  local copies, waits for them, and re-layouts  10.2 us (7%)
  between operations  2.45 us (2%)
    ppermute x10, waiting for transfers between devices, swapped(): return lax.ppermute(away, 'lat', [(d, d ^ bit) for d in range(parts)])  18.8 us
    all_to_all x3, starting transfers between devices, to_other(): lax.all_to_all(values.reshape(parts, rows_each, ch), 'lat', 0, 0, tiled=T...  17 us
    pallas_call x1, Pallas kernels, body(): pl.pallas_call(functools.partial(mlp_kernel, orders, rows_dev), out_shape...  15.5 us
    pallas_call x4, Pallas kernels, run(): pl.pallas_call(kernel, out_shape=out_shape, in_specs=[pl.BlockSpec(memory...  14.9 us
    ppermute x10, starting transfers between devices, swapped(): return lax.ppermute(away, 'lat', [(d, d ^ bit) for d in range(parts)])  12.2 us
    all_to_all x3, waiting for transfers between devices, to_other(): lax.all_to_all(values.reshape(parts, rows_each, ch), 'lat', 0, 0, tiled=T...  10.5 us
    pallas_call x2, Pallas kernels, run(): pl.pallas_call(kernel, out_shape=out_shape, grid_spec=pltpu.PrefetchScala...  7.31 us
    pallas_call x1, Pallas kernels, body(): pl.pallas_call(functools.partial(filter_kernel, blocks, size), out_shape=...  5.99 us
  transfers between devices with their start and end apart: 16, of which 7 were waited for; matrix products, arithmetic and copies ran while one was open for 12% of the time, Pallas kernels for 14%

profile of v5, /device:TPU:0, one launch (start us, length us, event | category | flops | bytes accessed | tf_op | source)
XLA Modules:
  0.0 153.2 jit_solution(6946788731674625009)
XLA Ops:
  0.6 1.0 copy.53
  1.6 2.4 %all-gather = bf16[4,180,384]{2,1,0:T(8,128)(2,1)} all-gather(bf16[2,180,384]{2,1,0:T(8,128)(2,1)S(1)} %copy.53), channel_id=2, replica_groups=mesh['lat'=16,'mp'=2] {'mp'}, dimensions={0}, use_global_device_ids=true | all-gather | bytes 829440 | tf_op jit(solution)/shard_map/all_gather | solution.py:645
  4.1 3.6 %shard_map.317 = (f32[384,384]{1,0:T(8,128)}, f32[384,384]{1,0:T(8,128)}, f32[384,1]{1,0:T(8,128)}) custom-call(s32[32]{0:T(128)} %groups.3, bf16[2,2,180,384]{3,2,1,0:T(8,128)(2,1)} %bitcast.21, f32[384]{0:T(512)} %gain.5, f32[384]{0:T(512)} %bias.1, bf16[4,384,384]{2,1,0:T(8,128)(2,1)} %constant.66.clone.high.high_h, ...), custom_call_target="tpu_custom_call" | custom-call | tf_op jit(solution)/shard_map/pallas_call | solution.py:647
  7.8 8.4 %all-to-all-start = ((f32[16,24,384]{2,1,0:T(8,128)}), f32[16,24,384]{2,1,0:T(8,128)S(1)}, u32[]{:S(2)}, u32[]{:S(2)}) async-start(f32[16,24,384]{2,1,0:T(8,128)} %bitcast.29), calls=%async_computation | async-start | bytes 1179648 | tf_op jit(solution)/shard_map/all_to_all | solution.py:663
  16.3 0.1 fusion.11
  16.7 0.1 copy.55
  16.8 0.7 sub.27.keep
  17.6 0.1 maximum_bitcast_fusion
  17.7 0.2 copy.57
  17.9 1.0 reshape.161.weights
  18.9 0.2 fusion.3
  19.2 0.3 select_multiply_fusion.1
  19.5 0.7 pad_maximum_fusion.1.tables
  20.2 2.6 %shard_map.318 = (bf16[768,384]{1,0:T(8,128)(2,1)}, bf16[768,384]{1,0:T(8,128)(2,1)}) custom-call(f32[32,64]{1,0:T(8,128)} %pad_maximum_fusion.1.tables, bf16[192,32]{1,0:T(8,128)(2,1)} %constant.68.clone.left, bf16[4,64,384]{2,1,0:T(8,128)(2,1)} %constant.69.clone.right, bf16[192,384]{1,0:T(8,128)(2,1)} %constant.70.clone.same, f32[192,1]{1,0:T(8,128)} %sub.27.keep), custom_call_target="tpu_custom_call" | custom-call | bytes 1544960 | tf_op jit(solution)/shard_map/pallas_call | solution.py:554
  22.8 1.9 %all_gather.23.vectors = f32[2,4,384]{2,1,0:T(4,128)} all-gather(f32[1,4,384]{2,1,0:T(4,128)S(1)} %all_gather_reshape.3), channel_id=1, replica_groups=mesh['lat'=16,'mp'=2] {'mp'}, dimensions={0}, use_global_device_ids=true | all-gather | bytes 18432 | tf_op jit(solution)/shard_map/all_gather | solution.py:684
  24.7 0.6 pad_maximum_fusion.3.biases
  25.3 2.3 %all-gather.1 = bf16[4,180,384]{2,1,0:T(8,128)(2,1)} all-gather(bf16[2,180,384]{2,1,0:T(8,128)(2,1)S(1)} %copy.54), channel_id=3, replica_groups=mesh['lat'=16,'mp'=2] {'mp'}, dimensions={0}, use_global_device_ids=true | all-gather | bytes 829440 | tf_op jit(solution)/shard_map/all_gather | solution.py:685
  27.6 5.1 %all-to-all-done = f32[16,24,384]{2,1,0:T(8,128)S(1)} async-done(((f32[16,24,384]{2,1,0:T(8,128)}), f32[16,24,384]{2,1,0:T(8,128)S(1)}, u32[]{:S(2)}, u32[]{:S(2)}) %all-to-all-start) | async-done | bytes 589856 | tf_op jit(solution)/shard_map/all_to_all | solution.py:663
  32.8 0.8 copy-done.1
  33.6 6.0 %shard_map.319 = (bf16[384,384]{1,0:T(8,128)(2,1)}, bf16[384,768]{1,0:T(8,128)(2,1)}, bf16[384,768]{1,0:T(8,128)(2,1)}, f32[384,768]{1,0:T(8,128)}, f32[384,768]{1,0:T(8,128)}) custom-call(f32[384,384]{1,0:T(8,128)} %bitcast.25, bf16[768,384]{1,0:T(8,128)(2,1)} %get-tuple-element.83.high, bf16[768,384]{1,0:T(8,128)(2,1)} %get-tuple-element.84.low, ...), custom_call_target="tpu_custom_call" | custom-call | tf_op jit(solution)/shard_map/pallas_call | solution.py:690
  39.6 4.2 %all-to-all-start.1 = ((bf16[16,24,384]{2,1,0:T(8,128)(2,1)}), bf16[16,24,384]{2,1,0:T(8,128)(2,1)S(1)}, u32[]{:S(2)}, u32[]{:S(2)}) async-start(bf16[16,24,384]{2,1,0:T(8,128)(2,1)} %bitcast.32), calls=%async_computation.1 | async-start | bytes 589824 | tf_op jit(solution)/shard_map/all_to_all | solution.py:663
  43.8 0.6 reshape.160.b1
  44.4 3.8 %shard_map.320 = (bf16[768,384]{1,0:T(8,128)(2,1)}, bf16[384,768]{1,0:T(8,128)(2,1)}, f32[2,384,384]{2,1,0:T(8,128)}) custom-call(bf16[2,2,180,384]{3,2,1,0:T(8,128)(2,1)} %bitcast.23, s32[768,2]{1,0:T(8,128)} %constant.71.clone.places, bf16[2,2,180,384]{3,2,1,0:T(8,128)(2,1)} %bitcast.22, f32[2,4,384]{2,1,0:T(4,128)} %all_gather.23.vectors), custom_call_target="tpu_custom_call" | custom-call | bytes 3483648 | tf_op jit(solution)/shard_map/pallas_call | solution.py:554
  48.2 5.4 %all-to-all-done.1 = bf16[16,24,384]{2,1,0:T(8,128)(2,1)S(1)} async-done(((bf16[16,24,384]{2,1,0:T(8,128)(2,1)}), bf16[16,24,384]{2,1,0:T(8,128)(2,1)S(1)}, u32[]{:S(2)}, u32[]{:S(2)}) %all-to-all-start.1) | async-done | bytes 294944 | tf_op jit(solution)/shard_map/all_to_all | solution.py:663
  53.6 2.5 %all-gather.2 = bf16[768,384]{1,0:T(8,128)(2,1)} all-gather(bf16[384,384]{1,0:T(8,128)(2,1)S(1)} %bitcast.28), channel_id=4, replica_groups=mesh['lat'=16,'mp'=2] {'mp'}, dimensions={0}, use_global_device_ids=true | all-gather | bytes 884736 | tf_op jit(solution)/shard_map/all_gather | solution.py:716
  56.1 15.5 %shard_map.321 = (bf16[384,896]{1,0:T(8,128)(2,1)}, bf16[1,384,896]{2,1,0:T(8,128)(2,1)}, f32[1,1536]{1,0:T(1,128)}, f32[384,2]{1,0:T(8,128)}, f32[384,384]{1,0:...) custom-call(s32[32]{0:T(128)} %groups.3, ...), custom_call_target="tpu_custom_call" | custom-call | flops 4529848320 | bytes 16777216 | tf_op jit(solution)/shard_map/pallas_call | solution.py:720
  71.7 0.6 collective-permute-start.1
  72.3 0.8 collective-permute-start.2
  73.1 1.0 collective-permute-start.3
  74.1 0.6 fusion.15
  76.0 0.9 copy-done.9
  76.9 3.9 %shard_map.322 = (bf16[2,180,384]{2,1,0:T(8,128)(2,1)}, f32[384,384]{1,0:T(8,128)}, bf16[384,384]{1,0:T(8,128)(2,1)}, f32[8,384]{1,0:T(8,128)}) custom-call(s32[1]{0:T(128)S(6)} %add.112.choice, bf16[2,2,180,384]{3,2,1,0:T(8,128)(2,1)} %bitcast.24, f32[384]{0:T(512)} %gain.4, f32[384]{0:T(512)} %bias2.1, bf16[4,384,384]{2,1,0:T(8,128)(2,1)} %constant.66.clone.high.high_h, ...), custom_call_target="tpu_custom_call" | custom-call | bytes 6057984 | tf_op jit(solution)/shard_map/pallas_call | solution.py:567
  80.8 4.4 %all-to-all-start.2 = ((bf16[16,24,384]{2,1,0:T(8,128)(2,1)}), bf16[16,24,384]{2,1,0:T(8,128)(2,1)S(1)}, u32[]{:S(2)}, u32[]{:S(2)}) async-start(bf16[16,24,384]{2,1,0:T(8,128)(2,1)} %bitcast.31), calls=%async_computation.2 | async-start | bytes 589824 | tf_op jit(solution)/shard_map/all_to_all | solution.py:663
  85.2 7.5 %collective-permute-done.1 = bf16[2,384,512]{2,1,0:T(8,128)(2,1)S(1)} collective-permute-done((bf16[2,384,512]{2,1,0:T(8,128)(2,1)}, bf16[2,384,512]{2,1,0:T(8,128)(2,1)S(1)}, u32[]{:S(2)}, u32[]{:S(2)}) %collective-permute-start.1) | collective-permute-done | bytes 786464 | tf_op jit(solution)/shard_map/ppermute | solution.py:587
  92.7 0.8 add_convert_fusion.2
  93.6 0.4 collective-permute-start.4
  94.0 1.8 %add_convert_fusion.1 = bf16[2,192,512]{2,1,0:T(8,128)(2,1)} fusion(bf16[2,384,512]{2,1,0:T(8,128)(2,1)} %collective-permute-done.2, bf16[2,384,512]{2,1,0:T(8,128)(2,1)S(1)} %copy-done.6), kind=kLoop, calls=%fused_computation.1 | loop fusion | flops 786432 | bytes 1179648 | tf_op jit(solution)/shard_map/convert_element_type | solution.py:778
  95.8 1.2 collective-permute-start.5
  97.0 1.8 %add_convert_fusion = bf16[2,192,512]{2,1,0:T(8,128)(2,1)} fusion(bf16[2,384,512]{2,1,0:T(8,128)(2,1)} %collective-permute-done.3, bf16[2,384,512]{2,1,0:T(8,128)(2,1)S(1)} %copy-done.5), kind=kLoop, calls=%fused_computation | loop fusion | flops 786432 | bytes 1179648 | tf_op jit(solution)/shard_map/convert_element_type | solution.py:778
  98.8 1.5 collective-permute-start.6
  100.3 0.7 copy-done.4
  101.0 7.3 %shard_map.323 = bf16[16,56,384]{2,1,0:T(8,128)(2,1)} custom-call(bf16[384,384]{1,0:T(8,128)(2,1)} %bitcast.27, bf16[768,384]{1,0:T(8,128)(2,1)} %get-tuple-element.83.high, bf16[768,384]{1,0:T(8,128)(2,1)} %get-tuple-element.84.low, bf16[4,96,384]{2,1,0:T(8,128)(2,1)} %reshape.161.weights, bf16[384,768]{1,0:T(8,128)(2,1)} %get-tuple-element.105.s_ref, ...), custom_call_target="tpu_custom_call" | custom-call | bytes 6014976 | tf_op jit(solution)/shard_map/pallas_call | solution.py:554
  108.3 0.9 collective-permute-done.6
  109.2 3.9 %all-to-all-start.3 = ((bf16[16,56,384]{2,1,0:T(8,128)(2,1)}), bf16[16,56,384]{2,1,0:T(8,128)(2,1)S(1)}, u32[]{:S(2)}, u32[]{:S(2)}) async-start(bf16[16,56,384]{2,1,0:T(8,128)(2,1)} %shard_map.323), calls=%async_computation.3 | async-start | bytes 1376256 | tf_op jit(solution)/shard_map/all_to_all | solution.py:823
  113.1 1.4 add_convert_fusion.5
  114.5 2.0 %collective-permute-start.7 = (bf16[2,96,512]{2,1,0:T(8,128)(2,1)S(1)}, bf16[2,96,512]{2,1,0:T(8,128)(2,1)S(1)}, u32[]{:S(2)}, u32[]{:S(2)}) collective-permute-start(bf16[2,96,512]{2,1,0:T(8,128)(2,1)S(1)} %get-tuple-element.153), channel_id=1, source_target_pairs={{0,8},{2,10},{4,12},{6,14},{8,0},{10,2},{12,4},{14,6},{16,24},{18,... | collective-permute-start | bytes 589832 | tf_op jit(solution)/shard_map/ppermute | solution.py:587
  116.5 1.4 add_convert_fusion.4
  117.9 1.5 collective-permute-start.8
  119.4 1.4 add_convert_fusion.3
  120.8 1.5 collective-permute-start.9
  122.3 0.9 copy.58
  123.2 5.9 %collective-permute-done.7 = bf16[2,96,512]{2,1,0:T(8,128)(2,1)S(1)} collective-permute-done((bf16[2,96,512]{2,1,0:T(8,128)(2,1)S(1)}, bf16[2,96,512]{2,1,0:T(8,128)(2,1)S(1)}, u32[]{:S(2)}, u32[]{:S(2)}) %collective-permute-start.7) | collective-permute-done | bytes 196640 | tf_op jit(solution)/shard_map/ppermute | solution.py:587
  129.3 0.7 all-to-all-done.3.got
  130.0 1.8 %collective-permute-start.10 = (bf16[2,48,1536]{2,1,0:T(8,128)(2,1)S(1)}, bf16[2,48,1536]{2,1,0:T(8,128)(2,1)}, u32[]{:S(2)}, u32[]{:S(2)}) collective-permute-start(bf16[2,48,1536]{2,1,0:T(8,128)(2,1)S(1)} %pad_maximum_fusion), channel_id=1, source_target_pairs={{0,16},{2,18},{4,20},{6,22},{8,24},{10,26},{12,28},{14,30},{16,0},... | collective-permute-start | bytes 884744 | tf_op jit(solution)/shard_map/ppermute | solution.py:587
  131.8 3.4 %shard_map.324 = (f32[384,384]{1,0:T(8,128)}, f32[384,3]{1,0:T(8,128)}, bf16[16,32,384]{2,1,0:T(8,128)(2,1)}) custom-call(s32[1]{0:T(128)S(6)} %add.112.choice, bf16[16,56,384]{2,1,0:T(8,128)(2,1)} %copy-done, bf16[4,384,384]{2,1,0:T(8,128)(2,1)} %constant.66.clone.high.high_h, bf16[4,384,384]{2,1,0:T(8,128)(2,1)} %constant.67.clone.low.low_h, ...), custom_call_target="tpu_custom_call" | custom-call | bytes 5217792 | tf_op jit(solution)/shard_map/pallas_call | solution.py:567
  135.2 4.1 %all-to-all-start.4 = ((bf16[16,32,384]{2,1,0:T(8,128)(2,1)}), bf16[16,32,384]{2,1,0:T(8,128)(2,1)S(1)}, u32[]{:S(2)}, u32[]{:S(2)}) async-start(bf16[16,32,384]{2,1,0:T(8,128)(2,1)} %get-tuple-element.129), calls=%async_computation.4 | async-start | bytes 786432 | tf_op jit(solution)/shard_map/all_to_all | solution.py:849
  139.3 4.6 %psum.7 = f32[384,3]{1,0:T(8,128)S(1)} all-reduce(f32[384,3]{1,0:T(8,128)} %get-tuple-element.123), channel_id=1, replica_groups=mesh['lat'=16,'mp'=2] {'mp'}, use_global_device_ids=true, to_apply=%region_4.5 | all-reduce | flops 1152 | bytes 9216 | tf_op jit(solution)/shard_map/psum | solution.py:841
  143.9 4.5 %collective-permute-done.10 = bf16[2,48,1536]{2,1,0:T(8,128)(2,1)} collective-permute-done((bf16[2,48,1536]{2,1,0:T(8,128)(2,1)S(1)}, bf16[2,48,1536]{2,1,0:T(8,128)(2,1)}, u32[]{:S(2)}, u32[]{:S(2)}) %collective-permute-start.10) | collective-permute-done | bytes 294944 | tf_op jit(solution)/shard_map/ppermute | solution.py:587
  148.5 0.4 slice_reduce_fusion.2
  148.9 0.2 multiply_add_fusion
  149.2 1.1 copy.60
  150.3 1.0 maximum_add_fusion
  151.3 0.8 slice_bitcast_fusion
  152.1 1.1 shard_map.325
  (78 shorter events, 0.8 us)
Async XLA Ops:
  7.7 8.5 %copy-start.17 = (s32[32]{0:T(128)S(1)}, s32[32]{0:T(128)}, u32[]{:S(2)}) copy-start(s32[32]{0:T(128)} %groups.3) | copy-start | bytes 388
  7.7 8.6 %copy-start.24 = (s32[32]{0:T(128)S(1)}, s32[32]{0:T(128)}, u32[]{:S(2)}) copy-start(s32[32]{0:T(128)} %param.24) | copy-start | bytes 388
  7.7 8.7 %copy-start.22 = (f32[2,4,96]{2,1,0:T(4,128)S(1)}, f32[2,4,96]{2,1,0:T(4,128)}, u32[]{:S(2)}) copy-start(f32[2,4,96]{2,1,0:T(4,128)} %param.28) | copy-start | bytes 9220
  7.7 8.7 %copy-start.23 = (f32[2,4,96]{2,1,0:T(4,128)S(1)}, f32[2,4,96]{2,1,0:T(4,128)}, u32[]{:S(2)}) copy-start(f32[2,4,96]{2,1,0:T(4,128)} %param.30) | copy-start | bytes 9220
  7.7 8.8 %copy-start.15 = (f32[384]{0:T(512)S(1)}, f32[384]{0:T(512)}, u32[]{:S(2)}) copy-start(f32[384]{0:T(512)} %gain.5) | copy-start | bytes 4612
  7.8 8.8 %copy-start.19 = (f32[384]{0:T(512)S(1)}, f32[384]{0:T(512)}, u32[]{:S(2)}) copy-start(f32[384]{0:T(512)} %bias.1) | copy-start | bytes 4612
  7.8 8.8 %copy-start.20 = (f32[384]{0:T(512)S(1)}, f32[384]{0:T(512)}, u32[]{:S(2)}) copy-start(f32[384]{0:T(512)} %gain.4) | copy-start | bytes 4612
  7.8 8.8 %copy-start.25 = (f32[384]{0:T(512)S(1)}, f32[384]{0:T(512)}, u32[]{:S(2)}) copy-start(f32[384]{0:T(512)} %param.32) | copy-start | bytes 4612
  7.8 9.7 %copy-start.12 = (bf16[2,180,384]{2,0,1:T(2,128)(2,1)S(1)}, bf16[2,180,384]{2,0,1:T(2,128)(2,1)}, u32[]{:S(2)}) copy-start(bf16[2,180,384]{2,0,1:T(2,128)(2,1)} %param.37) | copy-start | bytes 829444
  7.8 9.8 %copy-start.13 = (bf16[2,4,96,96]{3,2,1,0:T(8,128)(2,1)S(1)}, bf16[2,4,96,96]{3,2,1,0:T(8,128)(2,1)}, u32[]{:S(2)}) copy-start(bf16[2,4,96,96]{3,2,1,0:T(8,128)(2,1)} %param.29) | copy-start | bytes 442372
  7.8 9.8 %copy-start.14 = (bf16[2,4,96,96]{3,2,1,0:T(8,128)(2,1)S(1)}, bf16[2,4,96,96]{3,2,1,0:T(8,128)(2,1)}, u32[]{:S(2)}) copy-start(bf16[2,4,96,96]{3,2,1,0:T(8,128)(2,1)} %param.27) | copy-start | bytes 442372
  7.8 24.9 %all-to-all-start = ((f32[16,24,384]{2,1,0:T(8,128)}), f32[16,24,384]{2,1,0:T(8,128)S(1)}, u32[]{:S(2)}, u32[]{:S(2)}) async-start(f32[16,24,384]{2,1,0:T(8,128)} %bitcast.29), calls=%async_computation | async-start | bytes 1179648 | tf_op jit(solution)/shard_map/all_to_all | solution.py:663
  32.8 0.8 copy-start.1
  33.6 10.2 %copy-start.21 = (f32[1536]{0:T(1024)S(1)}, f32[1536]{0:T(1024)}, u32[]{:S(2)}) copy-start(f32[1536]{0:T(1024)} %param.34) | copy-start | bytes 18436
  39.6 14.1 %all-to-all-start.1 = ((bf16[16,24,384]{2,1,0:T(8,128)(2,1)}), bf16[16,24,384]{2,1,0:T(8,128)(2,1)S(1)}, u32[]{:S(2)}, u32[]{:S(2)}) async-start(bf16[16,24,384]{2,1,0:T(8,128)(2,1)} %bitcast.32), calls=%async_computation.1 | async-start | bytes 589824 | tf_op jit(solution)/shard_map/all_to_all | solution.py:663
  56.1 17.9 %copy-start.18 = (s32[32]{0:T(128)S(1)}, s32[32]{0:T(128)}, u32[]{:S(2)}) copy-start(s32[32]{0:T(128)} %groups.3) | copy-start | bytes 388
  71.7 21.0 %collective-permute-start.1 = (bf16[2,384,512]{2,1,0:T(8,128)(2,1)}, bf16[2,384,512]{2,1,0:T(8,128)(2,1)S(1)}, u32[]{:S(2)}, u32[]{:S(2)}) collective-permute-start(bf16[2,384,512]{2,1,0:T(8,128)(2,1)} %get-tuple-element.99), channel_id=1, source_target_pairs={{0,2},{2,0},{4,6},{6,4},{8,10},{10,8},{12,14},{14,12},{16,18},{18,... | collective-permute-start | bytes 2359304 | tf_op jit(solution)/shard_map/ppermute | solution.py:587
  72.3 3.7 %collective-permute-start = (bf16[384,896]{1,0:T(8,128)(2,1)}, bf16[384,896]{1,0:T(8,128)(2,1)S(1)}, u32[]{:S(2)}, u32[]{:S(2)}) collective-permute-start(bf16[384,896]{1,0:T(8,128)(2,1)} %bitcast.35), channel_id=1, source_target_pairs={{0,1},{1,0},{2,3},{3,2},{4,5},{5,4},{6,7},{7,6},{8,9},{9,8},{10,11... | collective-permute-start | bytes 2064392 | tf_op jit(solution)/shard_map/ppermute | solution.py:767
  72.3 21.7 %collective-permute-start.2 = (bf16[2,384,512]{2,1,0:T(8,128)(2,1)}, bf16[2,384,512]{2,1,0:T(8,128)(2,1)}, u32[]{:S(2)}, u32[]{:S(2)}) collective-permute-start(bf16[2,384,512]{2,1,0:T(8,128)(2,1)} %get-tuple-element.101), channel_id=1, source_target_pairs={{0,4},{2,6},{4,0},{6,2},{8,12},{10,14},{12,8},{14,10},{16,20},{18,... | collective-permute-start | bytes 2359304 | tf_op jit(solution)/shard_map/ppermute | solution.py:587
  73.1 23.9 %collective-permute-start.3 = (bf16[2,384,512]{2,1,0:T(8,128)(2,1)}, bf16[2,384,512]{2,1,0:T(8,128)(2,1)}, u32[]{:S(2)}, u32[]{:S(2)}) collective-permute-start(bf16[2,384,512]{2,1,0:T(8,128)(2,1)} %get-tuple-element.103), channel_id=1, source_target_pairs={{0,8},{2,10},{4,12},{6,14},{8,0},{10,2},{12,4},{14,6},{16,24},{18,... | collective-permute-start | bytes 2359304 | tf_op jit(solution)/shard_map/ppermute | solution.py:587
  76.0 0.9 copy-start.9
  76.9 15.8 %copy-start.7 = (bf16[2,384,512]{2,1,0:T(8,128)(2,1)S(1)}, bf16[2,384,512]{2,1,0:T(8,128)(2,1)}, u32[]{:S(2)}) copy-start(bf16[2,384,512]{2,1,0:T(8,128)(2,1)} %get-tuple-element.98) | copy-start | bytes 2359300
  80.8 13.1 %copy-start.6 = (bf16[2,384,512]{2,1,0:T(8,128)(2,1)S(1)}, bf16[2,384,512]{2,1,0:T(8,128)(2,1)}, u32[]{:S(2)}) copy-start(bf16[2,384,512]{2,1,0:T(8,128)(2,1)} %get-tuple-element.100) | copy-start | bytes 2359300
  80.8 19.4 %all-to-all-start.2 = ((bf16[16,24,384]{2,1,0:T(8,128)(2,1)}), bf16[16,24,384]{2,1,0:T(8,128)(2,1)S(1)}, u32[]{:S(2)}, u32[]{:S(2)}) async-start(bf16[16,24,384]{2,1,0:T(8,128)(2,1)} %bitcast.31), calls=%async_computation.2 | async-start | bytes 589824 | tf_op jit(solution)/shard_map/all_to_all | solution.py:663
  92.7 15.6 %copy-start.8 = (bf16[2,384,512]{2,1,0:T(8,128)(2,1)}, bf16[2,384,512]{2,1,0:T(8,128)(2,1)S(1)}, u32[]{:S(2)}) copy-start(bf16[2,384,512]{2,1,0:T(8,128)(2,1)S(1)} %collective-permute-done.1) | copy-start | bytes 2359300
  92.7 4.2 %copy-start.5 = (bf16[2,384,512]{2,1,0:T(8,128)(2,1)S(1)}, bf16[2,384,512]{2,1,0:T(8,128)(2,1)}, u32[]{:S(2)}) copy-start(bf16[2,384,512]{2,1,0:T(8,128)(2,1)} %get-tuple-element.102) | copy-start | bytes 2359300
  93.6 14.7 %collective-permute-start.4 = (bf16[2,192,512]{2,1,0:T(8,128)(2,1)}, bf16[2,192,512]{2,1,0:T(8,128)(2,1)}, u32[]{:S(2)}, u32[]{:S(2)}) collective-permute-start(bf16[2,192,512]{2,1,0:T(8,128)(2,1)} %add_convert_fusion.2), channel_id=1, source_target_pairs={{0,4},{2,6},{4,0},{6,2},{8,12},{10,14},{12,8},{14,10},{16,20},{18,... | collective-permute-start | bytes 1179656 | tf_op jit(solution)/shard_map/ppermute | solution.py:587
  95.8 12.5 %collective-permute-start.5 = (bf16[2,192,512]{2,1,0:T(8,128)(2,1)}, bf16[2,192,512]{2,1,0:T(8,128)(2,1)}, u32[]{:S(2)}, u32[]{:S(2)}) collective-permute-start(bf16[2,192,512]{2,1,0:T(8,128)(2,1)} %add_convert_fusion.1), channel_id=1, source_target_pairs={{0,8},{2,10},{4,12},{6,14},{8,0},{10,2},{12,4},{14,6},{16,24},{18,... | collective-permute-start | bytes 1179656 | tf_op jit(solution)/shard_map/ppermute | solution.py:587
  98.8 10.4 %collective-permute-start.6 = (bf16[2,192,512]{2,1,0:T(8,128)(2,1)}, bf16[2,192,512]{2,1,0:T(8,128)(2,1)}, u32[]{:S(2)}, u32[]{:S(2)}) collective-permute-start(bf16[2,192,512]{2,1,0:T(8,128)(2,1)} %add_convert_fusion), channel_id=1, source_target_pairs={{0,2},{2,0},{4,6},{6,4},{8,10},{10,8},{12,14},{14,12},{16,18},{18,... | collective-permute-start | bytes 1179656 | tf_op jit(solution)/shard_map/ppermute | solution.py:587
  100.3 0.7 copy-start.4
  109.2 20.8 %all-to-all-start.3 = ((bf16[16,56,384]{2,1,0:T(8,128)(2,1)}), bf16[16,56,384]{2,1,0:T(8,128)(2,1)S(1)}, u32[]{:S(2)}, u32[]{:S(2)}) async-start(bf16[16,56,384]{2,1,0:T(8,128)(2,1)} %shard_map.323), calls=%async_computation.3 | async-start | bytes 1376256 | tf_op jit(solution)/shard_map/all_to_all | solution.py:823
  114.5 14.6 %collective-permute-start.7 = (bf16[2,96,512]{2,1,0:T(8,128)(2,1)S(1)}, bf16[2,96,512]{2,1,0:T(8,128)(2,1)S(1)}, u32[]{:S(2)}, u32[]{:S(2)}) collective-permute-start(bf16[2,96,512]{2,1,0:T(8,128)(2,1)S(1)} %get-tuple-element.153), channel_id=1, source_target_pairs={{0,8},{2,10},{4,12},{6,14},{8,0},{10,2},{12,4},{14,6},{16,24},{18,... | collective-permute-start | bytes 589832 | tf_op jit(solution)/shard_map/ppermute | solution.py:587
  117.9 4.4 %copy-start.11 = (bf16[2,180,384]{2,1,0:T(8,128)(2,1)S(1)}, bf16[2,180,384]{2,1,0:T(8,128)(2,1)}, u32[]{:S(2)}) copy-start(bf16[2,180,384]{2,1,0:T(8,128)(2,1)} %get-tuple-element.113) | copy-start | bytes 829444
  117.9 11.3 %collective-permute-start.8 = (bf16[2,96,512]{2,1,0:T(8,128)(2,1)S(1)}, bf16[2,96,512]{2,1,0:T(8,128)(2,1)S(1)}, u32[]{:S(2)}, u32[]{:S(2)}) collective-permute-start(bf16[2,96,512]{2,1,0:T(8,128)(2,1)S(1)} %get-tuple-element.151), channel_id=1, source_target_pairs={{0,2},{2,0},{4,6},{6,4},{8,10},{10,8},{12,14},{14,12},{16,18},{18,... | collective-permute-start | bytes 589832 | tf_op jit(solution)/shard_map/ppermute | solution.py:587
  120.8 8.4 %collective-permute-start.9 = (bf16[2,96,512]{2,1,0:T(8,128)(2,1)S(1)}, bf16[2,96,512]{2,1,0:T(8,128)(2,1)S(1)}, u32[]{:S(2)}, u32[]{:S(2)}) collective-permute-start(bf16[2,96,512]{2,1,0:T(8,128)(2,1)S(1)} %get-tuple-element.149), channel_id=1, source_target_pairs={{0,4},{2,6},{4,0},{6,2},{8,12},{10,14},{12,8},{14,10},{16,20},{18,... | collective-permute-start | bytes 589832 | tf_op jit(solution)/shard_map/ppermute | solution.py:587
  130.0 1.8 %copy-start = (bf16[16,56,384]{2,1,0:T(8,128)(2,1)}, bf16[16,56,384]{2,1,0:T(8,128)(2,1)S(1)}, u32[]{:S(2)}) copy-start(bf16[16,56,384]{2,1,0:T(8,128)(2,1)S(1)} %all-to-all-done.3.got) | copy-start | bytes 2064388
  130.0 18.4 %collective-permute-start.10 = (bf16[2,48,1536]{2,1,0:T(8,128)(2,1)S(1)}, bf16[2,48,1536]{2,1,0:T(8,128)(2,1)}, u32[]{:S(2)}, u32[]{:S(2)}) collective-permute-start(bf16[2,48,1536]{2,1,0:T(8,128)(2,1)S(1)} %pad_maximum_fusion), channel_id=1, source_target_pairs={{0,16},{2,18},{4,20},{6,22},{8,24},{10,26},{12,28},{14,30},{16,0},... | collective-permute-start | bytes 884744 | tf_op jit(solution)/shard_map/ppermute | solution.py:587
  135.2 13.6 %copy-start.2 = (f32[384,384]{1,0:T(8,128)S(1)}, f32[384,384]{1,0:T(8,128)}, u32[]{:S(2)}) copy-start(f32[384,384]{1,0:T(8,128)} %get-tuple-element.121.xh) | copy-start | bytes 1769476
  135.2 13.6 %copy-start.3 = (f32[384,384]{1,0:T(8,128)S(1)}, f32[384,384]{1,0:T(8,128)}, u32[]{:S(2)}) copy-start(f32[384,384]{1,0:T(8,128)} %get-tuple-element.115.dx1) | copy-start | bytes 1769476
  135.2 13.7 %copy-start.10 = (f32[384,384]{1,0:T(8,128)S(1)}, f32[384,384]{1,0:T(8,128)}, u32[]{:S(2)}) copy-start(f32[384,384]{1,0:T(8,128)} %get-tuple-element.128) | copy-start | bytes 1769476
  135.2 13.7 %copy-start.16 = (f32[384]{0:T(512)S(1)}, f32[384]{0:T(512)}, u32[]{:S(2)}) copy-start(f32[384]{0:T(512)} %gain.5) | copy-start | bytes 4612
  135.2 16.9 %all-to-all-start.4 = ((bf16[16,32,384]{2,1,0:T(8,128)(2,1)}), bf16[16,32,384]{2,1,0:T(8,128)(2,1)S(1)}, u32[]{:S(2)}, u32[]{:S(2)}) async-start(bf16[16,32,384]{2,1,0:T(8,128)(2,1)} %get-tuple-element.129), calls=%async_computation.4 | async-start | bytes 786432 | tf_op jit(solution)/shard_map/all_to_all | solution.py:849

commit v6 on v5

--- a/solution.py
+++ b/solution.py
@@ -5,7 +5,6 @@
 import jax.numpy as jnp
 import numpy as np
 from jax import lax
-from jax.experimental.layout import Layout, with_layout_constraint
 from jax.experimental import pallas as pl
 from jax.experimental.pallas import tpu as pltpu
 from jax.sharding import PartitionSpec as P
@@ -142,7 +141,7 @@
     return jnp.sum(values, axis=0, keepdims=True)
 
 
-def norm_one_kernel(columns, padded, groups, all_ref, gain, bias, high, low, freq, xh, inverse, pad, tables, sems):
+def norm_one_kernel(columns, padded, groups, all_ref, gain, bias, high, low, freq, pad, tables, sems):
     mp, rows_dev = all_ref.shape[0], all_ref.shape[1]
     width = mp * all_ref.shape[3]
     choice = width_choice(groups, rows_dev)
@@ -165,8 +164,6 @@
     x = pad[lax.axis_index("mp")]
     hat = (x - average) * inv
     u = hat * gain[...] + bias[...]
-    xh[...] = hat
-    inverse[...] = inv
     for copy in copies:
         copy.wait()
     freq[...] = times((tables[0], tables[1]), u)
@@ -282,7 +279,7 @@
     return jnp.where(lane == target, 1.0, 0.0).astype(BF)
 
 
-def cotangent_kernel(columns, padded, dy_all, places, field_all, vectors, dyt, dy_s, base, pad):
+def cotangent_kernel(columns, padded, dy_all, places, field_all, vectors, dyt, dy_s, base, xh, inverse, pad):
     mp, rows_dev, ch = dy_all.shape[0], dy_all.shape[1], dy_all.shape[3]
 
     for m in range(mp):
@@ -296,6 +293,8 @@
         for r in range(rows_dev):
             base[m, r * padded : r * padded + columns, :] = field_all[m, r].astype(F32)
     average, inv = second_norm([base[m] for m in range(mp)])
+    inverse[...] = inv
+    xh[...] = (base[lax.axis_index("mp")] - average) * inv
     for m in range(mp):
         x = base[m]
         base[m] = x + (x - average) * inv * vectors[m, 0:1, :] + vectors[m, 1:2, :]
@@ -328,9 +327,6 @@
         move.start(base_h, base),
     ]
     spans = [slice(p * chunk, (p + 1) * chunk) for p in range(pieces)]
-    swap = swap_matrix(places)
-    for copy in first:
-        copy.wait()
     load_dy = move.start(dy_h, dy)
     loads = [
         (
@@ -340,8 +336,12 @@
         for span in spans
     ]
     load_dyt = move.start(dyt_h, dyt)
+    swap = swap_matrix(places)
+    for copy in first[:3]:
+        copy.wait()
     every = jnp.concatenate([eo[m] for m in range(mp)], axis=1)
     filtered = mm_t(table[0], every) + mm_t(table[1], every)
+    first[3].wait()
     for m in range(mp):
         base[m] = base[m] + filtered[:, m * ch : (m + 1) * ch]
     move.store(base.at[mine], own_h)
@@ -386,9 +386,9 @@
         lanes = slice(m * ch, (m + 1) * ch)
 
         def put(ref):
-            ref[:, :ch] = out[:, lanes].astype(BF)
-            ref[:, ch : 2 * ch] = dn[:, lanes].astype(BF)
-            ref[:, 2 * ch :] = stat
+            ref[:, :ch] = dn[:, lanes].astype(BF)
+            ref[:, ch : ch + 128] = stat
+            ref[:, ch + 128 :] = out[:, lanes].astype(BF)
 
         @pl.when(mine == m)
         def _():
@@ -420,26 +420,24 @@
     move.finish()
 
 
-def back_mix_kernel(columns, padded, width, choice, dy, gain, bias2, high, low, norm_in, own, *refs):
-    got, (out_field, dx1, freq, sums, pad) = refs[:-5], refs[-5:]
+def back_mix_kernel(columns, padded, width, choice, dy, gain, high, low, norm_in, own, *refs):
+    got, (dx1, freq, sums, pad) = refs[:-4], refs[-4:]
     ch, rows_dev = own.shape[1], dy.shape[1]
     mine = lax.axis_index("mp")
     x1 = own[...]
     average, inv = norm_in[:, 0:1], norm_in[:, 1:2]
     hat = (x1 - average) * inv
-    total = sum(piece[...].astype(F32) for piece in got)
-    out = x1 + total[:, :ch] + bias2[...]
-    dn = total[:, ch : 2 * ch]
+    total = sum(piece[:, : ch + 128].astype(F32) for piece in got)
+    dn = total[:, :ch]
     pad[...] = jnp.zeros_like(pad)
     for r in range(rows_dev):
-        out_field[r] = out[r * padded : r * padded + columns, :].astype(BF)
         put_rows(pad, dy[mine, r].astype(F32), r, padded)
     grad = pad[...]
     sums[0:1, :] = column_sum(dn * hat)
     sums[1:2, :] = column_sum(dn)
     sums[2:3, :] = column_sum(grad)
     sums[3:8, :] = jnp.zeros((5, ch), F32)
-    stats = total[:, 2 * ch : 2 * ch + 128]
+    stats = total[:, ch:]
     plain = (stats[:, 0:1] + stats[:, 1:2] + stats[:, 2:3]) / width
     cross = (stats[:, 3:4] + stats[:, 4:5] + stats[:, 5:6]) / width
     grad = grad + inv * (dn * gain[...] - plain - hat * cross)
@@ -544,7 +542,7 @@
     return pl.BlockSpec(shape, lambda *_: (0,) * len(shape))
 
 
-def run(kernel, outs, args, scratch=(), picked=(), choice=None, flops=0, limit=56):
+def run(kernel, outs, args, scratch=(), picked=(), choice=None, flops=0, limit=56, narrow=(), lanes=0):
     moved = sum(math.prod(a.shape) * a.dtype.itemsize for a in args)
     moved += sum(math.prod(o.shape) * o.dtype.itemsize for o in outs)
     params = pltpu.CompilerParams(vmem_limit_bytes=limit * 2**20)
@@ -561,7 +559,9 @@
             cost_estimate=cost,
         )(*args)
     specs = [
-        pl.BlockSpec((1, *a.shape[1:]), lambda i, c: (c[0], 0, 0)) if i in picked else whole(a.shape)
+        pl.BlockSpec((1, *a.shape[1:]), lambda i, c: (c[0], 0, 0))
+        if i in picked
+        else whole((a.shape[0], lanes) if i in narrow else a.shape)
         for i, a in enumerate(args)
     ]
     return pl.pallas_call(
@@ -644,13 +644,13 @@
 
     field_all = lax.all_gather(field, "mp", axis=0)
     table = pltpu.VMEM((2, patches, tokens), BF)
-    freq, xh1, inv1 = pl.pallas_call(
+    (freq,) = pl.pallas_call(
         functools.partial(norm_one_kernel, columns, padded),
-        out_shape=[f32(patches, ch), f32(tokens, ch), f32(tokens, 1)],
+        out_shape=[f32(patches, ch)],
         in_specs=[pl.BlockSpec(memory_space=pltpu.SMEM)]
         + [pl.BlockSpec(memory_space=pltpu.VMEM)] * 3
         + [pl.BlockSpec(memory_space=pl.ANY)] * 2,
-        out_specs=[pl.BlockSpec(memory_space=pltpu.VMEM)] * 3,
+        out_specs=[pl.BlockSpec(memory_space=pltpu.VMEM)],
         scratch_shapes=[
             pltpu.VMEM((mp, tokens, ch), F32),
             table,
@@ -705,9 +705,15 @@
     places = np.stack(
         [np.arange(full_width) // share_rows, np.arange(full_width) % share_rows], axis=1
     ).astype(np.int32)
-    dyt, dy_pad, base = run(
+    dyt, dy_pad, base, xh1, inv1 = run(
         functools.partial(cotangent_kernel, columns, padded),
-        [bf(full_width, tokens), bf(tokens, full_width), f32(mp, tokens, ch)],
+        [
+            bf(full_width, tokens),
+            bf(tokens, full_width),
+            f32(mp, tokens, ch),
+            f32(tokens, ch),
+            f32(tokens, 1),
+        ],
         [dy_all, jnp.asarray(places), field_all, vectors_all],
         [pltpu.VMEM((tokens, ch), F32)],
     )
@@ -777,22 +783,15 @@
     streams = [[*terms, part] for terms, part in zip(streams, got_rows)]
     away = [added(terms, rows_each, 2 * rows_each).astype(BF) for terms in streams]
 
-    out_field, dx1, dfreq, sums2 = run(
+    dx1, dfreq, sums2 = run(
         functools.partial(back_mix_kernel, columns, padded, full_width),
-        [bf(rows_dev, columns, ch), f32(tokens, ch), bf(patches, ch), f32(8, ch)],
-        [
-            dy_all,
-            norm2_gain,
-            fc2_bias,
-            *lon,
-            norm2,
-            x1,
-            kept_send,
-            *got,
-        ],
+        [f32(tokens, ch), bf(patches, ch), f32(8, ch)],
+        [dy_all, norm2_gain, *lon, norm2, x1, kept_send, *got],
         [pltpu.VMEM((tokens, ch), F32)],
-        (3, 4),
+        (2, 3),
         choice,
+        narrow=range(6, 6 + mp),
+        lanes=ch + 128 if ch % 128 == 0 else send_lanes,
     )
 
     dz = to_other(dfreq, group).reshape(patches, ch)
@@ -809,9 +808,13 @@
             pltpu.VMEM((4 * size, ch), F32),
             pltpu.VMEM((max(parts, 16), ch), F32),
         ],
-    )
-    sent, got_rows, out_field = lax.optimization_barrier((sent, got_rows, out_field))
-    out_field = with_layout_constraint(out_field, Layout(major_to_minor=(1, 0, 2)))
+        limit=53,
+    )
+    sent, got_rows, (x1, halves) = lax.optimization_barrier(
+        (sent, got_rows, (x1, [kept_send, *got]))
+    )
+    out_field = x1 + sum(part[:, ch + 128 :].astype(F32) for part in halves) + fc2_bias
+    out_field = out_field.astype(BF).reshape(rows_dev, padded, ch)[:, :columns]
     streams = [[*terms, part] for terms, part in zip(streams, got_rows)]
     half = rows_each // 2
     kept = [added(terms, 0, half) for terms in streams]

time: 154 us -> 153 us (level)
  waiting for transfers between devices: 30.1 us -> 28.4 us
    ppermute x10, waiting for transfers between devices: 18.8 us -> 17.1 us  [swapped(): return lax.ppermute(away, 'lat', [(d, d ^ bit) for d in range(parts)])]
    unnamed x55 -> x59, local copies, waits for them, and re-layouts: 4.6 us -> 3.9 us
  transfers between devices with their start and end apart: 16 -> 16, of which waited for: 7 -> 8; matrix products, arithmetic and copies ran while one was open for 12% -> 13% of each run, Pallas kernels for 14% -> 14%
where the time goes in v6:
time: 153 us; the launch traced here: 152 us
  Pallas kernels  46.8 us (31%)
  starting transfers between devices  37.8 us (25%)
  waiting for transfers between devices  28.4 us (19%)
  blocking collectives  13.8 us (9%)
  other arithmetic  13.3 us (9%)
  local copies, waits for them, and re-layouts  9.55 us (6%)
  between operations  2.49 us (2%)
    ppermute x10, waiting for transfers between devices, swapped(): return lax.ppermute(away, 'lat', [(d, d ^ bit) for d in range(parts)])  17.1 us
    all_to_all x3, starting transfers between devices, to_other(): lax.all_to_all(values.reshape(parts, rows_each, ch), 'lat', 0, 0, tiled=T...  17 us
    pallas_call x1, Pallas kernels, body(): pl.pallas_call(functools.partial(mlp_kernel, orders, rows_dev), out_shape...  15.2 us
    pallas_call x4, Pallas kernels, run(): pl.pallas_call(kernel, out_shape=out_shape, in_specs=[pl.BlockSpec(memory...  15 us
    ppermute x10, starting transfers between devices, swapped(): return lax.ppermute(away, 'lat', [(d, d ^ bit) for d in range(parts)])  12.9 us
    all_to_all x3, waiting for transfers between devices, to_other(): lax.all_to_all(values.reshape(parts, rows_each, ch), 'lat', 0, 0, tiled=T...  10.2 us
    pallas_call x2, Pallas kernels, run(): pl.pallas_call(kernel, out_shape=out_shape, grid_spec=pltpu.PrefetchScala...  6.97 us
    pallas_call x1, Pallas kernels, body(): pl.pallas_call(functools.partial(filter_kernel, blocks, size), out_shape=...  5.99 us
  transfers between devices with their start and end apart: 16, of which 8 were waited for; matrix products, arithmetic and copies ran while one was open for 13% of the time, Pallas kernels for 14%

profile of v6, /device:TPU:0, one launch (start us, length us, event | category | flops | bytes accessed | tf_op | source)
XLA Modules:
  0.0 152.1 jit_solution(14687237124434888278)
XLA Ops:
  0.6 1.0 copy.53
  1.6 2.4 %all-gather = bf16[4,180,384]{2,1,0:T(8,128)(2,1)} all-gather(bf16[2,180,384]{2,1,0:T(8,128)(2,1)S(1)} %copy.53), channel_id=2, replica_groups=mesh['lat'=16,'mp'=2] {'mp'}, dimensions={0}, use_global_device_ids=true | all-gather | bytes 829440 | tf_op jit(solution)/shard_map/all_gather | solution.py:645
  4.1 3.6 %shard_map.317 = f32[384,384]{1,0:T(8,128)} custom-call(s32[32]{0:T(128)} %groups.3, bf16[2,2,180,384]{3,2,1,0:T(8,128)(2,1)} %bitcast.25, f32[384]{0:T(512)} %gain.5, f32[384]{0:T(512)} %bias.1, bf16[4,384,384]{2,1,0:T(8,128)(2,1)} %constant.66.clone.high.high_h, bf16[4,384,384]{2,1,0:T(8,128)(2,1)} %constant.67.clone.low.low_h), custom_call_target="tpu_custom_call" | custom-call | tf_op jit(solution)/shard_map/pallas_call | solution.py:647
  7.8 8.4 %all-to-all-start = ((f32[16,24,384]{2,1,0:T(8,128)}), f32[16,24,384]{2,1,0:T(8,128)S(1)}, u32[]{:S(2)}, u32[]{:S(2)}) async-start(f32[16,24,384]{2,1,0:T(8,128)} %bitcast.28), calls=%async_computation | async-start | bytes 1179648 | tf_op jit(solution)/shard_map/all_to_all | solution.py:663
  16.3 0.1 fusion.11
  16.7 0.1 copy.55
  16.8 0.7 sub.27.keep
  17.6 0.1 maximum_bitcast_fusion
  17.7 0.2 copy.57
  17.9 1.0 reshape.165.weights
  18.9 0.2 fusion.3
  19.2 0.3 select_multiply_fusion.1
  19.5 0.7 pad_maximum_fusion.1.tables
  20.2 2.6 %shard_map.318 = (bf16[768,384]{1,0:T(8,128)(2,1)}, bf16[768,384]{1,0:T(8,128)(2,1)}) custom-call(f32[32,64]{1,0:T(8,128)} %pad_maximum_fusion.1.tables, bf16[192,32]{1,0:T(8,128)(2,1)} %constant.68.clone.left, bf16[4,64,384]{2,1,0:T(8,128)(2,1)} %constant.69.clone.right, bf16[192,384]{1,0:T(8,128)(2,1)} %constant.70.clone.same, f32[192,1]{1,0:T(8,128)} %sub.27.keep), custom_call_target="tpu_custom_call" | custom-call | bytes 1544960 | tf_op jit(solution)/shard_map/pallas_call | solution.py:552
  22.8 1.9 %all_gather.23.vectors = f32[2,4,384]{2,1,0:T(4,128)} all-gather(f32[1,4,384]{2,1,0:T(4,128)S(1)} %all_gather_reshape.3), channel_id=1, replica_groups=mesh['lat'=16,'mp'=2] {'mp'}, dimensions={0}, use_global_device_ids=true | all-gather | bytes 18432 | tf_op jit(solution)/shard_map/all_gather | solution.py:684
  24.7 0.6 pad_maximum_fusion.3.biases
  25.3 2.3 %all-gather.1 = bf16[4,180,384]{2,1,0:T(8,128)(2,1)} all-gather(bf16[2,180,384]{2,1,0:T(8,128)(2,1)S(1)} %copy.54), channel_id=3, replica_groups=mesh['lat'=16,'mp'=2] {'mp'}, dimensions={0}, use_global_device_ids=true | all-gather | bytes 829440 | tf_op jit(solution)/shard_map/all_gather | solution.py:685
  27.7 5.1 %all-to-all-done = f32[16,24,384]{2,1,0:T(8,128)S(1)} async-done(((f32[16,24,384]{2,1,0:T(8,128)}), f32[16,24,384]{2,1,0:T(8,128)S(1)}, u32[]{:S(2)}, u32[]{:S(2)}) %all-to-all-start) | async-done | bytes 589856 | tf_op jit(solution)/shard_map/all_to_all | solution.py:663
  32.8 0.8 copy-done.5
  33.6 6.0 %shard_map.319 = (bf16[384,384]{1,0:T(8,128)(2,1)}, bf16[384,768]{1,0:T(8,128)(2,1)}, bf16[384,768]{1,0:T(8,128)(2,1)}, f32[384,768]{1,0:T(8,128)}, f32[384,768]{1,0:T(8,128)}) custom-call(f32[384,384]{1,0:T(8,128)} %bitcast.27, bf16[768,384]{1,0:T(8,128)(2,1)} %get-tuple-element.82.high, bf16[768,384]{1,0:T(8,128)(2,1)} %get-tuple-element.83.low, ...), custom_call_target="tpu_custom_call" | custom-call | tf_op jit(solution)/shard_map/pallas_call | solution.py:690
  39.6 4.2 %all-to-all-start.1 = ((bf16[16,24,384]{2,1,0:T(8,128)(2,1)}), bf16[16,24,384]{2,1,0:T(8,128)(2,1)S(1)}, u32[]{:S(2)}, u32[]{:S(2)}) async-start(bf16[16,24,384]{2,1,0:T(8,128)(2,1)} %bitcast.34), calls=%async_computation.1 | async-start | bytes 589824 | tf_op jit(solution)/shard_map/all_to_all | solution.py:663
  43.8 0.6 reshape.164.b1
  44.4 4.1 %shard_map.320 = (bf16[768,384]{1,0:T(8,128)(2,1)}, bf16[384,768]{1,0:T(8,128)(2,1)}, f32[2,384,384]{2,1,0:T(8,128)}, f32[384,384]{1,0:T(8,128)}, f32[384,1]{1,0:T(8,128)}) custom-call(bf16[2,2,180,384]{3,2,1,0:T(8,128)(2,1)} %bitcast.23, s32[768,2]{1,0:T(8,128)} %constant.71.clone.places, bf16[2,2,180,384]{3,2,1,0:T(8,128)(2,1)} %bitcast.26, ...), custom_call_target="tpu_custom_call" | custom-call | bytes 4075008 | tf_op jit(solution)/shard_map/pallas_call | solution.py:552
  48.5 5.2 %all-to-all-done.1 = bf16[16,24,384]{2,1,0:T(8,128)(2,1)S(1)} async-done(((bf16[16,24,384]{2,1,0:T(8,128)(2,1)}), bf16[16,24,384]{2,1,0:T(8,128)(2,1)S(1)}, u32[]{:S(2)}, u32[]{:S(2)}) %all-to-all-start.1) | async-done | bytes 294944 | tf_op jit(solution)/shard_map/all_to_all | solution.py:663
  53.6 2.5 %all-gather.2 = bf16[768,384]{1,0:T(8,128)(2,1)} all-gather(bf16[384,384]{1,0:T(8,128)(2,1)S(1)} %bitcast.30), channel_id=4, replica_groups=mesh['lat'=16,'mp'=2] {'mp'}, dimensions={0}, use_global_device_ids=true | all-gather | bytes 884736 | tf_op jit(solution)/shard_map/all_gather | solution.py:722
  56.2 15.2 %shard_map.321 = (bf16[384,896]{1,0:T(8,128)(2,1)}, bf16[1,384,896]{2,1,0:T(8,128)(2,1)}, f32[1,1536]{1,0:T(1,128)}, f32[384,2]{1,0:T(8,128)}, f32[384,384]{1,0:...) custom-call(s32[32]{0:T(128)} %groups.3, ...), custom_call_target="tpu_custom_call" | custom-call | flops 4529848320 | bytes 16777216 | tf_op jit(solution)/shard_map/pallas_call | solution.py:726
  71.4 0.6 collective-permute-start.1
  72.1 0.8 collective-permute-start.2
  72.8 1.0 collective-permute-start.3
  73.9 0.6 fusion.15
  75.8 0.8 copy-done.8
  76.6 3.6 %shard_map.322 = (f32[384,384]{1,0:T(8,128)}, bf16[384,384]{1,0:T(8,128)(2,1)}, f32[8,384]{1,0:T(8,128)}) custom-call(s32[1]{0:T(128)S(6)} %add.126.choice, bf16[2,2,180,384]{3,2,1,0:T(8,128)(2,1)} %bitcast.24, f32[384]{0:T(512)} %gain.4, bf16[4,384,384]{2,1,0:T(8,128)(2,1)} %constant.66.clone.high.high_h, bf16[4,384,384]{2,1,0:T(8,128)(2,1)} %constant.67.clone.low.low_h, ...), custom_call_target="tpu_custom_call" | custom-call | bytes 5779968 | tf_op jit(solution)/shard_map/pallas_call | solution.py:567
  80.2 4.4 %all-to-all-start.2 = ((bf16[16,24,384]{2,1,0:T(8,128)(2,1)}), bf16[16,24,384]{2,1,0:T(8,128)(2,1)S(1)}, u32[]{:S(2)}, u32[]{:S(2)}) async-start(bf16[16,24,384]{2,1,0:T(8,128)(2,1)} %bitcast.33), calls=%async_computation.2 | async-start | bytes 589824 | tf_op jit(solution)/shard_map/all_to_all | solution.py:663
  84.6 8.0 %collective-permute-done.1 = bf16[2,384,512]{2,1,0:T(8,128)(2,1)} collective-permute-done((bf16[2,384,512]{2,1,0:T(8,128)(2,1)}, bf16[2,384,512]{2,1,0:T(8,128)(2,1)}, u32[]{:S(2)}, u32[]{:S(2)}) %collective-permute-start.1) | collective-permute-done | bytes 786464 | tf_op jit(solution)/shard_map/ppermute | solution.py:587
  92.6 1.9 %add_convert_fusion.2 = bf16[2,192,512]{2,1,0:T(8,128)(2,1)} fusion(bf16[2,384,512]{2,1,0:T(8,128)(2,1)} %collective-permute-done.1, bf16[2,384,512]{2,1,0:T(8,128)(2,1)S(1)} %copy-done.11), kind=kLoop, calls=%fused_computation.2 | loop fusion | flops 786432 | bytes 1179648 | tf_op jit(solution)/shard_map/convert_element_type | solution.py:784
  94.5 0.8 collective-permute-start.4
  95.3 1.9 %add_convert_fusion.1 = bf16[2,192,512]{2,1,0:T(8,128)(2,1)} fusion(bf16[2,384,512]{2,1,0:T(8,128)(2,1)} %collective-permute-done.2, bf16[2,384,512]{2,1,0:T(8,128)(2,1)S(1)} %copy-done.10), kind=kLoop, calls=%fused_computation.1 | loop fusion | flops 786432 | bytes 1179648 | tf_op jit(solution)/shard_map/convert_element_type | solution.py:784
  97.2 1.0 collective-permute-start.5
  98.1 1.8 %add_convert_fusion = bf16[2,192,512]{2,1,0:T(8,128)(2,1)} fusion(bf16[2,384,512]{2,1,0:T(8,128)(2,1)} %collective-permute-done.3, bf16[2,384,512]{2,1,0:T(8,128)(2,1)S(1)} %copy-done.9), kind=kLoop, calls=%fused_computation | loop fusion | flops 786432 | bytes 1179648 | tf_op jit(solution)/shard_map/convert_element_type | solution.py:784
  100.0 0.6 collective-permute-start.6
  100.6 7.1 %shard_map.323 = bf16[16,56,384]{2,1,0:T(8,128)(2,1)} custom-call(bf16[384,384]{1,0:T(8,128)(2,1)S(1)} %bitcast.22, bf16[768,384]{1,0:T(8,128)(2,1)} %get-tuple-element.82.high, bf16[768,384]{1,0:T(8,128)(2,1)} %get-tuple-element.83.low, bf16[4,96,384]{2,1,0:T(8,128)(2,1)S(1)} %copy-done, bf16[384,768]{1,0:T(8,128)(2,1)} %get-tuple-element.104.s_ref, ...), custom_call_target="tpu_custom_call" | custom-call | bytes 6014976 | tf_op jit(solution)/shard_map/pallas_call | solution.py:552
  107.7 1.4 collective-permute-done.6
  109.1 4.2 %all-to-all-start.3 = ((bf16[16,56,384]{2,1,0:T(8,128)(2,1)}), bf16[16,56,384]{2,1,0:T(8,128)(2,1)S(1)}, u32[]{:S(2)}, u32[]{:S(2)}) async-start(bf16[16,56,384]{2,1,0:T(8,128)(2,1)} %shard_map.323), calls=%async_computation.3 | async-start | bytes 1376256 | tf_op jit(solution)/shard_map/all_to_all | solution.py:826
  113.3 1.4 add_convert_fusion.6
  114.7 2.0 %collective-permute-start.7 = (bf16[2,96,512]{2,1,0:T(8,128)(2,1)S(1)}, bf16[2,96,512]{2,1,0:T(8,128)(2,1)S(1)}, u32[]{:S(2)}, u32[]{:S(2)}) collective-permute-start(bf16[2,96,512]{2,1,0:T(8,128)(2,1)S(1)} %get-tuple-element.153), channel_id=1, source_target_pairs={{0,8},{2,10},{4,12},{6,14},{8,0},{10,2},{12,4},{14,6},{16,24},{18,... | collective-permute-start | bytes 589832 | tf_op jit(solution)/shard_map/ppermute | solution.py:587
  116.6 1.4 add_convert_fusion.5
  118.0 1.5 %collective-permute-start.8 = (bf16[2,96,512]{2,1,0:T(8,128)(2,1)S(1)}, bf16[2,96,512]{2,1,0:T(8,128)(2,1)S(1)}, u32[]{:S(2)}, u32[]{:S(2)}) collective-permute-start(bf16[2,96,512]{2,1,0:T(8,128)(2,1)S(1)} %get-tuple-element.151), channel_id=1, source_target_pairs={{0,2},{2,0},{4,6},{6,4},{8,10},{10,8},{12,14},{14,12},{16,18},{18,... | collective-permute-start | bytes 589832 | tf_op jit(solution)/shard_map/ppermute | solution.py:587
  119.6 1.2 add_convert_fusion.4
  120.7 1.5 %collective-permute-start.9 = (bf16[2,96,512]{2,1,0:T(8,128)(2,1)S(1)}, bf16[2,96,512]{2,1,0:T(8,128)(2,1)S(1)}, u32[]{:S(2)}, u32[]{:S(2)}) collective-permute-start(bf16[2,96,512]{2,1,0:T(8,128)(2,1)S(1)} %get-tuple-element.149), channel_id=1, source_target_pairs={{0,4},{2,6},{4,0},{6,2},{8,12},{10,14},{12,8},{14,10},{16,20},{18,... | collective-permute-start | bytes 589832 | tf_op jit(solution)/shard_map/ppermute | solution.py:587
  122.3 1.2 add_convert_fusion.3
  123.5 0.9 copy.60
  124.4 4.1 %collective-permute-done.7 = bf16[2,96,512]{2,1,0:T(8,128)(2,1)S(1)} collective-permute-done((bf16[2,96,512]{2,1,0:T(8,128)(2,1)S(1)}, bf16[2,96,512]{2,1,0:T(8,128)(2,1)S(1)}, u32[]{:S(2)}, u32[]{:S(2)}) %collective-permute-start.7) | collective-permute-done | bytes 196640 | tf_op jit(solution)/shard_map/ppermute | solution.py:587
  128.7 0.7 all-to-all-done.3.got
  129.4 3.2 %collective-permute-start.10 = (bf16[2,48,1536]{2,1,0:T(8,128)(2,1)S(1)}, bf16[2,48,1536]{2,1,0:T(8,128)(2,1)S(1)}, u32[]{:S(2)}, u32[]{:S(2)}) collective-permute-start(bf16[2,48,1536]{2,1,0:T(8,128)(2,1)S(1)} %pad_maximum_fusion), channel_id=1, source_target_pairs={{0,16},{2,18},{4,20},{6,22},{8,24},{10,26},{12,28},{14,30},{16,0},... | collective-permute-start | bytes 884744 | tf_op jit(solution)/shard_map/ppermute | solution.py:587
  132.6 3.4 %shard_map.324 = (f32[384,384]{1,0:T(8,128)}, f32[384,3]{1,0:T(8,128)}, bf16[16,32,384]{2,1,0:T(8,128)(2,1)}) custom-call(s32[1]{0:T(128)S(6)} %add.126.choice, bf16[16,56,384]{2,1,0:T(8,128)(2,1)} %copy-done.3, bf16[4,384,384]{2,1,0:T(8,128)(2,1)} %constant.66.clone.high.high_h, bf16[4,384,384]{2,1,0:T(8,128)(2,1)} %constant.67.clone.low.low_h, ...), custom_call_target="tpu_custom_call" | custom-call | bytes 5217792 | tf_op jit(solution)/shard_map/pallas_call | solution.py:567
  136.0 3.7 %all-to-all-start.4 = ((bf16[16,32,384]{2,1,0:T(8,128)(2,1)}), bf16[16,32,384]{2,1,0:T(8,128)(2,1)S(1)}, u32[]{:S(2)}, u32[]{:S(2)}) async-start(bf16[16,32,384]{2,1,0:T(8,128)(2,1)} %get-tuple-element.129), calls=%async_computation.4 | async-start | bytes 786432 | tf_op jit(solution)/shard_map/all_to_all | solution.py:852
  139.8 4.6 %psum.7 = f32[384,3]{1,0:T(8,128)S(1)} all-reduce(f32[384,3]{1,0:T(8,128)} %get-tuple-element.123), channel_id=1, replica_groups=mesh['lat'=16,'mp'=2] {'mp'}, use_global_device_ids=true, to_apply=%region_4.5 | all-reduce | flops 1152 | bytes 9216 | tf_op jit(solution)/shard_map/psum | solution.py:844
  144.4 3.6 %collective-permute-done.10 = bf16[2,48,1536]{2,1,0:T(8,128)(2,1)S(1)} collective-permute-done((bf16[2,48,1536]{2,1,0:T(8,128)(2,1)S(1)}, bf16[2,48,1536]{2,1,0:T(8,128)(2,1)S(1)}, u32[]{:S(2)}, u32[]{:S(2)}) %collective-permute-start.10) | collective-permute-done | bytes 294944 | tf_op jit(solution)/shard_map/ppermute | solution.py:587
  148.0 0.4 slice_reduce_fusion.2
  148.4 0.2 multiply_add_fusion
  148.7 1.1 copy.61
  149.8 0.8 slice_bitcast_fusion
  150.7 0.4 all-to-all-done.4.tail
  151.1 1.1 shard_map.325
  (84 shorter events, 0.9 us)
Async XLA Ops:
  7.7 8.5 %copy-start.18 = (s32[32]{0:T(128)S(1)}, s32[32]{0:T(128)}, u32[]{:S(2)}) copy-start(s32[32]{0:T(128)} %groups.3) | copy-start | bytes 388
  7.7 8.6 %copy-start.26 = (s32[32]{0:T(128)S(1)}, s32[32]{0:T(128)}, u32[]{:S(2)}) copy-start(s32[32]{0:T(128)} %param.24) | copy-start | bytes 388
  7.7 8.7 %copy-start.23 = (f32[2,4,96]{2,1,0:T(4,128)S(1)}, f32[2,4,96]{2,1,0:T(4,128)}, u32[]{:S(2)}) copy-start(f32[2,4,96]{2,1,0:T(4,128)} %param.28) | copy-start | bytes 9220
  7.7 8.7 %copy-start.24 = (f32[2,4,96]{2,1,0:T(4,128)S(1)}, f32[2,4,96]{2,1,0:T(4,128)}, u32[]{:S(2)}) copy-start(f32[2,4,96]{2,1,0:T(4,128)} %param.30) | copy-start | bytes 9220
  7.7 8.8 %copy-start.16 = (f32[384]{0:T(512)S(1)}, f32[384]{0:T(512)}, u32[]{:S(2)}) copy-start(f32[384]{0:T(512)} %gain.5) | copy-start | bytes 4612
  7.8 8.8 %copy-start.20 = (f32[384]{0:T(512)S(1)}, f32[384]{0:T(512)}, u32[]{:S(2)}) copy-start(f32[384]{0:T(512)} %gain.4) | copy-start | bytes 4612
  7.8 8.8 %copy-start.21 = (f32[384]{0:T(512)S(1)}, f32[384]{0:T(512)}, u32[]{:S(2)}) copy-start(f32[384]{0:T(512)} %bias.1) | copy-start | bytes 4612
  7.8 8.8 %copy-start.27 = (f32[384]{0:T(512)S(1)}, f32[384]{0:T(512)}, u32[]{:S(2)}) copy-start(f32[384]{0:T(512)} %param.32) | copy-start | bytes 4612
  7.8 9.7 %copy-start.13 = (bf16[2,180,384]{2,0,1:T(2,128)(2,1)S(1)}, bf16[2,180,384]{2,0,1:T(2,128)(2,1)}, u32[]{:S(2)}) copy-start(bf16[2,180,384]{2,0,1:T(2,128)(2,1)} %param.37) | copy-start | bytes 829444
  7.8 9.8 %copy-start.14 = (bf16[2,4,96,96]{3,2,1,0:T(8,128)(2,1)S(1)}, bf16[2,4,96,96]{3,2,1,0:T(8,128)(2,1)}, u32[]{:S(2)}) copy-start(bf16[2,4,96,96]{3,2,1,0:T(8,128)(2,1)} %param.29) | copy-start | bytes 442372
  7.8 9.8 %copy-start.15 = (bf16[2,4,96,96]{3,2,1,0:T(8,128)(2,1)S(1)}, bf16[2,4,96,96]{3,2,1,0:T(8,128)(2,1)}, u32[]{:S(2)}) copy-start(bf16[2,4,96,96]{3,2,1,0:T(8,128)(2,1)} %param.27) | copy-start | bytes 442372
  7.8 24.9 %all-to-all-start = ((f32[16,24,384]{2,1,0:T(8,128)}), f32[16,24,384]{2,1,0:T(8,128)S(1)}, u32[]{:S(2)}, u32[]{:S(2)}) async-start(f32[16,24,384]{2,1,0:T(8,128)} %bitcast.28), calls=%async_computation | async-start | bytes 1179648 | tf_op jit(solution)/shard_map/all_to_all | solution.py:663
  32.8 0.8 copy-start.5
  33.6 10.2 %copy-start.22 = (f32[1536]{0:T(1024)S(1)}, f32[1536]{0:T(1024)}, u32[]{:S(2)}) copy-start(f32[1536]{0:T(1024)} %param.34) | copy-start | bytes 18436
  39.6 14.1 %all-to-all-start.1 = ((bf16[16,24,384]{2,1,0:T(8,128)(2,1)}), bf16[16,24,384]{2,1,0:T(8,128)(2,1)S(1)}, u32[]{:S(2)}, u32[]{:S(2)}) async-start(bf16[16,24,384]{2,1,0:T(8,128)(2,1)} %bitcast.34), calls=%async_computation.1 | async-start | bytes 589824 | tf_op jit(solution)/shard_map/all_to_all | solution.py:663
  56.2 17.6 %copy-start.19 = (s32[32]{0:T(128)S(1)}, s32[32]{0:T(128)}, u32[]{:S(2)}) copy-start(s32[32]{0:T(128)} %groups.3) | copy-start | bytes 388
  71.4 21.2 %collective-permute-start.1 = (bf16[2,384,512]{2,1,0:T(8,128)(2,1)}, bf16[2,384,512]{2,1,0:T(8,128)(2,1)}, u32[]{:S(2)}, u32[]{:S(2)}) collective-permute-start(bf16[2,384,512]{2,1,0:T(8,128)(2,1)} %get-tuple-element.98), channel_id=1, source_target_pairs={{0,2},{2,0},{4,6},{6,4},{8,10},{10,8},{12,14},{14,12},{16,18},{18,... | collective-permute-start | bytes 2359304 | tf_op jit(solution)/shard_map/ppermute | solution.py:587
  72.0 3.7 %collective-permute-start = (bf16[384,896]{1,0:T(8,128)(2,1)}, bf16[384,896]{1,0:T(8,128)(2,1)S(1)}, u32[]{:S(2)}, u32[]{:S(2)}) collective-permute-start(bf16[384,896]{1,0:T(8,128)(2,1)} %bitcast.37), channel_id=1, source_target_pairs={{0,1},{1,0},{2,3},{3,2},{4,5},{5,4},{6,7},{7,6},{8,9},{9,8},{10,11... | collective-permute-start | bytes 2064392 | tf_op jit(solution)/shard_map/ppermute | solution.py:773
  72.1 23.2 %collective-permute-start.2 = (bf16[2,384,512]{2,1,0:T(8,128)(2,1)}, bf16[2,384,512]{2,1,0:T(8,128)(2,1)}, u32[]{:S(2)}, u32[]{:S(2)}) collective-permute-start(bf16[2,384,512]{2,1,0:T(8,128)(2,1)} %get-tuple-element.100), channel_id=1, source_target_pairs={{0,4},{2,6},{4,0},{6,2},{8,12},{10,14},{12,8},{14,10},{16,20},{18,... | collective-permute-start | bytes 2359304 | tf_op jit(solution)/shard_map/ppermute | solution.py:587
  72.8 25.3 %collective-permute-start.3 = (bf16[2,384,512]{2,1,0:T(8,128)(2,1)}, bf16[2,384,512]{2,1,0:T(8,128)(2,1)}, u32[]{:S(2)}, u32[]{:S(2)}) collective-permute-start(bf16[2,384,512]{2,1,0:T(8,128)(2,1)} %get-tuple-element.102), channel_id=1, source_target_pairs={{0,8},{2,10},{4,12},{6,14},{8,0},{10,2},{12,4},{14,6},{16,24},{18,... | collective-permute-start | bytes 2359304 | tf_op jit(solution)/shard_map/ppermute | solution.py:587
  75.8 0.9 copy-start.8
  76.6 16.0 %copy-start.11 = (bf16[2,384,512]{2,1,0:T(8,128)(2,1)S(1)}, bf16[2,384,512]{2,1,0:T(8,128)(2,1)}, u32[]{:S(2)}) copy-start(bf16[2,384,512]{2,1,0:T(8,128)(2,1)} %get-tuple-element.97) | copy-start | bytes 2359300
  80.2 15.0 %copy-start.10 = (bf16[2,384,512]{2,1,0:T(8,128)(2,1)S(1)}, bf16[2,384,512]{2,1,0:T(8,128)(2,1)}, u32[]{:S(2)}) copy-start(bf16[2,384,512]{2,1,0:T(8,128)(2,1)} %get-tuple-element.99) | copy-start | bytes 2359300
  80.2 20.3 %all-to-all-start.2 = ((bf16[16,24,384]{2,1,0:T(8,128)(2,1)}), bf16[16,24,384]{2,1,0:T(8,128)(2,1)S(1)}, u32[]{:S(2)}, u32[]{:S(2)}) async-start(bf16[16,24,384]{2,1,0:T(8,128)(2,1)} %bitcast.33), calls=%async_computation.2 | async-start | bytes 589824 | tf_op jit(solution)/shard_map/all_to_all | solution.py:663
  92.6 5.5 %copy-start.9 = (bf16[2,384,512]{2,1,0:T(8,128)(2,1)S(1)}, bf16[2,384,512]{2,1,0:T(8,128)(2,1)}, u32[]{:S(2)}) copy-start(bf16[2,384,512]{2,1,0:T(8,128)(2,1)} %get-tuple-element.101) | copy-start | bytes 2359300
  94.5 13.2 %collective-permute-start.4 = (bf16[2,192,512]{2,1,0:T(8,128)(2,1)}, bf16[2,192,512]{2,1,0:T(8,128)(2,1)}, u32[]{:S(2)}, u32[]{:S(2)}) collective-permute-start(bf16[2,192,512]{2,1,0:T(8,128)(2,1)} %add_convert_fusion.2), channel_id=1, source_target_pairs={{0,4},{2,6},{4,0},{6,2},{8,12},{10,14},{12,8},{14,10},{16,20},{18,... | collective-permute-start | bytes 1179656 | tf_op jit(solution)/shard_map/ppermute | solution.py:587
  95.3 5.3 %copy-start = (bf16[4,96,384]{2,1,0:T(8,128)(2,1)S(1)}, bf16[4,96,384]{2,1,0:T(8,128)(2,1)}, u32[]{:S(2)}) copy-start(bf16[4,96,384]{2,1,0:T(8,128)(2,1)} %reshape.165.weights) | copy-start | bytes 884740
  95.3 5.3 %copy-start.1 = (f32[8,384]{1,0:T(8,128)S(1)}, f32[8,384]{1,0:T(8,128)}, u32[]{:S(2)}) copy-start(f32[8,384]{1,0:T(8,128)} %get-tuple-element.108.mlp_sums) | copy-start | bytes 36868
  95.3 5.3 %copy-start.2 = (f32[1,1536]{1,0:T(1,128)S(1)}, f32[1,1536]{1,0:T(1,128)}, u32[]{:S(2)}) copy-start(f32[1,1536]{1,0:T(1,128)} %get-tuple-element.109.hidden_sums) | copy-start | bytes 18436
  97.2 10.5 %collective-permute-start.5 = (bf16[2,192,512]{2,1,0:T(8,128)(2,1)}, bf16[2,192,512]{2,1,0:T(8,128)(2,1)}, u32[]{:S(2)}, u32[]{:S(2)}) collective-permute-start(bf16[2,192,512]{2,1,0:T(8,128)(2,1)} %add_convert_fusion.1), channel_id=1, source_target_pairs={{0,8},{2,10},{4,12},{6,14},{8,0},{10,2},{12,4},{14,6},{16,24},{18,... | collective-permute-start | bytes 1179656 | tf_op jit(solution)/shard_map/ppermute | solution.py:587
  100.0 9.2 %collective-permute-start.6 = (bf16[2,192,512]{2,1,0:T(8,128)(2,1)}, bf16[2,192,512]{2,1,0:T(8,128)(2,1)S(1)}, u32[]{:S(2)}, u32[]{:S(2)}) collective-permute-start(bf16[2,192,512]{2,1,0:T(8,128)(2,1)} %add_convert_fusion), channel_id=1, source_target_pairs={{0,2},{2,0},{4,6},{6,4},{8,10},{10,8},{12,14},{14,12},{16,18},{18,... | collective-permute-start | bytes 1179656 | tf_op jit(solution)/shard_map/ppermute | solution.py:587
  109.1 20.3 %all-to-all-start.3 = ((bf16[16,56,384]{2,1,0:T(8,128)(2,1)}), bf16[16,56,384]{2,1,0:T(8,128)(2,1)S(1)}, u32[]{:S(2)}, u32[]{:S(2)}) async-start(bf16[16,56,384]{2,1,0:T(8,128)(2,1)} %shard_map.323), calls=%async_computation.3 | async-start | bytes 1376256 | tf_op jit(solution)/shard_map/all_to_all | solution.py:826
  114.7 13.8 %collective-permute-start.7 = (bf16[2,96,512]{2,1,0:T(8,128)(2,1)S(1)}, bf16[2,96,512]{2,1,0:T(8,128)(2,1)S(1)}, u32[]{:S(2)}, u32[]{:S(2)}) collective-permute-start(bf16[2,96,512]{2,1,0:T(8,128)(2,1)S(1)} %get-tuple-element.153), channel_id=1, source_target_pairs={{0,8},{2,10},{4,12},{6,14},{8,0},{10,2},{12,4},{14,6},{16,24},{18,... | collective-permute-start | bytes 589832 | tf_op jit(solution)/shard_map/ppermute | solution.py:587
  118.0 4.2 %copy-start.4 = (f32[384,384]{1,0:T(8,128)S(1)}, f32[384,384]{1,0:T(8,128)}, u32[]{:S(2)}) copy-start(f32[384,384]{1,0:T(8,128)} %get-tuple-element.111.own) | copy-start | bytes 1769476
  118.0 4.2 %copy-start.25 = (f32[384]{0:T(512)S(1)}, f32[384]{0:T(512)}, u32[]{:S(2)}) copy-start(f32[384]{0:T(512)} %param.36) | copy-start | bytes 4612
  118.0 10.5 %collective-permute-start.8 = (bf16[2,96,512]{2,1,0:T(8,128)(2,1)S(1)}, bf16[2,96,512]{2,1,0:T(8,128)(2,1)S(1)}, u32[]{:S(2)}, u32[]{:S(2)}) collective-permute-start(bf16[2,96,512]{2,1,0:T(8,128)(2,1)S(1)} %get-tuple-element.151), channel_id=1, source_target_pairs={{0,2},{2,0},{4,6},{6,4},{8,10},{10,8},{12,14},{14,12},{16,18},{18,... | collective-permute-start | bytes 589832 | tf_op jit(solution)/shard_map/ppermute | solution.py:587
  120.7 7.9 %collective-permute-start.9 = (bf16[2,96,512]{2,1,0:T(8,128)(2,1)S(1)}, bf16[2,96,512]{2,1,0:T(8,128)(2,1)S(1)}, u32[]{:S(2)}, u32[]{:S(2)}) collective-permute-start(bf16[2,96,512]{2,1,0:T(8,128)(2,1)S(1)} %get-tuple-element.149), channel_id=1, source_target_pairs={{0,4},{2,6},{4,0},{6,2},{8,12},{10,14},{12,8},{14,10},{16,20},{18,... | collective-permute-start | bytes 589832 | tf_op jit(solution)/shard_map/ppermute | solution.py:587
  129.4 3.2 %copy-start.3 = (bf16[16,56,384]{2,1,0:T(8,128)(2,1)}, bf16[16,56,384]{2,1,0:T(8,128)(2,1)S(1)}, u32[]{:S(2)}) copy-start(bf16[16,56,384]{2,1,0:T(8,128)(2,1)S(1)} %all-to-all-done.3.got) | copy-start | bytes 2064388
  129.4 18.6 %collective-permute-start.10 = (bf16[2,48,1536]{2,1,0:T(8,128)(2,1)S(1)}, bf16[2,48,1536]{2,1,0:T(8,128)(2,1)S(1)}, u32[]{:S(2)}, u32[]{:S(2)}) collective-permute-start(bf16[2,48,1536]{2,1,0:T(8,128)(2,1)S(1)} %pad_maximum_fusion), channel_id=1, source_target_pairs={{0,16},{2,18},{4,20},{6,22},{8,24},{10,26},{12,28},{14,30},{16,0},... | collective-permute-start | bytes 884744 | tf_op jit(solution)/shard_map/ppermute | solution.py:587
  136.0 12.4 %copy-start.6 = (f32[384,384]{1,0:T(8,128)S(1)}, f32[384,384]{1,0:T(8,128)}, u32[]{:S(2)}) copy-start(f32[384,384]{1,0:T(8,128)} %get-tuple-element.121.xh) | copy-start | bytes 1769476
  136.0 12.4 %copy-start.7 = (f32[384,384]{1,0:T(8,128)S(1)}, f32[384,384]{1,0:T(8,128)}, u32[]{:S(2)}) copy-start(f32[384,384]{1,0:T(8,128)} %get-tuple-element.115.dx1) | copy-start | bytes 1769476
  136.0 12.4 %copy-start.12 = (f32[384,384]{1,0:T(8,128)S(1)}, f32[384,384]{1,0:T(8,128)}, u32[]{:S(2)}) copy-start(f32[384,384]{1,0:T(8,128)} %get-tuple-element.128) | copy-start | bytes 1769476
  136.0 12.4 %copy-start.17 = (f32[384]{0:T(512)S(1)}, f32[384]{0:T(512)}, u32[]{:S(2)}) copy-start(f32[384]{0:T(512)} %gain.5) | copy-start | bytes 4612
  136.0 15.0 %all-to-all-start.4 = ((bf16[16,32,384]{2,1,0:T(8,128)(2,1)}), bf16[16,32,384]{2,1,0:T(8,128)(2,1)S(1)}, u32[]{:S(2)}, u32[]{:S(2)}) async-start(bf16[16,32,384]{2,1,0:T(8,128)(2,1)} %get-tuple-element.129), calls=%async_computation.4 | async-start | bytes 786432 | tf_op jit(solution)/shard_map/all_to_all | solution.py:852
